TPU v7x, 128 devices: a whole 4x4x4 slice. The times are simulated.
128 devices in a mesh: seq: 4 (over x), grp: 16 (over y, z), exp: 2 (over core).
Axes of the slice: x: 4, y: 4, z: 4, core: 2. Of those that a mesh axis runs over, the one named last changes fastest.
Arguments:
- tokens: bfloat16 [16, 2048, 1024], P('grp', ('seq', 'exp')), may hold values from -6 to 6
- segments: int32 [16, 2048], P('grp', ('seq', 'exp')), may hold values from 0 to 3, never falling along the last dimension, each value on 1 to 1792 neighbouring positions
- routes: int32 [16, 2048, 8], P('grp', ('seq', 'exp')), may hold values from 0 to 31, all different within a row
- rank_order: int32 [16, 2048, 8], P('grp', ('seq', 'exp')), may hold values from 0 to 7, each once within a row
- attn_gain: float32 [1024], replicated, may hold values from 0.5 to 1.5
- w_query: bfloat16 [1024, 1024], replicated, may hold values from -0.75 to 0.75
- w_key: bfloat16 [1024, 512], replicated, may hold values from -0.75 to 0.75
- w_value: bfloat16 [1024, 512], replicated, may hold values from -0.1875 to 0.1875
- w_output: bfloat16 [1024, 1024], replicated, may hold values from -4 to 4
- ffn_gain: float32 [1024], replicated, may hold values from 0.5 to 1.5
- w_router: bfloat16 [1024, 32], replicated, may hold values from -0.09375 to 0.09375
- expert_in: bfloat16 [32, 1024, 1024], P(('grp', 'exp')), may hold values from -0.1875 to 0.1875
- expert_out: bfloat16 [32, 512, 1024], P(('grp', 'exp')), may hold values from -2 to 2
- cotangent: bfloat16 [16, 2048, 1024], P('grp', ('seq', 'exp')), may hold values from -6 to 6
Outputs:
- output: bfloat16 [16, 2048, 1024], P('grp', ('seq', 'exp'))
- input_grad: bfloat16 [16, 2048, 1024], P('grp', ('seq', 'exp'))
- attn_gain_grad: float32 [1024], replicated
- query_grad: float32 [1024, 1024], replicated
- key_grad: float32 [1024, 512], replicated
- value_grad: float32 [1024, 512], replicated
- output_w_grad: float32 [1024, 1024], replicated
- ffn_gain_grad: float32 [1024], replicated
- router_grad: float32 [1024, 32], replicated
- expert_in_grad: float32 [32, 1024, 1024], P(('grp', 'exp'))
- expert_out_grad: float32 [32, 512, 1024], P(('grp', 'exp'))
Inputs may be any that keep to these rules, and one draw needn't show every extreme that they name: `segments`: document numbers never fall along a sequence; one document of each sequence has 1792 tokens. `routes`: each token names 8 different experts; every expert is named somewhere. `rank_order`: each token's row is a permutation of 0 to 7.
All inputs are finite; a program needn't handle non-finite values.
Results may differ from a plain program's by a relative error of at most 0.015.
The roundings to bfloat16 on the way count: a program that leaves them out, or rounds other values in their place, can miss the bound.
Values may be sent and summed in bfloat16 or wider, within the bound.
A program may use at most 256 MiB of HBM per device.

v0:
```python
import math

import jax
import jax.numpy as jnp
from jax import lax
from jax.sharding import PartitionSpec as P

HEADS = 16
KV_HEADS = 8
HEAD = 64
WINDOW = 1024


EPSILON = 1e-06
ATTENTION_FACTOR = 0.015625
RESIDUAL_MULT = 0.22
ROPE_BASE = 10000.0
MASKED = -1e30


def from_behind(value, axis, steps):
    count = lax.axis_size(axis)
    initial, last = (max(0, -steps), min(count, count - steps))
    return lax.ppermute(value, axis, [(source, source + steps) for source in range(initial, last)])


def product(left_side, right_side):
    return jnp.dot(left_side, right_side, preferred_element_type=jnp.float32)


def inner_rows(left_side, right_side):
    return jnp.einsum("ta,tb->ab", left_side, right_side, preferred_element_type=jnp.float32)


def product_back(left_side, right_side):
    return jnp.einsum("tb,ab->ta", left_side, right_side, preferred_element_type=jnp.float32)


def rope_tables(positions, head_dim):
    half_dim = head_dim // 2
    frequency = jnp.exp(
        jnp.arange(half_dim, dtype=jnp.float32) * (-2.0 * math.log(ROPE_BASE) / head_dim)
    )
    angles = positions.astype(jnp.float32)[:, None] * frequency[None, :]
    return (jnp.cos(angles)[:, None, :], jnp.sin(angles)[:, None, :])


def rotate(values, cosine, sine_part):
    half_dim = values.shape[-1] // 2
    first_half = values[..., :half_dim]
    second_half = values[..., half_dim:]
    return jnp.concatenate(
        [
            first_half * cosine - second_half * sine_part,
            second_half * cosine + first_half * sine_part,
        ],
        axis=-1,
    )


def unrotate(values, cosine, sine_part):
    half_dim = values.shape[-1] // 2
    first_half = values[..., :half_dim]
    second_half = values[..., half_dim:]
    return jnp.concatenate(
        [
            first_half * cosine + second_half * sine_part,
            second_half * cosine - first_half * sine_part,
        ],
        axis=-1,
    )


def place_pairs(route_ids, rank_ids, experts, capacity):
    tok_rows, top_count = route_ids.shape
    by_order = (
        rank_ids[:, :, None] == jnp.arange(top_count, dtype=jnp.int32)[None, None, :]
    ).astype(jnp.int32)
    by_expert = (
        route_ids[:, :, None] == jnp.arange(experts, dtype=jnp.int32)[None, None, :]
    ).astype(jnp.int32)
    counts = jnp.sum(by_order[:, :, :, None] * by_expert[:, :, None, :], axis=1)
    before = (jnp.cumsum(counts, axis=0) - counts).reshape(tok_rows, top_count * experts)
    totals = jnp.sum(counts, axis=0)
    offsets = (jnp.cumsum(totals, axis=0) - totals).reshape(top_count * experts)
    flat_index = rank_ids * experts + route_ids
    slot_place = jnp.take_along_axis(before, flat_index, axis=1) + offsets[flat_index]
    destination = jnp.where(
        slot_place < capacity, route_ids * capacity + slot_place, experts * capacity
    )
    source = jnp.full((experts * capacity + 1,), tok_rows * top_count, jnp.int32)
    source = source.at[destination.reshape(-1)].set(
        jnp.arange(tok_rows * top_count, dtype=jnp.int32)
    )
    return (destination, source[: experts * capacity])


def on_device(
    tokens,
    segments,
    routes,
    rank_order,
    attn_gain,
    w_query,
    w_key,
    w_value,
    w_output,
    ffn_gain,
    w_router,
    expert_in,
    expert_out,
    cotangent,
):
    tok_rows = tokens.shape[1]
    model_width = tokens.shape[2]
    top_count = routes.shape[2]
    experts = w_router.shape[1]
    local_experts = expert_in.shape[0]
    inner_width = expert_out.shape[1]
    kv_width = w_key.shape[1]
    kv_heads = KV_HEADS
    head_dim = HEAD
    q_heads = HEADS
    group_size = q_heads // kv_heads
    capacity = 5 * tok_rows * top_count // (4 * experts)
    blocks = lax.axis_size(("seq", "exp"))
    block_id = lax.axis_index(("seq", "exp"))
    hop_count = min(-(-WINDOW // tok_rows), blocks - 1)
    key_span = (hop_count + 1) * tok_rows
    inputs = tokens[0].astype(jnp.float32)
    seg_ids = segments[0]
    route_ids = routes[0]
    rank_ids = rank_order[0]
    positions = block_id * tok_rows + jnp.arange(tok_rows, dtype=jnp.int32)
    cosine, sine_part = rope_tables(positions, head_dim)
    scale_one = lax.rsqrt(jnp.mean(inputs * inputs, axis=-1, keepdims=True) + EPSILON)
    normed = (inputs * scale_one * attn_gain).astype(jnp.bfloat16)
    query_pre = product(normed, w_query).reshape(tok_rows, q_heads, head_dim)
    key_pre = product(normed, w_key).reshape(tok_rows, kv_heads, head_dim)
    value_own = product(normed, w_value).astype(jnp.bfloat16)
    query_rows = (
        rotate(query_pre, cosine, sine_part)
        .astype(jnp.bfloat16)
        .reshape(tok_rows, kv_heads, group_size, head_dim)
    )
    key_own = rotate(key_pre, cosine, sine_part).astype(jnp.bfloat16).reshape(tok_rows, kv_width)
    key_parts = [key_own]
    value_parts = [value_own]
    seg_parts = [seg_ids]
    for hop_index in range(1, hop_count + 1):
        key_far, value_far, seg_far = from_behind(
            (key_own, value_own, seg_ids), ("seq", "exp"), hop_index
        )
        key_parts.insert(0, key_far)
        value_parts.insert(0, value_far)
        seg_parts.insert(0, seg_far)
    key_gathered = jnp.concatenate(key_parts, axis=0).reshape(key_span, kv_heads, head_dim)
    value_gathered = jnp.concatenate(value_parts, axis=0).reshape(key_span, kv_heads, head_dim)
    seg_all = jnp.concatenate(seg_parts, axis=0)
    key_pos = (block_id - hop_count) * tok_rows + jnp.arange(key_span, dtype=jnp.int32)
    distance = positions[:, None] - key_pos[None, :]
    allowed = (
        (seg_ids[:, None] == seg_all[None, :])
        & (distance >= 0)
        & (distance < WINDOW)
        & (key_pos[None, :] >= 0)
    )

    def scores_of():
        raw_scores = ATTENTION_FACTOR * jnp.einsum(
            "dklp,okp->kldo", query_rows, key_gathered, preferred_element_type=jnp.float32
        )
        return jnp.where(allowed[None, None], raw_scores, MASKED)

    score_matrix = scores_of()
    top_score = jnp.max(score_matrix, axis=-1, keepdims=True)
    expsum = jnp.sum(jnp.exp(score_matrix - top_score), axis=-1, keepdims=True)
    probability_lowered = (jnp.exp(score_matrix - top_score) / expsum).astype(jnp.bfloat16)
    heads_out = (
        jnp.einsum(
            "uzjq,quk->juzk",
            probability_lowered,
            value_gathered,
            preferred_element_type=jnp.float32,
        )
        .astype(jnp.bfloat16)
        .reshape(tok_rows, model_width)
    )
    branch = product(heads_out, w_output)
    residual = inputs + RESIDUAL_MULT * branch
    scale_two = lax.rsqrt(jnp.mean(residual * residual, axis=-1, keepdims=True) + EPSILON)
    routed_in = (residual * scale_two * ffn_gain).astype(jnp.bfloat16)
    logits = product(routed_in, w_router)
    picked = jnp.take_along_axis(logits, route_ids, axis=1)
    gate_weights = jax.nn.softmax(picked, axis=1)
    destination, source = place_pairs(route_ids, rank_ids, experts, capacity)
    token_of_slot = source // top_count
    padded_in = jnp.concatenate([routed_in, jnp.zeros((1, model_width), jnp.bfloat16)], axis=0)
    send_rows = padded_in[token_of_slot].reshape(experts, capacity, model_width)
    arrived = lax.all_to_all(send_rows, ("grp", "exp"), split_axis=0, concat_axis=0, tiled=True)
    by_source = arrived.reshape(-1, local_experts, arrived.shape[1], model_width)
    gate_up = jnp.einsum("nxcd,xdf->nxcf", by_source, expert_in, preferred_element_type=jnp.float32)
    hidden = (jax.nn.silu(gate_up[..., :inner_width]) * gate_up[..., inner_width:]).astype(
        jnp.bfloat16
    )
    result = jnp.einsum(
        "nxcf,xfd->nxcd", hidden, expert_out, preferred_element_type=jnp.float32
    ).astype(jnp.bfloat16)
    expert_res = result.reshape(arrived.shape)
    returned = lax.all_to_all(expert_res, ("grp", "exp"), split_axis=0, concat_axis=0, tiled=True)
    flat_res = jnp.concatenate(
        [
            returned.reshape(experts * capacity, model_width),
            jnp.zeros((1, model_width), jnp.bfloat16),
        ],
        axis=0,
    )
    gathered = flat_res[destination].astype(jnp.float32)
    moe_out = jnp.sum(gate_weights[:, :, None] * gathered, axis=1)
    output = (residual + RESIDUAL_MULT * moe_out).astype(jnp.bfloat16)[None]
    upstream = cotangent[0].astype(jnp.float32)
    moe_grad = RESIDUAL_MULT * upstream
    gate_grad = jnp.sum(moe_grad[:, None, :] * gathered, axis=-1)
    slot_gate = jnp.concatenate([gate_weights.reshape(-1), jnp.zeros((1,), jnp.float32)], axis=0)[
        source
    ]
    padded_grad = jnp.concatenate([moe_grad, jnp.zeros((1, model_width), jnp.float32)], axis=0)
    res_grad_send = (
        (padded_grad[token_of_slot] * slot_gate[:, None])
        .astype(jnp.bfloat16)
        .reshape(experts, capacity, model_width)
    )
    rows_at, res_grad_at = (
        lax.all_to_all(send_rows, ("grp", "exp"), split_axis=0, concat_axis=0, tiled=True),
        lax.all_to_all(res_grad_send, ("grp", "exp"), split_axis=0, concat_axis=0, tiled=True),
    )
    by_source = rows_at.reshape(-1, local_experts, capacity, model_width)
    out_grid = res_grad_at.reshape(-1, local_experts, capacity, model_width)
    gate_up = jnp.einsum("nxcd,xdf->nxcf", by_source, expert_in, preferred_element_type=jnp.float32)
    gate_half = gate_up[..., :inner_width]
    up_half = gate_up[..., inner_width:]
    sigmoid_gate = jax.nn.sigmoid(gate_half)
    activated = jax.nn.silu(gate_half)
    hidden = (activated * up_half).astype(jnp.bfloat16)
    hidden_grad = jnp.einsum(
        "nxcd,xfd->nxcf", out_grid, expert_out, preferred_element_type=jnp.float32
    )
    gate_part = hidden_grad * up_half * sigmoid_gate * (1.0 + gate_half * (1.0 - sigmoid_gate))
    up_part = hidden_grad * activated
    pair_grad = jnp.concatenate([gate_part, up_part], axis=-1).astype(jnp.bfloat16)
    down_w_grad = jnp.einsum("nxcf,nxcd->xfd", hidden, out_grid, preferred_element_type=jnp.float32)
    up_w_grad = jnp.einsum(
        "nxcd,nxcf->xdf", by_source, pair_grad, preferred_element_type=jnp.float32
    )
    row_grad = (
        jnp.einsum("nxcf,xdf->nxcd", pair_grad, expert_in, preferred_element_type=jnp.float32)
        .astype(jnp.bfloat16)
        .reshape(-1, capacity, model_width)
    )
    row_back = lax.all_to_all(row_grad, ("grp", "exp"), split_axis=0, concat_axis=0, tiled=True)
    flat_back = jnp.concatenate(
        [
            row_back.reshape(experts * capacity, model_width),
            jnp.zeros((1, model_width), jnp.bfloat16),
        ],
        axis=0,
    )
    expert_row_sum = jnp.sum(flat_back[destination].astype(jnp.float32), axis=1)
    choice_grad = gate_weights * (
        gate_grad - jnp.sum(gate_weights * gate_grad, axis=1, keepdims=True)
    )
    onehot = (route_ids[:, :, None] == jnp.arange(experts, dtype=jnp.int32)[None, None, :]).astype(
        jnp.float32
    )
    logit_grad = jnp.sum(onehot * choice_grad[:, :, None], axis=1).astype(jnp.bfloat16)
    router_w_grad = inner_rows(routed_in, logit_grad)
    routed_grad = product_back(logit_grad, w_router) + expert_row_sum
    normal_two = residual * scale_two
    ffn_gain_grad = jnp.sum(routed_grad * normal_two, axis=0)
    weighted_two = routed_grad * ffn_gain
    residual_grad = (
        upstream
        + scale_two * weighted_two
        - residual * scale_two**3 * jnp.mean(weighted_two * residual, axis=-1, keepdims=True)
    )
    branch_grad = (RESIDUAL_MULT * residual_grad).astype(jnp.bfloat16)
    out_w_grad = inner_rows(heads_out, branch_grad)
    head_gradient = (
        product_back(branch_grad, w_output)
        .astype(jnp.bfloat16)
        .reshape(tok_rows, kv_heads, group_size, head_dim)
    )
    score_matrix = scores_of()
    probs_full = jnp.exp(score_matrix - top_score) / expsum
    probability_lowered = probs_full.astype(jnp.bfloat16)
    prob_grad = jnp.einsum(
        "dklp,okp->kldo", head_gradient, value_gathered, preferred_element_type=jnp.float32
    )
    score_gradient = (
        probs_full * (prob_grad - jnp.sum(probs_full * prob_grad, axis=-1, keepdims=True))
    ).astype(jnp.bfloat16)
    queries_grad = ATTENTION_FACTOR * jnp.einsum(
        "uzjq,quk->juzk", score_gradient, key_gathered, preferred_element_type=jnp.float32
    )
    keys_grad_all = (
        ATTENTION_FACTOR
        * jnp.einsum(
            "ykze,zykm->eym", score_gradient, query_rows, preferred_element_type=jnp.float32
        )
    ).reshape(key_span, kv_width)
    values_grad_all = jnp.einsum(
        "ykze,zykm->eym", probability_lowered, head_gradient, preferred_element_type=jnp.float32
    ).reshape(key_span, kv_width)
    keys_grad = keys_grad_all[hop_count * tok_rows :]
    values_grad = values_grad_all[hop_count * tok_rows :]
    for hop_index in range(1, hop_count + 1):
        first_row = (hop_count - hop_index) * tok_rows
        key_back, value_back = (
            from_behind(
                keys_grad_all[first_row : first_row + tok_rows].astype(jnp.bfloat16),
                ("seq", "exp"),
                -hop_index,
            ).astype(jnp.float32),
            from_behind(
                values_grad_all[first_row : first_row + tok_rows].astype(jnp.bfloat16),
                ("seq", "exp"),
                -hop_index,
            ).astype(jnp.float32),
        )
        keys_grad = keys_grad + key_back
        values_grad = values_grad + value_back
    query_pre_grad = (
        unrotate(queries_grad.reshape(tok_rows, q_heads, head_dim), cosine, sine_part)
        .astype(jnp.bfloat16)
        .reshape(tok_rows, model_width)
    )
    key_pre_grad = (
        unrotate(keys_grad.reshape(tok_rows, kv_heads, head_dim), cosine, sine_part)
        .astype(jnp.bfloat16)
        .reshape(tok_rows, kv_width)
    )
    value_pre_grad = values_grad.astype(jnp.bfloat16)
    query_w_grad = inner_rows(normed, query_pre_grad)
    key_w_grad = inner_rows(normed, key_pre_grad)
    value_w_grad = inner_rows(normed, value_pre_grad)
    normed_grad = (
        product_back(query_pre_grad, w_query)
        + product_back(key_pre_grad, w_key)
        + product_back(value_pre_grad, w_value)
    )
    attn_gain_grad = jnp.sum(normed_grad * inputs * scale_one, axis=0)
    weighted_one = normed_grad * attn_gain
    input_grad = (
        residual_grad
        + scale_one * weighted_one
        - inputs * scale_one**3 * jnp.mean(weighted_one * inputs, axis=-1, keepdims=True)
    )
    up_total, down_total = (
        lax.psum(up_w_grad.astype(jnp.bfloat16), "seq").astype(jnp.float32),
        lax.psum(down_w_grad.astype(jnp.bfloat16), "seq").astype(jnp.float32),
    )
    gain_one_total, query_total, key_total, value_total, out_total, gain_two_total, router_total = (
        lax.psum(
            (
                attn_gain_grad,
                query_w_grad,
                key_w_grad,
                value_w_grad,
                out_w_grad,
                ffn_gain_grad,
                router_w_grad,
            ),
            ("seq", "grp", "exp"),
        )
    )
    return (
        output,
        input_grad.astype(jnp.bfloat16)[None],
        gain_one_total,
        query_total,
        key_total,
        value_total,
        out_total,
        gain_two_total,
        router_total,
        up_total,
        down_total,
    )


def solution(mesh):
    placed = (
        P("grp", ("seq", "exp"), None),
        P("grp", ("seq", "exp")),
        P("grp", ("seq", "exp"), None),
        P("grp", ("seq", "exp"), None),
        P(),
        P(),
        P(),
        P(),
        P(),
        P(),
        P(),
        P(("grp", "exp"), None, None),
        P(("grp", "exp"), None, None),
        P("grp", ("seq", "exp"), None),
    )
    return jax.shard_map(
        on_device,
        mesh=mesh,
        in_specs=placed,
        out_specs=(
            P("grp", ("seq", "exp"), None),
            P("grp", ("seq", "exp"), None),
            P(),
            P(),
            P(),
            P(),
            P(),
            P(),
            P(),
            P(("grp", "exp"), None, None),
            P(("grp", "exp"), None, None),
        ),
        check_vma=False,
    )
```

profile of v0, /device:TPU:1, one launch (start us, length us, event | category | flops | bytes accessed | tf_op | source)
XLA Modules:
  0.0 815.8 jit_solution(6519029585768564125)
XLA Ops:
  29.7 18.0 %reduce-window.6 = s32[32,8,2,128]{3,1,2,0:T(8,128)S(1)} reduce-window(s32[32,8,2,128]{3,1,2,0:T(8,128)S(1)} %bitcast.353, s32[]{:T(128)} %constant.44.clone.1), window={size=1x1x1x128 pad=0_0x0_0x0_0x127_0}, to_apply=%region_7.8 | reduce-window | flops 8323072 | bytes 524292 | tf_op jit(solution)/shard_map/reduce-window
  48.7 16.8 %gather_fusion.7 = s32[2048]{0:T(1024)S(1)} fusion(s32[256,256]{0,1:T(8,128)S(1)} %bitcast.328, s32[2048]{0:T(1024)S(1)} %reshape.844), kind=kCustom, calls=%fused_computation.7 | custom fusion | bytes 32768 | tf_op jit(solution)/shard_map/jit(take_along_axis)/gather | solution.py:87
  65.5 13.1 %gather_fusion = s32[2048]{0:T(1024)S(1)} fusion(s32[256]{0:T(256)S(1)} %sub.125, s32[2048]{0:T(1024)S(1)} %broadcast_clamp_fusion.1), kind=kCustom, calls=%fused_computation | custom fusion | bytes 24576 | tf_op jit(solution)/shard_map/gather | solution.py:87
  78.7 8.1 scatter_custom_fusion
  109.3 9.0 %collective-permute-done = bf16[256,512]{1,0:T(8,128)(2,1)S(1)} collective-permute-done((bf16[256,512]{1,0:T(8,128)(2,1)}, bf16[256,512]{1,0:T(8,128)(2,1)S(1)}, u32[]{:S(2)}, u32[]{:S(2)}) %collective-permute-start) | collective-permute-done | bytes 262176 | tf_op jit(solution)/shard_map/ppermute | solution.py:24
  121.0 8.5 %collective-permute-start.9 = (bf16[256,512]{0,1:T(8,128)(2,1)}, bf16[256,512]{0,1:T(8,128)(2,1)}, u32[]{:S(2)}, u32[]{:S(2)}) collective-permute-start(bf16[256,512]{0,1:T(8,128)(2,1)} %bitcast.359), channel_id=1, source_target_pairs={{0,33},{1,64},{32,65},{33,96},{64,97},{2,35},{3,66},{34,67},{35,98... | collective-permute-start | bytes 786440 | tf_op jit(solution)/shard_map/ppermute | solution.py:24
  147.9 12.6 %exponential_reduce_fusion = (f32[8,2,256]{2,1,0:T(2,128)S(1)}, f32[8,2,256,1280]{2,3,1,0:T(8,128)}) fusion(pred[256,1280]{0,1:T(8,128)(4,1)} %fusion.46, bf16[1280,8,64]{0,2,1:T(8,128)(2,1)} %constant_dynamic-update-slice_fusion.6, bf16[256,8,2,32]{0,3,2,1:T(8,128)(2,1)} %bitcast.349, bf16[256,8,2,32]{0,3,2,1:T(8,128)(2,1)S(1)} %bitcast.345), kind=kOutput, calls=%fused_computation.18 | convolution fusion | flops 693110016 | bytes 23150592 | tf_op jit(solution)/shard_map/sub | solution.py:178
  160.6 11.9 %fusion.47 = bf16[8,64,2,256]{3,1,2,0:T(8,128)(2,1)S(1)} fusion(bf16[1280,8,64,1]{0,2,3,1:T(8,128)(2,1)} %bitcast.343, f32[8,2,256]{2,1,0:T(2,128)S(1)} %get-tuple-element.60, pred[256,1280]{0,1:T(8,128)(4,1)} %fusion.46, bf16[1280,8,64]{0,2,1:T(8,128)(2,1)} %constant_dynamic-update-slice_fusion.6, bf16[256,8,2,32]{0,3,2,1:T(8,128)(2,1)} %bitcast.350, ...), kind=kOutput, calls=%fused_computation.83 | convolution fusion | flops 1369707776 | bytes 4014080 | tf_op jit(solution)/shard_map/uzjq,quk->juzk/dot_general | solution.py:180
  176.4 8.9 %gather_fusion.1 = bf16[2560,1024]{1,0:T(8,128)(2,1)} fusion(bf16[257,1024]{1,0:T(8,128)(2,1)S(1)} %concatenate.74, s32[3072]{0:T(1024)S(1)} %get-tuple-element.73), kind=kCustom, calls=%fused_computation.1 | custom fusion | bytes 10496000 | tf_op jit(solution)/shard_map/gather | solution.py:199
  185.3 9.0 %all-to-all-start = ((bf16[32,80,1024]{2,1,0:T(8,128)(2,1)}), bf16[32,80,1024]{2,1,0:T(8,128)(2,1)}, u32[]{:S(2)}, u32[]{:S(2)}) async-start(bf16[32,80,1024]{2,1,0:T(8,128)(2,1)} %bitcast.330), calls=%async_computation | async-start | bytes 10485760 | tf_op jit(solution)/shard_map/all_to_all | solution.py:200
  195.7 8.9 %gather_fusion.3 = f32[2560,1024]{1,0:T(8,128)} fusion(f32[257,1024]{1,0:T(8,128)S(1)} %concatenate.76, s32[3072]{0:T(1024)S(1)} %get-tuple-element.73), kind=kCustom, calls=%fused_computation.3 | custom fusion | bytes 20981760 | tf_op jit(solution)/shard_map/gather | solution.py:229
  205.9 16.8 %gather_fusion.6 = f32[2048]{0:T(1024)S(1)} fusion(f32[256,32]{0,1:T(8,128)S(1)} %fusion.139, s32[2048]{0:T(1024)S(1)} %reshape.838), kind=kCustom, calls=%fused_computation.6 | custom fusion | bytes 32768 | tf_op jit(solution)/shard_map/jit(take_along_axis)/gather | solution.py:194
  223.6 13.6 %gather_fusion.4 = f32[2560]{0:T(1024)S(1)} fusion(f32[2049]{0:T(1024)S(1)} %pad_maximum_fusion.12, s32[3072]{0:T(1024)S(1)} %get-tuple-element.72), kind=kCustom, calls=%fused_computation.4 | custom fusion | bytes 30720 | tf_op jit(solution)/shard_map/gather | solution.py:224
  244.2 14.6 %all-to-all-done = bf16[32,80,1024]{2,1,0:T(8,128)(2,1)} async-done(((bf16[32,80,1024]{2,1,0:T(8,128)(2,1)}), bf16[32,80,1024]{2,1,0:T(8,128)(2,1)}, u32[]{:S(2)}, u32[]{:S(2)}) %all-to-all-start) | async-done | bytes 5242912 | tf_op jit(solution)/shard_map/all_to_all | solution.py:200
  258.8 9.1 %all-to-all-start.2 = ((bf16[32,80,1024]{2,1,0:T(8,128)(2,1)}), bf16[32,80,1024]{2,1,0:T(8,128)(2,1)}, u32[]{:S(2)}, u32[]{:S(2)}) async-start(bf16[32,80,1024]{2,1,0:T(8,128)(2,1)} %multiply_convert_fusion), calls=%async_computation.2 | async-start | bytes 10485760 | tf_op jit(solution)/shard_map/all_to_all | solution.py:235
  267.9 10.7 %convolution_bitcast_fusion = f32[32,1,80,1024]{3,2,0,1:T(8,128)} fusion(bf16[32,80,1024]{2,1,0:T(8,128)(2,1)} %all-to-all-done, bf16[1,1024,1024]{2,1,0:T(8,128)(2,1)S(1)} %copy-done), kind=kOutput, calls=%fused_computation.40 | convolution fusion | flops 5368709120 | bytes 17825792 | tf_op jit(solution)/shard_map/nxcd,xdf->nxcf/dot_general | solution.py:202
  278.6 53.9 %all-to-all-done.2 = bf16[32,80,1024]{2,1,0:T(8,128)(2,1)} async-done(((bf16[32,80,1024]{2,1,0:T(8,128)(2,1)}), bf16[32,80,1024]{2,1,0:T(8,128)(2,1)}, u32[]{:S(2)}, u32[]{:S(2)}) %all-to-all-start.2) | async-done | bytes 5242912 | tf_op jit(solution)/shard_map/all_to_all | solution.py:235
  332.5 11.5 %fusion.26 = (bf16[32,80,512]{2,1,0:T(8,128)(2,1)S(1)}, bf16[32,80,512]{2,1,0:T(8,128)(2,1)S(1)}, bf16[32,80,512]{2,1,0:T(8,128)(2,1)}) fusion(f32[32,1,80,1024]{3,2,0,1:T(8,128)} %convolution_bitcast_fusion, bf16[32,80,1024]{2,1,0:T(8,128)(2,1)} %all-to-all-done.2, bf16[1,512,1024]{2,1,0:T(8,128)(2,1)} %param.26), kind=kOutput, calls=%fused_computation.53 | convolution fusion | flops 2704015360 | bytes 24641536 | tf_op jit(solution)/shard_map/nxcd,xfd->nxcf/dot_general | solution.py:245
  346.4 7.3 fusion.23
  353.7 8.8 %all-to-all-start.3 = ((bf16[32,80,1024]{2,1,0:T(8,128)(2,1)}), bf16[32,80,1024]{2,1,0:T(8,128)(2,1)}, u32[]{:S(2)}, u32[]{:S(2)}) async-start(bf16[32,80,1024]{2,1,0:T(8,128)(2,1)} %fusion.23), calls=%async_computation.3 | async-start | bytes 10485760 | tf_op jit(solution)/shard_map/all_to_all | solution.py:260
  369.0 58.1 %all-to-all-done.3 = bf16[32,80,1024]{2,1,0:T(8,128)(2,1)} async-done(((bf16[32,80,1024]{2,1,0:T(8,128)(2,1)}), bf16[32,80,1024]{2,1,0:T(8,128)(2,1)}, u32[]{:S(2)}, u32[]{:S(2)}) %all-to-all-start.3) | async-done | bytes 5242912 | tf_op jit(solution)/shard_map/all_to_all | solution.py:260
  427.0 8.1 all-to-all-start.1
  435.8 7.3 fusion.30
  443.1 9.5 %fusion.27 = bf16[1,1024,1024]{2,1,0:T(8,128)(2,1)} fusion(bf16[32,80,1024]{2,1,0:T(8,128)(2,1)} %all-to-all-done, bf16[32,80,512]{2,1,0:T(8,128)(2,1)S(1)} %copy-done.62, bf16[32,80,512]{2,1,0:T(8,128)(2,1)S(1)} %copy-done.60), kind=kOutput, calls=%fused_computation.54 | convolution fusion | flops 5380243456 | bytes 12582912 | tf_op jit(solution)/shard_map/nxcd,nxcf->xdf/dot_general | solution.py:252
  458.1 14.3 %gather_fusion.5 = bf16[2048,1024]{1,0:T(8,128)(2,1)} fusion(bf16[2561,1024]{1,0:T(8,128)(2,1)} %concatenate.81, s32[2048]{0:T(1024)S(1)} %broadcast_clamp_fusion), kind=kCustom, calls=%fused_computation.5 | custom fusion | bytes 8396800 | tf_op jit(solution)/shard_map/gather | solution.py:268
  478.9 20.9 %all-to-all-done.1 = bf16[32,80,1024]{2,1,0:T(8,128)(2,1)} async-done(((bf16[32,80,1024]{2,1,0:T(8,128)(2,1)}), bf16[32,80,1024]{2,1,0:T(8,128)(2,1)}, u32[]{:S(2)}, u32[]{:S(2)}) %all-to-all-start.1) | async-done | bytes 5242912 | tf_op jit(solution)/shard_map/all_to_all | solution.py:210
  505.4 14.2 %gather_fusion.2 = bf16[2048,1024]{1,0:T(8,128)(2,1)} fusion(bf16[2561,1024]{1,0:T(8,128)(2,1)} %concatenate.75, s32[2048]{0:T(1024)S(1)} %broadcast_clamp_fusion), kind=kCustom, calls=%fused_computation.2 | custom fusion | bytes 8396800 | tf_op jit(solution)/shard_map/gather | solution.py:218
  531.7 12.8 %fusion.134 = (bf16[1280,8,64]{0,2,1:T(8,128)(2,1)}, f32[1280,8,64]{0,2,1:T(8,128)}) fusion(bf16[256,8,2,64]{0,3,2,1:T(8,128)(2,1)} %bitcast.355, f32[8,2,256]{2,1,0:T(2,128)S(1)} %copy-done.52, pred[256,1280]{0,1:T(8,128)(4,1)} %fusion.46, bf16[1280,8,64]{0,2,1:T(8,128)(2,1)S(1)} %copy-done.19, bf16[256,8,2,32]{0,3,2,1:T(8,128)(2,1)S(1)} %bitcast.351, ...), kind=kOutput, calls=%fused_computation.239 | convolution fusion | flops 1370100992 | bytes 6635520 | tf_op jit(solution)/shard_map/ykze,zykm->eym/dot_general | solution.py:311
  544.5 13.8 %fusion.2 = (f32[8,2,256]{2,1,0:T(2,128)S(1)}, f32[8,1280,256,2]{2,1,3,0:T(8,128)}) fusion(f32[8,2,256]{2,1,0:T(2,128)S(1)} %copy-done.52, f32[8,2,256,1280]{2,3,1,0:T(8,128)} %get-tuple-element.61, bf16[1280,8,64,1]{0,2,3,1:T(8,128)(2,1)} %bitcast.344, bf16[256,8,2,64]{0,3,2,1:T(8,128)(2,1)S(1)} %bitcast.356), kind=kOutput, calls=%fused_computation.13 | convolution fusion | flops 686813184 | bytes 43810816 | tf_op jit(solution)/shard_map/dklp,okp->kldo/dot_general | solution.py:296
  558.3 14.2 %fusion.4 = bf16[8,2,256,1280]{2,3,1,0:T(8,128)(2,1)S(1)} fusion(f32[8,1280,256,2]{2,1,3,0:T(8,128)} %get-tuple-element.66, f32[8,2,256]{2,1,0:T(2,128)S(1)} %get-tuple-element.65, f32[8,2,256]{2,1,0:T(2,128)S(1)} %copy-done.52, f32[8,2,256,1280]{2,3,1,0:T(8,128)} %get-tuple-element.61), kind=kLoop, calls=%fused_computation.15 | loop fusion | flops 20971520 | bytes 52461568 | tf_op jit(solution)/shard_map/convert_element_type | solution.py:301
  623.8 76.6 %all-reduce.4 = (f32[1024]{0:T(1024)}, f32[1024]{0:T(1024)}) all-reduce(f32[1024]{0:T(1024)S(1)} %get-tuple-element.15, f32[1024]{0:T(1024)S(1)} %get-tuple-element.13), channel_id=1, replica_groups=mesh['seq'=4,'grp'=16,'exp'=2] {'seq','grp','exp'}, use_global_device_ids=true, to_apply=%region_21.22 | all-reduce | flops 2048 | bytes 16384 | tf_op jit(solution)/shard_map/psum | solution.py:363
  701.6 95.9 %all-reduce.10.cloned.1.call-done = (f32[1024,1024]{1,0:T(8,128)}, f32[1024,512]{1,0:T(8,128)}, f32[1024,512]{1,0:T(8,128)}, f32[1024,1024]{1,0:T(8,128)}, f32[1024,32]{0,1:T(8,128)}) async-done(((f32[1024,1024]{1,0:T(8,128)}, f32[1024,512]{1,0:T(8,128)}, f32[1024,512]{1,0:T(8,128)}, f32[1024,1024]{1,0:T(8,128)}, f32[1024,32]{0,1:T(8,128)}), (f32[1024,1024]{1,0:T(8,128)}, f32[1024,512]{1,0:T(8,128)}, ...) | async-done | bytes 12714000 | tf_op jit(solution)/shard_map/psum | solution.py:363
  (301 shorter events, 183.4 us)
Async XLA Ops:
  7.2 260.7 %copy-start = (bf16[1,1024,1024]{2,1,0:T(8,128)(2,1)S(1)}, bf16[1,1024,1024]{2,1,0:T(8,128)(2,1)}, u32[]{:S(2)}) copy-start(bf16[1,1024,1024]{2,1,0:T(8,128)(2,1)} %param.25) | copy-start | bytes 6291460
  7.2 98.1 %collective-permute-start.7 = (s32[256]{0:T(256)}, s32[256]{0:T(256)S(1)}, u32[]{:S(2)}, u32[]{:S(2)}) collective-permute-start(s32[256]{0:T(256)} %bitcast.374), channel_id=1, source_target_pairs={{0,1},{1,32},{32,33},{33,64},{64,65},{65,96},{96,97},{2,3},{3,34},... | collective-permute-start | bytes 3080 | tf_op jit(solution)/shard_map/ppermute | solution.py:24
  11.9 92.1 %collective-permute-start.6 = (s32[256]{0:T(256)}, s32[256]{0:T(256)S(1)}, u32[]{:S(2)}, u32[]{:S(2)}) collective-permute-start(s32[256]{0:T(256)} %bitcast.375), channel_id=1, source_target_pairs={{0,32},{1,33},{32,64},{33,65},{64,96},{65,97},{2,34},{3,35},{34,66... | collective-permute-start | bytes 3080 | tf_op jit(solution)/shard_map/ppermute | solution.py:24
  15.0 86.7 %collective-permute-start.5 = (s32[256]{0:T(256)}, s32[256]{0:T(256)S(1)}, u32[]{:S(2)}, u32[]{:S(2)}) collective-permute-start(s32[256]{0:T(256)} %bitcast.376), channel_id=1, source_target_pairs={{0,33},{1,64},{32,65},{33,96},{64,97},{2,35},{3,66},{34,67},{35,98... | collective-permute-start | bytes 3080 | tf_op jit(solution)/shard_map/ppermute | solution.py:24
  18.4 81.6 %collective-permute-start.4 = (s32[256]{0:T(256)}, s32[256]{0:T(256)S(1)}, u32[]{:S(2)}, u32[]{:S(2)}) collective-permute-start(s32[256]{0:T(256)} %bitcast.377), channel_id=1, source_target_pairs={{0,64},{1,65},{32,96},{33,97},{2,66},{3,67},{34,98},{35,99},{4,68}... | collective-permute-start | bytes 3080 | tf_op jit(solution)/shard_map/ppermute | solution.py:24
  21.6 74.0 %copy-start.46 = (f32[256]{0:T(256)}, f32[256]{0:T(256)S(1)}, u32[]{:S(2)}) copy-start(f32[256]{0:T(256)S(1)} %get-tuple-element.57) | copy-start | bytes 3076
  24.2 108.3 %collective-permute-start.3 = (bf16[256,512]{1,0:T(8,128)(2,1)}, bf16[256,512]{1,0:T(8,128)(2,1)}, u32[]{:S(2)}, u32[]{:S(2)}) collective-permute-start(bf16[256,512]{1,0:T(8,128)(2,1)} %convolution_convert_fusion.2), channel_id=1, source_target_pairs={{0,1},{1,32},{32,33},{33,64},{64,65},{65,96},{96,97},{2,3},{3,34},... | collective-permute-start | bytes 786440 | tf_op jit(solution)/shard_map/ppermute | solution.py:24
  100.0 30.2 %collective-permute-start.2 = (bf16[256,512]{1,0:T(8,128)(2,1)}, bf16[256,512]{1,0:T(8,128)(2,1)S(1)}, u32[]{:S(2)}, u32[]{:S(2)}) collective-permute-start(bf16[256,512]{1,0:T(8,128)(2,1)} %convolution_convert_fusion.2), channel_id=1, source_target_pairs={{0,32},{1,33},{32,64},{33,65},{64,96},{65,97},{2,34},{3,35},{34,66... | collective-permute-start | bytes 786440 | tf_op jit(solution)/shard_map/ppermute | solution.py:24
  101.7 19.3 %collective-permute-start.1 = (bf16[256,512]{1,0:T(8,128)(2,1)}, bf16[256,512]{1,0:T(8,128)(2,1)S(1)}, u32[]{:S(2)}, u32[]{:S(2)}) collective-permute-start(bf16[256,512]{1,0:T(8,128)(2,1)} %convolution_convert_fusion.2), channel_id=1, source_target_pairs={{0,33},{1,64},{32,65},{33,96},{64,97},{2,35},{3,66},{34,67},{35,98... | collective-permute-start | bytes 786440 | tf_op jit(solution)/shard_map/ppermute | solution.py:24
  103.9 14.3 %collective-permute-start = (bf16[256,512]{1,0:T(8,128)(2,1)}, bf16[256,512]{1,0:T(8,128)(2,1)S(1)}, u32[]{:S(2)}, u32[]{:S(2)}) collective-permute-start(bf16[256,512]{1,0:T(8,128)(2,1)} %convolution_convert_fusion.2), channel_id=1, source_target_pairs={{0,64},{1,65},{32,96},{33,97},{2,66},{3,67},{34,98},{35,99},{4,68}... | collective-permute-start | bytes 786440 | tf_op jit(solution)/shard_map/ppermute | solution.py:24
  105.3 40.2 %collective-permute-start.11 = (bf16[256,512]{0,1:T(8,128)(2,1)}, bf16[256,512]{0,1:T(8,128)(2,1)}, u32[]{:S(2)}, u32[]{:S(2)}) collective-permute-start(bf16[256,512]{0,1:T(8,128)(2,1)} %bitcast.357), channel_id=1, source_target_pairs={{0,1},{1,32},{32,33},{33,64},{64,65},{65,96},{96,97},{2,3},{3,34},... | collective-permute-start | bytes 786440 | tf_op jit(solution)/shard_map/ppermute | solution.py:24
  118.3 25.6 %collective-permute-start.10 = (bf16[256,512]{0,1:T(8,128)(2,1)}, bf16[256,512]{0,1:T(8,128)(2,1)}, u32[]{:S(2)}, u32[]{:S(2)}) collective-permute-start(bf16[256,512]{0,1:T(8,128)(2,1)} %bitcast.358), channel_id=1, source_target_pairs={{0,32},{1,33},{32,64},{33,65},{64,96},{65,97},{2,34},{3,35},{34,66... | collective-permute-start | bytes 786440 | tf_op jit(solution)/shard_map/ppermute | solution.py:24
  121.0 21.2 %collective-permute-start.9 = (bf16[256,512]{0,1:T(8,128)(2,1)}, bf16[256,512]{0,1:T(8,128)(2,1)}, u32[]{:S(2)}, u32[]{:S(2)}) collective-permute-start(bf16[256,512]{0,1:T(8,128)(2,1)} %bitcast.359), channel_id=1, source_target_pairs={{0,33},{1,64},{32,65},{33,96},{64,97},{2,35},{3,66},{34,67},{35,98... | collective-permute-start | bytes 786440 | tf_op jit(solution)/shard_map/ppermute | solution.py:24
  130.2 8.8 %collective-permute-start.8 = (bf16[256,512]{0,1:T(8,128)(2,1)}, bf16[256,512]{0,1:T(8,128)(2,1)S(1)}, u32[]{:S(2)}, u32[]{:S(2)}) collective-permute-start(bf16[256,512]{0,1:T(8,128)(2,1)} %bitcast.360), channel_id=1, source_target_pairs={{0,64},{1,65},{32,96},{33,97},{2,66},{3,67},{34,98},{35,99},{4,68}... | collective-permute-start | bytes 786440 | tf_op jit(solution)/shard_map/ppermute | solution.py:24
  185.3 73.5 %all-to-all-start = ((bf16[32,80,1024]{2,1,0:T(8,128)(2,1)}), bf16[32,80,1024]{2,1,0:T(8,128)(2,1)}, u32[]{:S(2)}, u32[]{:S(2)}) async-start(bf16[32,80,1024]{2,1,0:T(8,128)(2,1)} %bitcast.330), calls=%async_computation | async-start | bytes 10485760 | tf_op jit(solution)/shard_map/all_to_all | solution.py:200
  258.8 73.7 %all-to-all-start.2 = ((bf16[32,80,1024]{2,1,0:T(8,128)(2,1)}), bf16[32,80,1024]{2,1,0:T(8,128)(2,1)}, u32[]{:S(2)}, u32[]{:S(2)}) async-start(bf16[32,80,1024]{2,1,0:T(8,128)(2,1)} %multiply_convert_fusion), calls=%async_computation.2 | async-start | bytes 10485760 | tf_op jit(solution)/shard_map/all_to_all | solution.py:235
  353.7 73.3 %all-to-all-start.3 = ((bf16[32,80,1024]{2,1,0:T(8,128)(2,1)}), bf16[32,80,1024]{2,1,0:T(8,128)(2,1)}, u32[]{:S(2)}, u32[]{:S(2)}) async-start(bf16[32,80,1024]{2,1,0:T(8,128)(2,1)} %fusion.23), calls=%async_computation.3 | async-start | bytes 10485760 | tf_op jit(solution)/shard_map/all_to_all | solution.py:260
  369.0 66.2 %copy-start.18 = (s32[2048]{0:T(1024)S(1)}, s32[2048]{0:T(1024)}, u32[]{:S(2)}) copy-start(s32[2048]{0:T(1024)} %copy-done.17) | copy-start | bytes 24580
  369.0 66.4 %copy-start.16 = (s32[2048]{0:T(1024)S(1)}, s32[2048]{0:T(1024)}, u32[]{:S(2)}) copy-start(s32[2048]{0:T(1024)} %copy-done.15) | copy-start | bytes 24580
  369.0 66.5 %copy-start.27 = (s32[256,8,1]{1,0,2:T(8,128)S(1)}, s32[256,8,1]{1,0,2:T(8,128)}, u32[]{:S(2)}) copy-start(s32[256,8,1]{1,0,2:T(8,128)} %copy-done.26) | copy-start | bytes 24580
  427.0 72.7 %all-to-all-start.1 = ((bf16[32,80,1024]{2,1,0:T(8,128)(2,1)}), bf16[32,80,1024]{2,1,0:T(8,128)(2,1)}, u32[]{:S(2)}, u32[]{:S(2)}) async-start(bf16[32,80,1024]{2,1,0:T(8,128)(2,1)} %convolution_convert_fusion), calls=%async_computation.1 | async-start | bytes 10485760 | tf_op jit(solution)/shard_map/all_to_all | solution.py:210
  435.2 180.8 %all-reduce.12.cloned.1.call-start = ((), (), s32[]{:S(2)}) async-start(), calls=%async_computation.5 | async-start | bytes 6291456 | tf_op jit(solution)/shard_map/psum | solution.py:359
  452.6 344.8 %all-reduce.10.cloned.1.call-start = ((), (), s32[]{:S(2)}) async-start(), calls=%async_computation.4 | async-start | bytes 25427968 | tf_op jit(solution)/shard_map/psum | solution.py:363
  577.9 22.9 %collective-permute-start.19 = (bf16[256,512]{0,1:T(8,128)(2,1)S(1)}, bf16[256,512]{0,1:T(8,128)(2,1)S(1)}, u32[]{:S(2)}, u32[]{:S(2)}) collective-permute-start(bf16[256,512]{0,1:T(8,128)(2,1)S(1)} %bitcast.365), channel_id=1, source_target_pairs={{64,0},{65,1},{96,32},{97,33},{66,2},{67,3},{98,34},{99,35},{68,4}... | collective-permute-start | bytes 786440 | tf_op jit(solution)/shard_map/ppermute | solution.py:24
  579.4 14.6 %collective-permute-start.15 = (bf16[256,512]{0,1:T(8,128)(2,1)S(1)}, bf16[256,512]{0,1:T(8,128)(2,1)S(1)}, u32[]{:S(2)}, u32[]{:S(2)}) collective-permute-start(bf16[256,512]{0,1:T(8,128)(2,1)S(1)} %bitcast.369), channel_id=1, source_target_pairs={{64,0},{65,1},{96,32},{97,33},{66,2},{67,3},{98,34},{99,35},{68,4}... | collective-permute-start | bytes 786440 | tf_op jit(solution)/shard_map/ppermute | solution.py:24
  580.7 16.9 %collective-permute-start.12 = (bf16[256,512]{0,1:T(8,128)(2,1)S(1)}, bf16[256,512]{0,1:T(8,128)(2,1)S(1)}, u32[]{:S(2)}, u32[]{:S(2)}) collective-permute-start(bf16[256,512]{0,1:T(8,128)(2,1)S(1)} %bitcast.368), channel_id=1, source_target_pairs={{1,0},{32,1},{33,32},{64,33},{65,64},{96,65},{97,96},{3,2},{34,3},... | collective-permute-start | bytes 786440 | tf_op jit(solution)/shard_map/ppermute | solution.py:24
  583.6 15.4 %collective-permute-start.14 = (bf16[256,512]{0,1:T(8,128)(2,1)S(1)}, bf16[256,512]{0,1:T(8,128)(2,1)S(1)}, u32[]{:S(2)}, u32[]{:S(2)}) collective-permute-start(bf16[256,512]{0,1:T(8,128)(2,1)S(1)} %bitcast.367), channel_id=1, source_target_pairs={{33,0},{64,1},{65,32},{96,33},{97,64},{35,2},{66,3},{67,34},{98,35... | collective-permute-start | bytes 786440 | tf_op jit(solution)/shard_map/ppermute | solution.py:24
  584.9 15.6 %collective-permute-start.13 = (bf16[256,512]{0,1:T(8,128)(2,1)S(1)}, bf16[256,512]{0,1:T(8,128)(2,1)S(1)}, u32[]{:S(2)}, u32[]{:S(2)}) collective-permute-start(bf16[256,512]{0,1:T(8,128)(2,1)S(1)} %bitcast.366), channel_id=1, source_target_pairs={{32,0},{33,1},{64,32},{65,33},{96,64},{97,65},{34,2},{35,3},{66,34... | collective-permute-start | bytes 786440 | tf_op jit(solution)/shard_map/ppermute | solution.py:24
  594.1 8.1 collective-permute-start.16
  597.7 9.3 %collective-permute-start.18 = (bf16[256,512]{0,1:T(8,128)(2,1)S(1)}, bf16[256,512]{0,1:T(8,128)(2,1)S(1)}, u32[]{:S(2)}, u32[]{:S(2)}) collective-permute-start(bf16[256,512]{0,1:T(8,128)(2,1)S(1)} %bitcast.363), channel_id=1, source_target_pairs={{33,0},{64,1},{65,32},{96,33},{97,64},{35,2},{66,3},{67,34},{98,35... | collective-permute-start | bytes 786440 | tf_op jit(solution)/shard_map/ppermute | solution.py:24
  599.0 13.0 %collective-permute-start.17 = (bf16[256,512]{0,1:T(8,128)(2,1)S(1)}, bf16[256,512]{0,1:T(8,128)(2,1)S(1)}, u32[]{:S(2)}, u32[]{:S(2)}) collective-permute-start(bf16[256,512]{0,1:T(8,128)(2,1)S(1)} %bitcast.362), channel_id=1, source_target_pairs={{32,0},{33,1},{64,32},{65,33},{96,64},{97,65},{34,2},{35,3},{66,34... | collective-permute-start | bytes 786440 | tf_op jit(solution)/shard_map/ppermute | solution.py:24
  622.6 77.8 %copy-start.55 = (f32[256]{0:T(256)S(1)}, f32[256]{0:T(256)}, u32[]{:S(2)}) copy-start(f32[256]{0:T(256)} %get-tuple-element.56) | copy-start | bytes 3076
  (57 other events, 499.6 us)
Sparse Core Ops, SparseCore 0:
  452.8 77.5 all-reduce.11
  616.1 181.3 all-reduce.9
where the time goes:
time: 828 us; the launch traced here: 816 us
  waiting for transfers between devices  267 us (32%)
  local copies, waits for them, and re-layouts  168 us (20%)
  matrix products  134 us (16%)
  starting transfers between devices  83.1 us (10%)
  blocking collectives  76.6 us (9%)
  other arithmetic  72.1 us (9%)
  between operations  15.6 us (2%)
    psum x1, waiting for transfers between devices, on_device(): lax.psum((attn_gain_grad, query_w_grad, key_w_grad, value_w_grad, out_w_g...  95.9 us
    psum x1, blocking collectives, on_device(): lax.psum((attn_gain_grad, query_w_grad, key_w_grad, value_w_grad, out_w_g...  76.6 us
    all_to_all x1, waiting for transfers between devices, on_device(): lax.all_to_all(row_grad, ('grp', 'exp'), split_axis=0, concat_axis=0, til...  58.1 us
    all_to_all x1, waiting for transfers between devices, on_device(): lax.all_to_all(res_grad_send, ('grp', 'exp'), split_axis=0, concat_axis=0...  53.9 us
    ppermute x20, starting transfers between devices, from_behind(): lax.ppermute(value, axis, [(source, source + steps) for source in range(i...  48 us
    unnamed x147, local copies, waits for them, and re-layouts  32.8 us
    ppermute x20, waiting for transfers between devices, from_behind(): lax.ppermute(value, axis, [(source, source + steps) for source in range(i...  23.4 us
    all_to_all x1, waiting for transfers between devices, on_device(): lax.all_to_all(expert_res, ('grp', 'exp'), split_axis=0, concat_axis=0, t...  20.9 us
  transfers between devices with their start and end apart: 26, of which 10 were waited for; matrix products, arithmetic and copies ran while one was open for 37% of the time, Pallas kernels for 0%

commit v1 on v0

--- a/solution.py
+++ b/solution.py
@@ -1,8 +1,11 @@
+import functools
 import math
 
 import jax
 import jax.numpy as jnp
 from jax import lax
+from jax.experimental import pallas as pl
+from jax.experimental.pallas import tpu as pltpu
 from jax.sharding import PartitionSpec as P
 
 HEADS = 16
@@ -71,28 +74,642 @@
     )
 
 
-def place_pairs(route_ids, rank_ids, experts, capacity):
+MESH = pl.DeviceIdType.MESH
+CAPACITY = 80
+BLOCK = 256
+HALF = 128
+QUARTER = 64
+WIDTH = 1024
+INNER = 512
+PLANE = 16
+GROUP = 4
+BF = jnp.bfloat16
+F32 = jnp.float32
+
+
+def mod4(value):
+    return lax.rem(value + 8, 4)
+
+
+def plane_id(part, first, second):
+    return first * 4 + second if part == 0 else second * 4 + first
+
+
+def plane_coords(part):
+    index = lax.axis_index("grp")
+    row, column = index // 4, lax.rem(index, 4)
+    return (row, column) if part == 0 else (column, row)
+
+
+def plane_copy(source, target, send_sem, recv_sem, index):
+    return pltpu.make_async_remote_copy(
+        src_ref=source,
+        dst_ref=target,
+        send_sem=send_sem,
+        recv_sem=recv_sem,
+        device_id={"grp": index},
+        device_id_type=MESH,
+    )
+
+
+def greet_plane():
+    row, column = plane_coords(0)
+    barrier = pltpu.get_barrier_semaphore()
+    for index in (
+        mod4(row + 1) * 4 + column,
+        mod4(row - 1) * 4 + column,
+        row * 4 + mod4(column + 1),
+        row * 4 + mod4(column - 1),
+    ):
+        pl.semaphore_signal(barrier, inc=1, device_id={"grp": index}, device_id_type=MESH)
+    pl.semaphore_wait(barrier, 4)
+
+
+class PlaneGather:
+    order = {0: 0, -1: 1, 1: 2, 2: 3}
+
+    def __init__(self, part, blocks, send_sems, recv_sems):
+        self.part, self.blocks = part, blocks
+        self.send_sems, self.recv_sems = send_sems, recv_sems
+        self.first, self.second = plane_coords(part)
+        self.started = []
+
+    def ref(self, da, db, half=None):
+        index = plane_id(self.part, mod4(self.first + da), mod4(self.second + db))
+        begin = self.part * HALF
+        if half is None:
+            return self.blocks.at[index, pl.ds(begin, HALF)]
+        return self.blocks.at[index, pl.ds(begin + half * QUARTER, QUARTER)]
+
+    def copy(self, da, db, half, axis, step, slot):
+        if axis == 0:
+            to = plane_id(self.part, mod4(self.first + step), self.second)
+        else:
+            to = plane_id(self.part, self.first, mod4(self.second + step))
+        ref, sem = self.ref(da, db, half), self.part * 20 + slot
+        return plane_copy(ref, ref, self.send_sems.at[sem], self.recv_sems.at[sem], to)
+
+    def send(self, *where):
+        self.copy(*where).start()
+        self.started.append(where)
+
+    def wait(self, da, db, half, slot):
+        ref, sem = self.ref(da, db, half), self.part * 20 + slot
+        plane_copy(
+            ref, ref, self.send_sems.at[sem], self.recv_sems.at[sem],
+            plane_id(self.part, self.first, self.second),
+        ).wait_recv()
+
+    def begin(self):
+        self.send(0, 0, None, 0, 1, 0)
+        self.send(0, 0, None, 0, -1, 1)
+
+    def spread(self, da):
+        slot = 4 + 4 * self.order[da]
+        self.send(da, 0, None, 1, 1, slot)
+        self.send(da, 0, None, 1, -1, slot + 1)
+
+    def forward_first(self):
+        self.wait(-1, 0, None, 0)
+        self.send(-1, 0, 0, 0, 1, 2)
+        self.wait(1, 0, None, 1)
+        self.send(1, 0, 1, 0, -1, 3)
+
+    def forward_second(self, da):
+        slot = 4 + 4 * self.order[da]
+        self.wait(da, -1, None, slot)
+        self.send(da, -1, 0, 1, 1, slot + 2)
+        self.wait(da, 1, None, slot + 1)
+        self.send(da, 1, 1, 1, -1, slot + 3)
+
+    def wait_far_first(self):
+        self.wait(2, 0, 0, 2)
+        self.wait(2, 0, 1, 3)
+
+    def wait_far_second(self, da):
+        slot = 4 + 4 * self.order[da]
+        self.wait(da, 2, 0, slot + 2)
+        self.wait(da, 2, 1, slot + 3)
+
+    def finish(self):
+        for where in self.started:
+            self.copy(*where).wait_send()
+
+
+class PlaneReduce:
+    order = {2: 0, 1: 1, -1: 2, 0: 3}
+
+    def __init__(self, part, partial, buffers, send_sems, recv_sems, total):
+        self.part, self.partial, self.total = part, partial, total
+        self.far, self.near, self.summed, self.far_two, self.near_two = buffers
+        self.send_sems, self.recv_sems = send_sems, recv_sems
+        self.first, self.second = plane_coords(part)
+        self.started = []
+
+    def ref(self, da, db, half=None):
+        index = plane_id(self.part, mod4(self.first + da), mod4(self.second + db))
+        begin = self.part * HALF
+        if half is None:
+            return self.partial.at[index, pl.ds(begin, HALF)]
+        return self.partial.at[index, pl.ds(begin + half * QUARTER, QUARTER)]
+
+    def send(self, source, target, axis, step, slot):
+        if axis == 0:
+            to = plane_id(self.part, mod4(self.first + step), self.second)
+        else:
+            to = plane_id(self.part, self.first, mod4(self.second + step))
+        sem = self.part * 20 + slot
+        copy = plane_copy(source, target, self.send_sems.at[sem], self.recv_sems.at[sem], to)
+        copy.start()
+        self.started.append(copy)
+
+    def wait(self, target, slot):
+        sem = self.part * 20 + slot
+        plane_copy(
+            target, target, self.send_sems.at[sem], self.recv_sems.at[sem],
+            plane_id(self.part, self.first, self.second),
+        ).wait_recv()
+
+    def add(self, target, source):
+        target[...] = (target[...].astype(F32) + source[...].astype(F32)).astype(BF)
+
+    def step_far(self, da):
+        part, place = self.part, self.order[da]
+        self.send(self.ref(da, 2, 0), self.far.at[part, place, 0], 1, 1, 4 * place)
+        self.send(self.ref(da, 2, 1), self.far.at[part, place, 1], 1, -1, 4 * place + 1)
+
+    def step_near(self, da):
+        part, place = self.part, self.order[da]
+        self.wait(self.far.at[part, place, 0], 4 * place)
+        self.add(self.ref(da, 1, 0), self.far.at[part, place, 0])
+        self.send(self.ref(da, 1), self.near.at[part, place, 0], 1, 1, 4 * place + 2)
+        self.wait(self.far.at[part, place, 1], 4 * place + 1)
+        self.add(self.ref(da, -1, 1), self.far.at[part, place, 1])
+        self.send(self.ref(da, -1), self.near.at[part, place, 1], 1, -1, 4 * place + 3)
+
+    def step_sum(self, da):
+        part, place = self.part, self.order[da]
+        self.wait(self.near.at[part, place, 0], 4 * place + 2)
+        self.wait(self.near.at[part, place, 1], 4 * place + 3)
+        value = (
+            self.ref(da, 0)[...].astype(F32)
+            + self.near[part, place, 0].astype(F32)
+            + self.near[part, place, 1].astype(F32)
+        )
+        rows = pl.ds(part * HALF, HALF)
+        if da == 0:
+            self.total[rows] = value
+            self.wait(self.near_two.at[part, 0], 18)
+            self.wait(self.near_two.at[part, 1], 19)
+            self.total[rows] += self.near_two[part, 0].astype(F32) + self.near_two[part, 1].astype(F32)
+            return
+        self.summed[part, place] = value.astype(BF)
+        lower, upper = pl.ds(0, QUARTER), pl.ds(QUARTER, QUARTER)
+        if da == 2:
+            self.send(self.summed.at[part, 0, lower], self.far_two.at[part, 0], 0, 1, 16)
+            self.send(self.summed.at[part, 0, upper], self.far_two.at[part, 1], 0, -1, 17)
+        if da == 1:
+            self.wait(self.far_two.at[part, 0], 16)
+            self.add(self.summed.at[part, 1, lower], self.far_two.at[part, 0])
+            self.send(self.summed.at[part, 1], self.near_two.at[part, 0], 0, 1, 18)
+        if da == -1:
+            self.wait(self.far_two.at[part, 1], 17)
+            self.add(self.summed.at[part, 2, upper], self.far_two.at[part, 1])
+            self.send(self.summed.at[part, 2], self.near_two.at[part, 1], 0, -1, 19)
+
+    def finish(self):
+        for copy in self.started:
+            copy.wait_send()
+
+
+def reduce_buffers():
+    return [
+        pltpu.VMEM((2, 4, 2, QUARTER, WIDTH), BF),
+        pltpu.VMEM((2, 4, 2, HALF, WIDTH), BF),
+        pltpu.VMEM((2, 3, HALF, WIDTH), BF),
+        pltpu.VMEM((2, 2, QUARTER, WIDTH), BF),
+        pltpu.VMEM((2, 2, HALF, WIDTH), BF),
+    ]
+
+
+def run_reduce(reducers):
+    for da in (2, 1, -1, 0):
+        for reducer in reducers:
+            reducer.step_far(da)
+    for da in (2, 1, -1, 0):
+        for reducer in reducers:
+            reducer.step_near(da)
+    for da in (2, 1, -1, 0):
+        for reducer in reducers:
+            reducer.step_sum(da)
+    for reducer in reducers:
+        reducer.finish()
+
+
+def gather_kernel(own_ref, out_ref, blocks, send_sems, recv_sems, local_sem):
+    greet_plane()
+    blocks[lax.axis_index("grp")] = own_ref[...]
+    gathers = [PlaneGather(part, blocks, send_sems, recv_sems) for part in (0, 1)]
+    for gather in gathers:
+        gather.begin()
+    for gather in gathers:
+        gather.spread(0)
+    for gather in gathers:
+        gather.forward_first()
+        gather.spread(-1)
+        gather.spread(1)
+    for gather in gathers:
+        gather.forward_second(0)
+    for gather in gathers:
+        gather.wait_far_first()
+        gather.spread(2)
+    for da in (-1, 1, 2):
+        for gather in gathers:
+            gather.forward_second(da)
+    for da in (0, -1, 1, 2):
+        for gather in gathers:
+            gather.wait_far_second(da)
+    for gather in gathers:
+        gather.finish()
+    copy = pltpu.make_async_copy(blocks, out_ref, local_sem)
+    copy.start()
+    copy.wait()
+
+
+def gather_plane(own):
+    return pl.pallas_call(
+        gather_kernel,
+        out_shape=jax.ShapeDtypeStruct((PLANE, BLOCK, WIDTH), BF),
+        in_specs=[pl.BlockSpec(memory_space=pltpu.VMEM)],
+        out_specs=pl.BlockSpec(memory_space=pl.ANY),
+        scratch_shapes=[
+            pltpu.VMEM((PLANE, BLOCK, WIDTH), BF),
+            pltpu.SemaphoreType.DMA((40,)),
+            pltpu.SemaphoreType.DMA((40,)),
+            pltpu.SemaphoreType.DMA,
+        ],
+        compiler_params=pltpu.CompilerParams(
+            collective_id=0, has_side_effects=True, vmem_limit_bytes=58 << 20
+        ),
+    )(own)
+
+
+def reduce_kernel(partial_ref, out_ref, partial, far, near, summed, far_two, near_two, send_sems, recv_sems, local_sem):
+    copy = pltpu.make_async_copy(partial_ref, partial, local_sem)
+    copy.start()
+    greet_plane()
+    copy.wait()
+    buffers = (far, near, summed, far_two, near_two)
+    run_reduce([PlaneReduce(part, partial, buffers, send_sems, recv_sems, out_ref) for part in (0, 1)])
+
+
+def reduce_plane(partial):
+    return pl.pallas_call(
+        reduce_kernel,
+        out_shape=jax.ShapeDtypeStruct((BLOCK, WIDTH), F32),
+        in_specs=[pl.BlockSpec(memory_space=pl.ANY)],
+        out_specs=pl.BlockSpec(memory_space=pltpu.VMEM),
+        scratch_shapes=[pltpu.VMEM((PLANE, BLOCK, WIDTH), BF)]
+        + reduce_buffers()
+        + [
+            pltpu.SemaphoreType.DMA((40,)),
+            pltpu.SemaphoreType.DMA((40,)),
+            pltpu.SemaphoreType.DMA,
+        ],
+        compiler_params=pltpu.CompilerParams(
+            collective_id=1, has_side_effects=True, vmem_limit_bytes=58 << 20
+        ),
+    )(partial)
+
+
+def dot_tn(left, right):
+    return lax.dot_general(left, right, (((0,), (0,)), ((), ())), preferred_element_type=F32)
+
+
+def dot_nt(left, right):
+    return lax.dot_general(left, right, (((1,), (1,)), ((), ())), preferred_element_type=F32)
+
+
+def dot_nn(left, right):
+    return lax.dot_general(left, right, (((1,), (0,)), ((), ())), preferred_element_type=F32)
+
+
+def expert_kernel(
+    rows_ref,
+    meta_ref,
+    cot_ref,
+    w_in_ref,
+    w_out_ref,
+    row_total_ref,
+    score_out_ref,
+    moe_ref,
+    d_in_ref,
+    d_out_ref,
+    blocks,
+    meta_in,
+    score_send,
+    cots,
+    w_in,
+    w_out,
+    d_in,
+    d_out,
+    row_partial,
+    moe_stage,
+    picks,
+    slot_rows,
+    slot_cots,
+    slot_grads,
+    slot_res,
+    slot_back,
+    far,
+    near,
+    summed,
+    far_two,
+    near_two,
+    send_sems,
+    recv_sems,
+    rsend_sems,
+    rrecv_sems,
+    meta_send,
+    meta_recv,
+    score_ssem,
+    score_rsem,
+    weight_send,
+    weight_recv,
+    local_sems,
+    cot_sems,
+    moe_sems,
+):
+    me = lax.axis_index("grp")
+    core = lax.axis_index("exp")
+    row, column = me // 4, lax.rem(me, 4)
+    barrier = pltpu.get_barrier_semaphore()
+    for step in range(1, PLANE):
+        pl.semaphore_signal(
+            barrier, inc=1, device_id={"grp": lax.rem(me + step, PLANE)}, device_id_type=MESH
+        )
+    pl.semaphore_signal(barrier, inc=1, device_id={"exp": 1 - core}, device_id_type=MESH)
+
+    load_in = pltpu.make_async_copy(w_in_ref, w_in.at[core], local_sems.at[0])
+    load_out = pltpu.make_async_copy(w_out_ref, w_out.at[core], local_sems.at[1])
+    load_in.start()
+    load_out.start()
+    blocks[me] = rows_ref[...]
+    meta_in[me] = meta_ref[me]
+    d_in[...] = jnp.zeros_like(d_in)
+    d_out[...] = jnp.zeros_like(d_out)
+
+    def cot_copy(group, j):
+        shift = group + group // 2 - 2 * (group // 3)
+        index = mod4(row + j) * 4 + mod4(column + shift)
+        return pltpu.make_async_copy(
+            cot_ref.at[index], cots.at[lax.rem(group, 2), j], cot_sems.at[lax.rem(group, 2), j]
+        )
+
+    for j in range(GROUP):
+        cot_copy(0, j).start()
+    pl.semaphore_wait(barrier, PLANE)
+
+    gathers = [PlaneGather(part, blocks, send_sems, recv_sems) for part in (0, 1)]
+    for gather in gathers:
+        gather.begin()
+    for gather in gathers:
+        gather.spread(0)
+    meta_copies = []
+    for step in range(1, PLANE):
+        to = lax.rem(me + step, PLANE)
+        copy = plane_copy(
+            meta_ref.at[to], meta_in.at[me], meta_send.at[step], meta_recv.at[step], to
+        )
+        copy.start()
+        meta_copies.append(copy)
+    weight_copies = []
+    for slot, (source, target) in enumerate(((w_in_ref, w_in), (w_out_ref, w_out))):
+        copy = pltpu.make_async_remote_copy(
+            src_ref=source,
+            dst_ref=target.at[core],
+            send_sem=weight_send.at[slot],
+            recv_sem=weight_recv.at[slot],
+            device_id={"exp": 1 - core},
+            device_id_type=MESH,
+        )
+        copy.start()
+        weight_copies.append(copy)
+    load_in.wait()
+    load_out.wait()
+    for copy in weight_copies:
+        copy.wait()
+    for copy in meta_copies:
+        copy.wait()
+    for gather in gathers:
+        gather.forward_first()
+        gather.spread(-1)
+        gather.spread(1)
+    gathers[1].forward_second(0)
+    for gather in gathers:
+        gather.wait_far_first()
+        gather.spread(2)
+    gathers[1].wait_far_second(0)
+
+    def moe_copy(j, index):
+        return pltpu.make_async_copy(moe_stage.at[j], moe_ref.at[index], moe_sems.at[j])
+
+    @pl.loop(0, 4)
+    def _(group):
+        shift = group + group // 2 - 2 * (group // 3)
+        place = mod4(column + shift)
+        parity = lax.rem(group, 2)
+
+        @pl.when(group == 0)
+        def _():
+            gathers[0].forward_second(0)
+            gathers[0].forward_second(-1)
+            gathers[0].forward_second(1)
+            gathers[0].forward_second(2)
+            gathers[1].forward_second(-1)
+            gathers[1].forward_second(1)
+
+        @pl.when(group == 1)
+        def _():
+            gathers[1].wait_far_second(1)
+            gathers[1].wait_far_second(-1)
+            gathers[1].forward_second(2)
+
+        @pl.when(group == 2)
+        def _():
+            for da in (0, -1, 1, 2):
+                gathers[0].wait_far_second(da)
+            gathers[1].wait_far_second(2)
+
+        @pl.when(group < 3)
+        def _():
+            for j in range(GROUP):
+                cot_copy(group + 1, j).start()
+
+        for j in range(GROUP):
+            cot_copy(group, j).wait()
+
+        for expert in range(2):
+            gates = []
+            for j in range(GROUP):
+                index = mod4(row + j) * 4 + place
+                slots = meta_in[index, pl.ds(expert, 1), :]
+                gate_row = meta_in[index, pl.ds(2 + expert, 1), :]
+                slot_id = lax.broadcasted_iota(jnp.int32, (CAPACITY, BLOCK), 0).astype(F32)
+                hit = slot_id == slots
+                pick = jnp.where(hit, 1.0, 0.0).astype(BF)
+                gate = jnp.sum(jnp.where(hit, gate_row, 0.0), axis=1, keepdims=True)
+                gates.append(gate)
+                here = pl.ds(j * CAPACITY, CAPACITY)
+                picks[j, pl.ds(expert * CAPACITY, CAPACITY), :] = pick
+                slot_rows[here, :] = dot_nn(pick, blocks[index]).astype(BF)
+                cot_rows = dot_nn(pick, cots[parity, j])
+                slot_cots[here, :] = cot_rows.astype(BF)
+                slot_grads[here, :] = (gate * (RESIDUAL_MULT * cot_rows)).astype(BF)
+            gate = jnp.concatenate(gates, axis=0)
+            gate_up = dot_nn(slot_rows[...], w_in[expert])
+            gate_half, up_half = gate_up[:, :INNER], gate_up[:, INNER:]
+            sigmoid = jax.nn.sigmoid(gate_half)
+            activated = gate_half * sigmoid
+            hidden = (activated * up_half).astype(BF)
+            result = dot_nn(hidden, w_out[expert]).astype(BF).astype(F32)
+            scored = RESIDUAL_MULT * jnp.sum(
+                slot_cots[...].astype(F32) * result, axis=1, keepdims=True
+            )
+            slot_res[expert] = (gate * result).astype(BF)
+            hidden_grad = dot_nt(slot_grads[...], w_out[expert])
+            gate_part = hidden_grad * up_half * sigmoid * (1.0 + gate_half * (1.0 - sigmoid))
+            up_part = hidden_grad * activated
+            pair_grad = jnp.concatenate([gate_part.astype(BF), up_part.astype(BF)], axis=1)
+            slot_back[expert] = dot_nt(pair_grad, w_in[expert]).astype(BF)
+            d_out[expert] += dot_tn(hidden, slot_grads[...])
+            d_in[expert] += dot_tn(slot_rows[...], pair_grad)
+            for j in range(GROUP):
+                index = mod4(row + j) * 4 + place
+                pick = picks[j, pl.ds(expert * CAPACITY, CAPACITY), :].astype(F32)
+                spread = jnp.sum(
+                    pick * scored[j * CAPACITY : (j + 1) * CAPACITY], axis=0, keepdims=True
+                )
+                score_send[index, pl.ds(expert, 1), :] = spread
+
+        for j in range(GROUP):
+            index = mod4(row + j) * 4 + place
+            here = pl.ds(j * CAPACITY, CAPACITY)
+            pick = picks[j]
+
+            @pl.when(group > 0)
+            def _():
+                moe_copy(j, index).wait()
+
+            values = jnp.concatenate([slot_res[0, here, :], slot_res[1, here, :]], axis=0)
+            moe_stage[j] = dot_tn(pick, values).astype(BF)
+            moe_copy(j, index).start()
+            values = jnp.concatenate([slot_back[0, here, :], slot_back[1, here, :]], axis=0)
+            row_partial[index] = dot_tn(pick, values).astype(BF)
+
+    for gather in gathers:
+        gather.finish()
+    reducers = [
+        PlaneReduce(
+            part, row_partial, (far, near, summed, far_two, near_two), rsend_sems, rrecv_sems, row_total_ref
+        )
+        for part in (0, 1)
+    ]
+    for da in (2, 1, -1, 0):
+        for reducer in reducers:
+            reducer.step_far(da)
+    score_out_ref[me] = score_send[me]
+    score_copies = []
+    for step in range(1, PLANE):
+        to = lax.rem(me + step, PLANE)
+        copy = plane_copy(
+            score_send.at[to], score_out_ref.at[me], score_ssem.at[step], score_rsem.at[step], to
+        )
+        copy.start()
+        score_copies.append(copy)
+    store_in = pltpu.make_async_copy(d_in, d_in_ref, local_sems.at[0])
+    store_out = pltpu.make_async_copy(d_out, d_out_ref, local_sems.at[1])
+    store_in.start()
+    store_out.start()
+    for da in (2, 1, -1, 0):
+        for reducer in reducers:
+            reducer.step_near(da)
+    for da in (2, 1, -1, 0):
+        for reducer in reducers:
+            reducer.step_sum(da)
+    for reducer in reducers:
+        reducer.finish()
+    for copy in score_copies:
+        copy.wait()
+    for j in range(GROUP):
+        moe_copy(j, j).wait()
+    store_in.wait()
+    store_out.wait()
+
+
+def run_experts(rows, meta, cots, expert_in, expert_out):
+    vmem = pl.BlockSpec(memory_space=pltpu.VMEM)
+    hbm = pl.BlockSpec(memory_space=pl.ANY)
+    dma = pltpu.SemaphoreType.DMA
+    slots = GROUP * CAPACITY
+    return pl.pallas_call(
+        expert_kernel,
+        out_shape=(
+            jax.ShapeDtypeStruct((BLOCK, WIDTH), F32),
+            jax.ShapeDtypeStruct((PLANE, 8, BLOCK), F32),
+            jax.ShapeDtypeStruct((PLANE, BLOCK, WIDTH), BF),
+            jax.ShapeDtypeStruct((2, WIDTH, 2 * INNER), F32),
+            jax.ShapeDtypeStruct((2, INNER, WIDTH), F32),
+        ),
+        in_specs=[vmem, vmem, hbm, hbm, hbm],
+        out_specs=(vmem, vmem, hbm, hbm, hbm),
+        scratch_shapes=[
+            pltpu.VMEM((PLANE, BLOCK, WIDTH), BF),
+            pltpu.VMEM((PLANE, 8, BLOCK), F32),
+            pltpu.VMEM((PLANE, 8, BLOCK), F32),
+            pltpu.VMEM((2, GROUP, BLOCK, WIDTH), BF),
+            pltpu.VMEM((2, WIDTH, 2 * INNER), BF),
+            pltpu.VMEM((2, INNER, WIDTH), BF),
+            pltpu.VMEM((2, WIDTH, 2 * INNER), F32),
+            pltpu.VMEM((2, INNER, WIDTH), F32),
+            pltpu.VMEM((PLANE, BLOCK, WIDTH), BF),
+            pltpu.VMEM((GROUP, BLOCK, WIDTH), BF),
+            pltpu.VMEM((GROUP, 2 * CAPACITY, BLOCK), BF),
+            pltpu.VMEM((slots, WIDTH), BF),
+            pltpu.VMEM((slots, WIDTH), BF),
+            pltpu.VMEM((slots, WIDTH), BF),
+            pltpu.VMEM((2, slots, WIDTH), BF),
+            pltpu.VMEM((2, slots, WIDTH), BF),
+        ]
+        + reduce_buffers()
+        + [dma((40,))] * 4
+        + [dma((PLANE,))] * 4
+        + [dma((2,))] * 3
+        + [dma((2, GROUP)), dma((GROUP,))],
+        compiler_params=pltpu.CompilerParams(
+            collective_id=2, has_side_effects=True, vmem_limit_bytes=VMEM_LIMIT
+        ),
+    )(rows, meta, cots, expert_in, expert_out)
+
+
+VMEM_LIMIT = 63 << 20
+
+
+def place_slots(route_ids, rank_ids, experts):
     tok_rows, top_count = route_ids.shape
-    by_order = (
-        rank_ids[:, :, None] == jnp.arange(top_count, dtype=jnp.int32)[None, None, :]
-    ).astype(jnp.int32)
-    by_expert = (
-        route_ids[:, :, None] == jnp.arange(experts, dtype=jnp.int32)[None, None, :]
-    ).astype(jnp.int32)
-    counts = jnp.sum(by_order[:, :, :, None] * by_expert[:, :, None, :], axis=1)
-    before = (jnp.cumsum(counts, axis=0) - counts).reshape(tok_rows, top_count * experts)
-    totals = jnp.sum(counts, axis=0)
-    offsets = (jnp.cumsum(totals, axis=0) - totals).reshape(top_count * experts)
-    flat_index = rank_ids * experts + route_ids
-    slot_place = jnp.take_along_axis(before, flat_index, axis=1) + offsets[flat_index]
-    destination = jnp.where(
-        slot_place < capacity, route_ids * capacity + slot_place, experts * capacity
-    )
-    source = jnp.full((experts * capacity + 1,), tok_rows * top_count, jnp.int32)
-    source = source.at[destination.reshape(-1)].set(
-        jnp.arange(tok_rows * top_count, dtype=jnp.int32)
-    )
-    return (destination, source[: experts * capacity])
+    hits = route_ids[:, :, None] == jnp.arange(experts, dtype=jnp.int32)
+    rank_of = jnp.sum(jnp.where(hits, rank_ids[:, :, None] + 1, 0), axis=1) - 1
+    chosen = rank_of >= 0
+    ranks = jnp.arange(top_count, dtype=jnp.int32)
+    counts = (rank_of[:, None, :] == ranks[None, :, None]).reshape(tok_rows, top_count * experts)
+    lowered = counts.astype(BF)
+    tok = jnp.arange(tok_rows, dtype=jnp.int32)
+    earlier = (tok[:, None] > tok[None, :]).astype(BF)
+    before = product(earlier, lowered)
+    totals = jnp.sum(counts.astype(F32), axis=0).reshape(top_count, experts)
+    offsets = (jnp.cumsum(totals, axis=0) - totals).reshape(1, top_count * experts)
+    place = jnp.where(counts, before + offsets, 0.0).reshape(tok_rows, top_count, experts)
+    return chosen, jnp.sum(place, axis=1)
 
 
 def on_device(
@@ -113,16 +730,12 @@
 ):
     tok_rows = tokens.shape[1]
     model_width = tokens.shape[2]
-    top_count = routes.shape[2]
     experts = w_router.shape[1]
-    local_experts = expert_in.shape[0]
-    inner_width = expert_out.shape[1]
     kv_width = w_key.shape[1]
     kv_heads = KV_HEADS
     head_dim = HEAD
     q_heads = HEADS
     group_size = q_heads // kv_heads
-    capacity = 5 * tok_rows * top_count // (4 * experts)
     blocks = lax.axis_size(("seq", "exp"))
     block_id = lax.axis_index(("seq", "exp"))
     hop_count = min(-(-WINDOW // tok_rows), blocks - 1)
@@ -191,88 +804,36 @@
     scale_two = lax.rsqrt(jnp.mean(residual * residual, axis=-1, keepdims=True) + EPSILON)
     routed_in = (residual * scale_two * ffn_gain).astype(jnp.bfloat16)
     logits = product(routed_in, w_router)
-    picked = jnp.take_along_axis(logits, route_ids, axis=1)
-    gate_weights = jax.nn.softmax(picked, axis=1)
-    destination, source = place_pairs(route_ids, rank_ids, experts, capacity)
-    token_of_slot = source // top_count
-    padded_in = jnp.concatenate([routed_in, jnp.zeros((1, model_width), jnp.bfloat16)], axis=0)
-    send_rows = padded_in[token_of_slot].reshape(experts, capacity, model_width)
-    arrived = lax.all_to_all(send_rows, ("grp", "exp"), split_axis=0, concat_axis=0, tiled=True)
-    by_source = arrived.reshape(-1, local_experts, arrived.shape[1], model_width)
-    gate_up = jnp.einsum("nxcd,xdf->nxcf", by_source, expert_in, preferred_element_type=jnp.float32)
-    hidden = (jax.nn.silu(gate_up[..., :inner_width]) * gate_up[..., inner_width:]).astype(
-        jnp.bfloat16
-    )
-    result = jnp.einsum(
-        "nxcf,xfd->nxcd", hidden, expert_out, preferred_element_type=jnp.float32
-    ).astype(jnp.bfloat16)
-    expert_res = result.reshape(arrived.shape)
-    returned = lax.all_to_all(expert_res, ("grp", "exp"), split_axis=0, concat_axis=0, tiled=True)
-    flat_res = jnp.concatenate(
+    chosen, slot_place = place_slots(route_ids, rank_ids, experts)
+    gates = jax.nn.softmax(jnp.where(chosen, logits, MASKED), axis=1)
+    gates = jnp.where(chosen, gates, 0.0)
+    kept_place = jnp.where(chosen & (slot_place < CAPACITY), slot_place, -1.0)
+    meta = jnp.concatenate(
         [
-            returned.reshape(experts * capacity, model_width),
-            jnp.zeros((1, model_width), jnp.bfloat16),
+            kept_place.T.reshape(PLANE, 2, tok_rows),
+            gates.T.reshape(PLANE, 2, tok_rows),
+            jnp.zeros((PLANE, 4, tok_rows), jnp.float32),
         ],
-        axis=0,
-    )
-    gathered = flat_res[destination].astype(jnp.float32)
-    moe_out = jnp.sum(gate_weights[:, :, None] * gathered, axis=1)
+        axis=1,
+    )
+    cots = gather_plane(cotangent[0])
+    expert_row_sum, scores, moe_partial, d_in, d_out = run_experts(
+        routed_in, meta, cots, expert_in[0], expert_out[0]
+    )
+    moe_out = reduce_plane(moe_partial)
     output = (residual + RESIDUAL_MULT * moe_out).astype(jnp.bfloat16)[None]
     upstream = cotangent[0].astype(jnp.float32)
-    moe_grad = RESIDUAL_MULT * upstream
-    gate_grad = jnp.sum(moe_grad[:, None, :] * gathered, axis=-1)
-    slot_gate = jnp.concatenate([gate_weights.reshape(-1), jnp.zeros((1,), jnp.float32)], axis=0)[
-        source
-    ]
-    padded_grad = jnp.concatenate([moe_grad, jnp.zeros((1, model_width), jnp.float32)], axis=0)
-    res_grad_send = (
-        (padded_grad[token_of_slot] * slot_gate[:, None])
-        .astype(jnp.bfloat16)
-        .reshape(experts, capacity, model_width)
-    )
-    rows_at, res_grad_at = (
-        lax.all_to_all(send_rows, ("grp", "exp"), split_axis=0, concat_axis=0, tiled=True),
-        lax.all_to_all(res_grad_send, ("grp", "exp"), split_axis=0, concat_axis=0, tiled=True),
-    )
-    by_source = rows_at.reshape(-1, local_experts, capacity, model_width)
-    out_grid = res_grad_at.reshape(-1, local_experts, capacity, model_width)
-    gate_up = jnp.einsum("nxcd,xdf->nxcf", by_source, expert_in, preferred_element_type=jnp.float32)
-    gate_half = gate_up[..., :inner_width]
-    up_half = gate_up[..., inner_width:]
-    sigmoid_gate = jax.nn.sigmoid(gate_half)
-    activated = jax.nn.silu(gate_half)
-    hidden = (activated * up_half).astype(jnp.bfloat16)
-    hidden_grad = jnp.einsum(
-        "nxcd,xfd->nxcf", out_grid, expert_out, preferred_element_type=jnp.float32
-    )
-    gate_part = hidden_grad * up_half * sigmoid_gate * (1.0 + gate_half * (1.0 - sigmoid_gate))
-    up_part = hidden_grad * activated
-    pair_grad = jnp.concatenate([gate_part, up_part], axis=-1).astype(jnp.bfloat16)
-    down_w_grad = jnp.einsum("nxcf,nxcd->xfd", hidden, out_grid, preferred_element_type=jnp.float32)
-    up_w_grad = jnp.einsum(
-        "nxcd,nxcf->xdf", by_source, pair_grad, preferred_element_type=jnp.float32
-    )
-    row_grad = (
-        jnp.einsum("nxcf,xdf->nxcd", pair_grad, expert_in, preferred_element_type=jnp.float32)
-        .astype(jnp.bfloat16)
-        .reshape(-1, capacity, model_width)
-    )
-    row_back = lax.all_to_all(row_grad, ("grp", "exp"), split_axis=0, concat_axis=0, tiled=True)
-    flat_back = jnp.concatenate(
-        [
-            row_back.reshape(experts * capacity, model_width),
-            jnp.zeros((1, model_width), jnp.bfloat16),
-        ],
-        axis=0,
-    )
-    expert_row_sum = jnp.sum(flat_back[destination].astype(jnp.float32), axis=1)
-    choice_grad = gate_weights * (
-        gate_grad - jnp.sum(gate_weights * gate_grad, axis=1, keepdims=True)
-    )
-    onehot = (route_ids[:, :, None] == jnp.arange(experts, dtype=jnp.int32)[None, None, :]).astype(
-        jnp.float32
-    )
-    logit_grad = jnp.sum(onehot * choice_grad[:, :, None], axis=1).astype(jnp.bfloat16)
+    core = lax.axis_index("exp")
+
+    def pair_sum(value):
+        other = lax.dynamic_index_in_dim(value, 1 - core, 0, keepdims=True).astype(jnp.bfloat16)
+        own = lax.dynamic_index_in_dim(value, core, 0, keepdims=True)
+        return own + lax.ppermute(other, "exp", [(0, 1), (1, 0)]).astype(jnp.float32)
+
+    up_w_grad, down_w_grad = pair_sum(d_in), pair_sum(d_out)
+    gate_grad = scores[:, :2, :].reshape(experts, tok_rows).T
+    choice_grad = gates * (gate_grad - jnp.sum(gates * gate_grad, axis=1, keepdims=True))
+    logit_grad = choice_grad.astype(jnp.bfloat16)
     router_w_grad = inner_rows(routed_in, logit_grad)
     routed_grad = product_back(logit_grad, w_router) + expert_row_sum
     normal_two = residual * scale_two

time: 828 us -> 749 us (0.905)
  Pallas kernels: 0 us -> 237 us
  local copies, waits for them, and re-layouts: 168 us -> 49.4 us
  waiting for transfers between devices: 267 us -> 177 us
  matrix products: 134 us -> 86.4 us
  other arithmetic: 72.1 us -> 42.7 us
  starting transfers between devices: 83.1 us -> 57.6 us
    pallas_call x0 -> x3, Pallas kernels: none -> 237 us  [the longest x1 135 us: run_experts(): pl.pallas_call(expert_kernel, out_shape=(jax.ShapeDtypeStruct((BLOCK, WID...]
    all_to_all x4 -> x0, waiting for transfers between devices: 147 us -> none  [the longest x1 58.1 us: on_device(): lax.all_to_all(row_grad, ('grp', 'exp'), split_axis=0, concat_axis=0, til...]
    gather x13 -> x0, local copies, waits for them, and re-layouts: 107 us -> none  [the longest x3 17 us: on_device(): picked = jnp.take_along_axis(logits, route_ids, axis=1)]
    dot_general x6 -> x0, matrix products: 52.7 us -> none  [the longest x1 11.5 us: on_device(): jnp.einsum('nxcd,xfd->nxcf', out_grid, expert_out, preferred_element_type...]
    psum x1, waiting for transfers between devices: 95.9 us -> 135 us  [on_device(): lax.psum((attn_gain_grad, query_w_grad, key_w_grad, value_w_grad, out_w_g...]
    all_to_all x4 -> x0, starting transfers between devices: 35.1 us -> none  [the longest x1 9.13 us: on_device(): lax.all_to_all(res_grad_send, ('grp', 'exp'), split_axis=0, concat_axis=0...]
    ppermute x20, waiting for transfers between devices: 23.4 us -> 41.8 us  [from_behind(): lax.ppermute(value, axis, [(source, source + steps) for source in range(i...]
    another operation x5 -> x2, other arithmetic: 19.1 us -> 1.01 us
  transfers between devices with their start and end apart: 26 -> 24, of which waited for: 10 -> 8; matrix products, arithmetic and copies ran while one was open for 37% -> 15% of each run, Pallas kernels for 0% -> 7%
where the time goes in v1:
time: 749 us; the launch traced here: 740 us
  Pallas kernels  237 us (32%)
  waiting for transfers between devices  177 us (24%)
  matrix products  86.4 us (12%)
  blocking collectives  74.4 us (10%)
  starting transfers between devices  57.6 us (8%)
  local copies, waits for them, and re-layouts  49.4 us (7%)
  other arithmetic  42.7 us (6%)
  between operations  15.5 us (2%)
    psum x1, waiting for transfers between devices, on_device(): lax.psum((attn_gain_grad, query_w_grad, key_w_grad, value_w_grad, out_w_g...  135 us
    pallas_call x1, Pallas kernels, run_experts(): pl.pallas_call(expert_kernel, out_shape=(jax.ShapeDtypeStruct((BLOCK, WID...  135 us
    psum x1, blocking collectives, on_device(): lax.psum((attn_gain_grad, query_w_grad, key_w_grad, value_w_grad, out_w_g...  74.4 us
    pallas_call x1, Pallas kernels, gather_plane(): pl.pallas_call(gather_kernel, out_shape=jax.ShapeDtypeStruct((PLANE, BLOC...  53.4 us
    ppermute x20, starting transfers between devices, from_behind(): lax.ppermute(value, axis, [(source, source + steps) for source in range(i...  51.6 us
    pallas_call x1, Pallas kernels, reduce_plane(): pl.pallas_call(reduce_kernel, out_shape=jax.ShapeDtypeStruct((BLOCK, WIDT...  48.1 us
    ppermute x20, waiting for transfers between devices, from_behind(): lax.ppermute(value, axis, [(source, source + steps) for source in range(i...  41.8 us
    unnamed x127, local copies, waits for them, and re-layouts  31.8 us
  transfers between devices with their start and end apart: 24, of which 8 were waited for; matrix products, arithmetic and copies ran while one was open for 15% of the time, Pallas kernels for 7%

profile of v1, /device:TPU:1, one launch (start us, length us, event | category | flops | bytes accessed | tf_op | source)
XLA Modules:
  0.0 739.9 jit_solution(11080869379959027807)
XLA Ops:
  7.3 4.5 collective-permute-start.7
  11.8 3.7 collective-permute-start.6
  15.5 3.4 collective-permute-start.5
  41.7 53.4 %shard_map.221.cot_ref = bf16[16,256,1024]{2,1,0:T(8,128)(2,1)} custom-call(bf16[256,1024]{1,0:T(8,128)(2,1)} %bitcast.243), custom_call_target="tpu_custom_call" | custom-call | tf_op jit(solution)/shard_map/pallas_call | solution.py:340
  107.7 4.5 collective-permute-done
  114.3 11.1 %collective-permute-start.9 = (bf16[256,512]{0,1:T(8,128)(2,1)}, bf16[256,512]{0,1:T(8,128)(2,1)}, u32[]{:S(2)}, u32[]{:S(2)}) collective-permute-start(bf16[256,512]{0,1:T(8,128)(2,1)} %bitcast.9), channel_id=1, source_target_pairs={{0,33},{1,64},{32,65},{33,96},{64,97},{2,35},{3,66},{34,67},{35,98... | collective-permute-start | bytes 786440 | tf_op jit(solution)/shard_map/ppermute | solution.py:27
  128.7 5.6 collective-permute-done.8
  138.9 11.5 %exponential_reduce_fusion = (f32[8,2,256]{2,1,0:T(2,128)S(1)}, f32[8,2,256,1280]{2,3,1,0:T(8,128)}) fusion(pred[256,1280]{0,1:T(8,128)(4,1)S(1)} %copy-done.33, bf16[1280,8,64]{0,2,1:T(8,128)(2,1)S(1)} %constant_dynamic-update-slice_fusion.6, bf16[256,8,2,32]{0,3,2,1:T(8,128)(2,1)S(1)} %bitcast.256, bf16[256,8,2,32]{0,3,2,1:T(8,128)(2,1)S(1)} %bitcast.251), kind=kOutput, calls=%fused_computation.9 | convolution fusion | flops 693110016 | bytes 23150592 | tf_op jit(solution)/shard_map/sub | solution.py:791
  150.5 11.9 %fusion.30 = bf16[8,64,2,256]{3,1,2,0:T(8,128)(2,1)S(1)} fusion(bf16[1280,8,64,1]{0,2,3,1:T(8,128)(2,1)} %bitcast.249, f32[8,2,256]{2,1,0:T(2,128)S(1)} %get-tuple-element.60, pred[256,1280]{0,1:T(8,128)(4,1)} %fusion.29, bf16[1280,8,64]{0,2,1:T(8,128)(2,1)} %copy-done.16, bf16[256,8,2,32]{0,3,2,1:T(8,128)(2,1)} %bitcast.255, ...), kind=kOutput, calls=%fused_computation.44 | convolution fusion | flops 1369707776 | bytes 4014080 | tf_op jit(solution)/shard_map/uzjq,quk->juzk/dot_general | solution.py:793
  167.5 135.2 %shard_map.222 = (f32[256,1024]{1,0:T(8,128)}, f32[16,8,256]{2,1,0:T(8,128)}, bf16[16,256,1024]{2,1,0:T(8,128)(2,1)}, f32[2,1024,1024]{2,1,0:T(8,128)}, f32[2,512,1024]{2,1,0:T(8,128)}) custom-call(bf16[256,1024]{1,0:T(8,128)(2,1)} %copy-done.9, f32[16,8,256]{2,1,0:T(8,128)} %maximum_maximum_fusion.meta_ref, bf16[16,256,1024]{2,1,0:T(8,128)(2,1)} %shard_map.221.cot_ref, ...), custom_call_target="tpu_custom_call" | custom-call | tf_op jit(solution)/shard_map/pallas_call | solution.py:655
  302.7 48.1 %shard_map.223 = f32[256,1024]{1,0:T(8,128)} custom-call(bf16[16,256,1024]{2,1,0:T(8,128)(2,1)} %get-tuple-element.16.partial_ref), custom_call_target="tpu_custom_call" | custom-call | tf_op jit(solution)/shard_map/pallas_call | solution.py:367
  359.9 2.9 dynamic-slice_convert_fusion.1
  362.8 5.9 collective-permute-start.21
  368.7 3.9 dynamic-slice_convert_fusion
  372.7 13.3 %fusion.2 = (f32[8,2,256]{2,1,0:T(2,128)S(1)}, f32[8,1280,256,2]{2,1,3,0:T(8,128)}) fusion(f32[8,2,256]{2,1,0:T(2,128)S(1)} %copy-done.45, f32[8,2,256,1280]{2,3,1,0:T(8,128)} %get-tuple-element.61, bf16[1280,8,64,1]{0,2,3,1:T(8,128)(2,1)S(1)} %bitcast.250, bf16[256,8,2,64]{0,3,2,1:T(8,128)(2,1)S(1)} %bitcast.262), kind=kOutput, calls=%fused_computation.4 | convolution fusion | flops 686813184 | bytes 43810816 | tf_op jit(solution)/shard_map/dklp,okp->kldo/dot_general | solution.py:857
  386.0 14.4 %fusion.4 = bf16[8,2,256,1280]{2,3,1,0:T(8,128)(2,1)S(1)} fusion(f32[8,1280,256,2]{2,1,3,0:T(8,128)} %get-tuple-element.68, f32[8,2,256]{2,1,0:T(2,128)S(1)} %get-tuple-element.67, f32[8,2,256]{2,1,0:T(2,128)S(1)} %copy-done.45, f32[8,2,256,1280]{2,3,1,0:T(8,128)} %get-tuple-element.61), kind=kLoop, calls=%fused_computation.6 | loop fusion | flops 20971520 | bytes 52461568 | tf_op jit(solution)/shard_map/convert_element_type | solution.py:862
  400.5 4.0 copy-done.2
  404.5 4.8 fusion.101
  409.3 13.2 %fusion.102 = (bf16[1280,8,64]{0,2,1:T(8,128)(2,1)}, f32[1280,8,64]{0,2,1:T(8,128)}) fusion(bf16[256,8,2,64]{0,3,2,1:T(8,128)(2,1)} %bitcast.263, f32[8,2,256]{2,1,0:T(2,128)S(1)} %copy-done.45, pred[256,1280]{0,1:T(8,128)(4,1)} %fusion.29, bf16[1280,8,64]{0,2,1:T(8,128)(2,1)} %copy-done.16, bf16[256,8,2,32]{0,3,2,1:T(8,128)(2,1)S(1)} %bitcast.258, ...), kind=kOutput, calls=%fused_computation.166 | convolution fusion | flops 1370100992 | bytes 6635520 | tf_op jit(solution)/shard_map/ykze,zykm->eym/dot_general | solution.py:872
  422.4 7.6 %convolution_multiply_fusion = f32[8,64,2,256]{3,1,2,0:T(8,128)} fusion(bf16[8,2,256,1280]{2,3,1,0:T(8,128)(2,1)} %copy-done.2, bf16[1280,8,64]{0,2,1:T(8,128)(2,1)} %copy-done.16), kind=kOutput, calls=%fused_computation.24 | convolution fusion | flops 671350784 | bytes 12845056 | tf_op jit(solution)/shard_map/uzjq,quk->juzk/dot_general | solution.py:863
  432.6 4.9 add_convert_fusion
  449.8 2.9 fusion.60
  455.8 10.6 %collective-permute-done.15 = bf16[256,512]{0,1:T(8,128)(2,1)S(1)} collective-permute-done((bf16[256,512]{0,1:T(8,128)(2,1)S(1)}, bf16[256,512]{0,1:T(8,128)(2,1)S(1)}, u32[]{:S(2)}, u32[]{:S(2)}) %collective-permute-start.15) | collective-permute-done | bytes 262176 | tf_op jit(solution)/shard_map/ppermute | solution.py:27
  466.4 4.2 collective-permute-start.16
  471.9 4.5 collective-permute-done.14
  478.0 3.9 collective-permute-done.16
  481.9 3.7 collective-permute-done.18
  485.6 9.0 %collective-permute-done.17 = bf16[256,512]{0,1:T(8,128)(2,1)S(1)} collective-permute-done((bf16[256,512]{0,1:T(8,128)(2,1)S(1)}, bf16[256,512]{0,1:T(8,128)(2,1)S(1)}, u32[]{:S(2)}, u32[]{:S(2)}) %collective-permute-start.17) | collective-permute-done | bytes 262176 | tf_op jit(solution)/shard_map/ppermute | solution.py:27
  502.9 74.4 %all-reduce = (f32[1024]{0:T(1024)}, f32[1024]{0:T(1024)}) all-reduce(f32[1024]{0:T(1024)S(1)} %get-tuple-element.23, f32[1024]{0:T(1024)S(1)} %get-tuple-element.21), channel_id=1, replica_groups=mesh['seq'=4,'grp'=16,'exp'=2] {'seq','grp','exp'}, use_global_device_ids=true, to_apply=%region_15.16 | all-reduce | flops 2048 | bytes 16384 | tf_op jit(solution)/shard_map/psum | solution.py:924
  578.5 4.2 convert_element_type.240
  584.3 135.4 %all-reduce.6.cloned.1.call-done = (f32[1024,1024]{1,0:T(8,128)}, f32[1024,512]{1,0:T(8,128)}, f32[1024,512]{1,0:T(8,128)}, f32[1024,1024]{1,0:T(8,128)}, f32[1024,32]{0,1:T(8,128)}) async-done(((f32[1024,1024]{1,0:T(8,128)}, f32[1024,512]{1,0:T(8,128)}, f32[1024,512]{1,0:T(8,128)}, f32[1024,1024]{1,0:T(8,128)}, f32[1024,32]{0,1:T(8,128)}), (f32[1024,1024]{1,0:T(8,128)}, f32[1024,512]{1,0:T(8,128)}, ...) | async-done | bytes 12714000 | tf_op jit(solution)/shard_map/psum | solution.py:924
  719.7 4.9 copy.92
  (235 shorter events, 98.7 us)
Async XLA Ops:
  7.2 158.1 %copy-start = (bf16[1024,32]{0,1:T(8,128)(2,1)S(1)}, bf16[1024,32]{0,1:T(8,128)(2,1)}, u32[]{:S(2)}) copy-start(bf16[1024,32]{0,1:T(8,128)(2,1)} %param.24) | copy-start | bytes 196612
  7.2 571.3 %all-reduce.8.cloned.1.call-start = ((), (), s32[]{:S(2)}) async-start(), calls=%async_computation.1 | async-start | bytes 6291456 | tf_op jit(solution)/shard_map/psum | solution.py:920
  7.3 95.5 %collective-permute-start.7 = (s32[256]{0:T(256)}, s32[256]{0:T(256)}, u32[]{:S(2)}, u32[]{:S(2)}) collective-permute-start(s32[256]{0:T(256)} %bitcast.274), channel_id=1, source_target_pairs={{0,1},{1,32},{32,33},{33,64},{64,65},{65,96},{96,97},{2,3},{3,34},... | collective-permute-start | bytes 3080 | tf_op jit(solution)/shard_map/ppermute | solution.py:27
  11.8 89.0 %collective-permute-start.6 = (s32[256]{0:T(256)}, s32[256]{0:T(256)}, u32[]{:S(2)}, u32[]{:S(2)}) collective-permute-start(s32[256]{0:T(256)} %bitcast.275), channel_id=1, source_target_pairs={{0,32},{1,33},{32,64},{33,65},{64,96},{65,97},{2,34},{3,35},{34,66... | collective-permute-start | bytes 3080 | tf_op jit(solution)/shard_map/ppermute | solution.py:27
  15.5 82.1 %collective-permute-start.5 = (s32[256]{0:T(256)}, s32[256]{0:T(256)}, u32[]{:S(2)}, u32[]{:S(2)}) collective-permute-start(s32[256]{0:T(256)} %bitcast.276), channel_id=1, source_target_pairs={{0,33},{1,64},{32,65},{33,96},{64,97},{2,35},{3,66},{34,67},{35,98... | collective-permute-start | bytes 3080 | tf_op jit(solution)/shard_map/ppermute | solution.py:27
  18.9 76.7 %collective-permute-start.4 = (s32[256]{0:T(256)}, s32[256]{0:T(256)}, u32[]{:S(2)}, u32[]{:S(2)}) collective-permute-start(s32[256]{0:T(256)} %bitcast.277), channel_id=1, source_target_pairs={{0,64},{1,65},{32,96},{33,97},{2,66},{3,67},{34,98},{35,99},{4,68}... | collective-permute-start | bytes 3080 | tf_op jit(solution)/shard_map/ppermute | solution.py:27
  25.2 101.6 %collective-permute-start.3 = (bf16[256,512]{1,0:T(8,128)(2,1)}, bf16[256,512]{1,0:T(8,128)(2,1)}, u32[]{:S(2)}, u32[]{:S(2)}) collective-permute-start(bf16[256,512]{1,0:T(8,128)(2,1)} %convolution_convert_fusion.1), channel_id=1, source_target_pairs={{0,1},{1,32},{32,33},{33,64},{64,65},{65,96},{96,97},{2,3},{3,34},... | collective-permute-start | bytes 786440 | tf_op jit(solution)/shard_map/ppermute | solution.py:27
  39.2 55.8 %copy-start.30 = (f32[256,32]{0,1:T(8,128)}, f32[256,32]{0,1:T(8,128)S(1)}, u32[]{:S(2)}) copy-start(f32[256,32]{0,1:T(8,128)S(1)} %get-tuple-element.55) | copy-start | bytes 98308
  41.7 63.9 %copy-start.52 = (s32[1,256]{1,0:T(1,128)S(1)}, s32[1,256]{1,0:T(1,128)}, u32[]{:S(2)}) copy-start(s32[1,256]{1,0:T(1,128)} %param.15) | copy-start | bytes 3076
  41.7 64.0 %copy-start.42 = (s32[1280]{0:T(1024)S(1)}, s32[1280]{0:T(1024)}, u32[]{:S(2)}) copy-start(s32[1280]{0:T(1024)} %iota_add_fusion) | copy-start | bytes 15364
  41.7 64.0 %copy-start.48 = (pred[1280]{0:T(1024)(128)(4,1)S(1)}, pred[1280]{0:T(1024)(128)(4,1)}, u32[]{:S(2)}) copy-start(pred[1280]{0:T(1024)(128)(4,1)} %broadcast_compare_fusion.1) | copy-start | bytes 3844
  95.6 29.8 %collective-permute-start.2 = (bf16[256,512]{1,0:T(8,128)(2,1)}, bf16[256,512]{1,0:T(8,128)(2,1)S(1)}, u32[]{:S(2)}, u32[]{:S(2)}) collective-permute-start(bf16[256,512]{1,0:T(8,128)(2,1)} %convolution_convert_fusion.1), channel_id=1, source_target_pairs={{0,32},{1,33},{32,64},{33,65},{64,96},{65,97},{2,34},{3,35},{34,66... | collective-permute-start | bytes 786440 | tf_op jit(solution)/shard_map/ppermute | solution.py:27
  97.6 16.7 %collective-permute-start.1 = (bf16[256,512]{1,0:T(8,128)(2,1)}, bf16[256,512]{1,0:T(8,128)(2,1)S(1)}, u32[]{:S(2)}, u32[]{:S(2)}) collective-permute-start(bf16[256,512]{1,0:T(8,128)(2,1)} %convolution_convert_fusion.1), channel_id=1, source_target_pairs={{0,33},{1,64},{32,65},{33,96},{64,97},{2,35},{3,66},{34,67},{35,98... | collective-permute-start | bytes 786440 | tf_op jit(solution)/shard_map/ppermute | solution.py:27
  100.8 11.5 %collective-permute-start = (bf16[256,512]{1,0:T(8,128)(2,1)}, bf16[256,512]{1,0:T(8,128)(2,1)S(1)}, u32[]{:S(2)}, u32[]{:S(2)}) collective-permute-start(bf16[256,512]{1,0:T(8,128)(2,1)} %convolution_convert_fusion.1), channel_id=1, source_target_pairs={{0,64},{1,65},{32,96},{33,97},{2,66},{3,67},{34,98},{35,99},{4,68}... | collective-permute-start | bytes 786440 | tf_op jit(solution)/shard_map/ppermute | solution.py:27
  102.8 35.1 %collective-permute-start.11 = (bf16[256,512]{0,1:T(8,128)(2,1)}, bf16[256,512]{0,1:T(8,128)(2,1)}, u32[]{:S(2)}, u32[]{:S(2)}) collective-permute-start(bf16[256,512]{0,1:T(8,128)(2,1)} %bitcast.9), channel_id=1, source_target_pairs={{0,1},{1,32},{32,33},{33,64},{64,65},{65,96},{96,97},{2,3},{3,34},... | collective-permute-start | bytes 786440 | tf_op jit(solution)/shard_map/ppermute | solution.py:27
  112.3 24.6 %collective-permute-start.10 = (bf16[256,512]{0,1:T(8,128)(2,1)}, bf16[256,512]{0,1:T(8,128)(2,1)}, u32[]{:S(2)}, u32[]{:S(2)}) collective-permute-start(bf16[256,512]{0,1:T(8,128)(2,1)} %bitcast.9), channel_id=1, source_target_pairs={{0,32},{1,33},{32,64},{33,65},{64,96},{65,97},{2,34},{3,35},{34,66... | collective-permute-start | bytes 786440 | tf_op jit(solution)/shard_map/ppermute | solution.py:27
  114.3 21.5 %collective-permute-start.9 = (bf16[256,512]{0,1:T(8,128)(2,1)}, bf16[256,512]{0,1:T(8,128)(2,1)}, u32[]{:S(2)}, u32[]{:S(2)}) collective-permute-start(bf16[256,512]{0,1:T(8,128)(2,1)} %bitcast.9), channel_id=1, source_target_pairs={{0,33},{1,64},{32,65},{33,96},{64,97},{2,35},{3,66},{34,67},{35,98... | collective-permute-start | bytes 786440 | tf_op jit(solution)/shard_map/ppermute | solution.py:27
  125.4 8.9 %collective-permute-start.8 = (bf16[256,512]{0,1:T(8,128)(2,1)}, bf16[256,512]{0,1:T(8,128)(2,1)S(1)}, u32[]{:S(2)}, u32[]{:S(2)}) collective-permute-start(bf16[256,512]{0,1:T(8,128)(2,1)} %bitcast.9), channel_id=1, source_target_pairs={{0,64},{1,65},{32,96},{33,97},{2,66},{3,67},{34,98},{35,99},{4,68}... | collective-permute-start | bytes 786440 | tf_op jit(solution)/shard_map/ppermute | solution.py:27
  302.7 52.8 %copy-start.5 = (f32[256,1024]{1,0:T(8,128)S(1)}, f32[256,1024]{1,0:T(8,128)}, u32[]{:S(2)}) copy-start(f32[256,1024]{1,0:T(8,128)} %copy-done.4) | copy-start | bytes 3145732
  302.7 52.8 %copy-start.29 = (f32[256,1024]{1,0:T(8,128)S(1)}, f32[256,1024]{1,0:T(8,128)}, u32[]{:S(2)}) copy-start(f32[256,1024]{1,0:T(8,128)} %get-tuple-element.18) | copy-start | bytes 3145732
  362.8 67.3 %collective-permute-start.21 = (bf16[1,512,1024]{2,1,0:T(8,128)(2,1)}, bf16[1,512,1024]{2,1,0:T(8,128)(2,1)}, u32[]{:S(2)}, u32[]{:S(2)}) collective-permute-start(bf16[1,512,1024]{2,1,0:T(8,128)(2,1)} %dynamic-slice_convert_fusion.1), channel_id=1, source_target_pairs={{0,1},{1,0},{2,3},{3,2},{4,5},{5,4},{6,7},{7,6},{8,9},{9,8},{10,11... | collective-permute-start | bytes 3145736 | tf_op jit(solution)/shard_map/ppermute | solution.py:831
  372.7 59.9 %collective-permute-start.20 = (bf16[1,1024,1024]{2,1,0:T(8,128)(2,1)}, bf16[1,1024,1024]{2,1,0:T(8,128)(2,1)}, u32[]{:S(2)}, u32[]{:S(2)}) collective-permute-start(bf16[1,1024,1024]{2,1,0:T(8,128)(2,1)} %dynamic-slice_convert_fusion), channel_id=1, source_target_pairs={{0,1},{1,0},{2,3},{3,2},{4,5},{5,4},{6,7},{7,6},{8,9},{9,8},{10,11... | collective-permute-start | bytes 6291464 | tf_op jit(solution)/shard_map/ppermute | solution.py:831
  437.5 282.1 %all-reduce.6.cloned.1.call-start = ((), (), s32[]{:S(2)}) async-start(), calls=%async_computation | async-start | bytes 25427968 | tf_op jit(solution)/shard_map/psum | solution.py:924
  439.0 39.0 %collective-permute-start.19 = (bf16[256,512]{0,1:T(8,128)(2,1)S(1)}, bf16[256,512]{0,1:T(8,128)(2,1)S(1)}, u32[]{:S(2)}, u32[]{:S(2)}) collective-permute-start(bf16[256,512]{0,1:T(8,128)(2,1)S(1)} %bitcast.268), channel_id=1, source_target_pairs={{64,0},{65,1},{96,32},{97,33},{66,2},{67,3},{98,34},{99,35},{68,4}... | collective-permute-start | bytes 786440 | tf_op jit(solution)/shard_map/ppermute | solution.py:27
  440.4 26.0 %collective-permute-start.15 = (bf16[256,512]{0,1:T(8,128)(2,1)S(1)}, bf16[256,512]{0,1:T(8,128)(2,1)S(1)}, u32[]{:S(2)}, u32[]{:S(2)}) collective-permute-start(bf16[256,512]{0,1:T(8,128)(2,1)S(1)} %bitcast.272), channel_id=1, source_target_pairs={{64,0},{65,1},{96,32},{97,33},{66,2},{67,3},{98,34},{99,35},{68,4}... | collective-permute-start | bytes 786440 | tf_op jit(solution)/shard_map/ppermute | solution.py:27
  441.9 28.7 %collective-permute-start.12 = (bf16[256,512]{0,1:T(8,128)(2,1)S(1)}, bf16[256,512]{0,1:T(8,128)(2,1)S(1)}, u32[]{:S(2)}, u32[]{:S(2)}) collective-permute-start(bf16[256,512]{0,1:T(8,128)(2,1)S(1)} %bitcast.271), channel_id=1, source_target_pairs={{1,0},{32,1},{33,32},{64,33},{65,64},{96,65},{97,96},{3,2},{34,3},... | collective-permute-start | bytes 786440 | tf_op jit(solution)/shard_map/ppermute | solution.py:27
  444.3 32.1 %collective-permute-start.14 = (bf16[256,512]{0,1:T(8,128)(2,1)S(1)}, bf16[256,512]{0,1:T(8,128)(2,1)S(1)}, u32[]{:S(2)}, u32[]{:S(2)}) collective-permute-start(bf16[256,512]{0,1:T(8,128)(2,1)S(1)} %bitcast.270), channel_id=1, source_target_pairs={{33,0},{64,1},{65,32},{96,33},{97,64},{35,2},{66,3},{67,34},{98,35... | collective-permute-start | bytes 786440 | tf_op jit(solution)/shard_map/ppermute | solution.py:27
  445.6 32.1 %collective-permute-start.13 = (bf16[256,512]{0,1:T(8,128)(2,1)S(1)}, bf16[256,512]{0,1:T(8,128)(2,1)S(1)}, u32[]{:S(2)}, u32[]{:S(2)}) collective-permute-start(bf16[256,512]{0,1:T(8,128)(2,1)S(1)} %bitcast.269), channel_id=1, source_target_pairs={{32,0},{33,1},{64,32},{65,33},{96,64},{97,65},{34,2},{35,3},{66,34... | collective-permute-start | bytes 786440 | tf_op jit(solution)/shard_map/ppermute | solution.py:27
  466.4 15.5 %collective-permute-start.16 = (bf16[256,512]{0,1:T(8,128)(2,1)S(1)}, bf16[256,512]{0,1:T(8,128)(2,1)S(1)}, u32[]{:S(2)}, u32[]{:S(2)}) collective-permute-start(bf16[256,512]{0,1:T(8,128)(2,1)S(1)} %bitcast.267), channel_id=1, source_target_pairs={{1,0},{32,1},{33,32},{64,33},{65,64},{96,65},{97,96},{3,2},{34,3},... | collective-permute-start | bytes 786440 | tf_op jit(solution)/shard_map/ppermute | solution.py:27
  470.6 15.0 %collective-permute-start.18 = (bf16[256,512]{0,1:T(8,128)(2,1)S(1)}, bf16[256,512]{0,1:T(8,128)(2,1)S(1)}, u32[]{:S(2)}, u32[]{:S(2)}) collective-permute-start(bf16[256,512]{0,1:T(8,128)(2,1)S(1)} %bitcast.266), channel_id=1, source_target_pairs={{33,0},{64,1},{65,32},{96,33},{97,64},{35,2},{66,3},{67,34},{98,35... | collective-permute-start | bytes 786440 | tf_op jit(solution)/shard_map/ppermute | solution.py:27
  476.4 18.1 %collective-permute-start.17 = (bf16[256,512]{0,1:T(8,128)(2,1)S(1)}, bf16[256,512]{0,1:T(8,128)(2,1)S(1)}, u32[]{:S(2)}, u32[]{:S(2)}) collective-permute-start(bf16[256,512]{0,1:T(8,128)(2,1)S(1)} %bitcast.265), channel_id=1, source_target_pairs={{32,0},{33,1},{64,32},{65,33},{96,64},{97,65},{34,2},{35,3},{66,34... | collective-permute-start | bytes 786440 | tf_op jit(solution)/shard_map/ppermute | solution.py:27
  502.2 75.2 %copy-start.51 = (f32[256]{0:T(256)S(1)}, f32[256]{0:T(256)}, u32[]{:S(2)}) copy-start(f32[256]{0:T(256)} %get-tuple-element.56) | copy-start | bytes 3076
  (46 other events, 251.2 us)
Sparse Core Ops, SparseCore 0:
  437.7 104.7 all-reduce.7
  549.6 170.0 all-reduce.5

commit v2 on v1

--- a/solution.py
+++ b/solution.py
@@ -354,32 +354,515 @@
     )(own)
 
 
-def reduce_kernel(partial_ref, out_ref, partial, far, near, summed, far_two, near_two, send_sems, recv_sems, local_sem):
-    copy = pltpu.make_async_copy(partial_ref, partial, local_sem)
-    copy.start()
-    greet_plane()
-    copy.wait()
+class RowRing:
+    def __init__(self, summed, total, far, near, send_sems, recv_sems):
+        self.summed, self.total, self.far, self.near = summed, total, far, near
+        self.send_sems, self.recv_sems = send_sems, recv_sems
+        self.me = lax.axis_index("seq")
+        self.rows = summed.shape[0] // 4
+        self.started = []
+
+    def piece(self, ref, shift, half=None):
+        begin = mod4(self.me + shift) * self.rows
+        if half is None:
+            return ref.at[pl.ds(begin, self.rows)]
+        return ref.at[pl.ds(begin + half * (self.rows // 2), self.rows // 2)]
+
+    def send(self, source, target, step, slot):
+        copy = pltpu.make_async_remote_copy(
+            src_ref=source,
+            dst_ref=target,
+            send_sem=self.send_sems.at[slot],
+            recv_sem=self.recv_sems.at[slot],
+            device_id={"seq": mod4(self.me + step)},
+            device_id_type=MESH,
+        )
+        copy.start()
+        self.started.append(copy)
+
+    def wait(self, target, slot):
+        pltpu.make_async_remote_copy(
+            src_ref=target,
+            dst_ref=target,
+            send_sem=self.send_sems.at[slot],
+            recv_sem=self.recv_sems.at[slot],
+            device_id={"seq": self.me},
+            device_id_type=MESH,
+        ).wait_recv()
+
+    def add(self, target, source):
+        target[...] = (target[...].astype(F32) + source[...].astype(F32)).astype(BF)
+
+    def step_far(self):
+        self.send(self.piece(self.summed, 2, 0), self.far.at[0], 1, 0)
+        self.send(self.piece(self.summed, 2, 1), self.far.at[1], -1, 1)
+
+    def step_near(self):
+        self.wait(self.far.at[0], 0)
+        self.add(self.piece(self.summed, 1, 0), self.far.at[0])
+        self.send(self.piece(self.summed, 1), self.near.at[0], 1, 2)
+        self.wait(self.far.at[1], 1)
+        self.add(self.piece(self.summed, -1, 1), self.far.at[1])
+        self.send(self.piece(self.summed, -1), self.near.at[1], -1, 3)
+
+    def step_sum(self):
+        self.wait(self.near.at[0], 2)
+        self.wait(self.near.at[1], 3)
+        self.piece(self.total, 0)[...] = (
+            self.piece(self.summed, 0)[...].astype(F32)
+            + self.near[0].astype(F32)
+            + self.near[1].astype(F32)
+        ).astype(BF)
+        own = self.piece(self.total, 0)
+        self.send(own, own, 1, 4)
+        self.send(own, own, -1, 5)
+
+    def step_forward(self):
+        self.wait(self.piece(self.total, -1), 4)
+        half = self.piece(self.total, -1, 0)
+        self.send(half, half, 1, 6)
+        self.wait(self.piece(self.total, 1), 5)
+        half = self.piece(self.total, 1, 1)
+        self.send(half, half, -1, 7)
+
+    def finish(self):
+        self.wait(self.piece(self.total, 2, 0), 6)
+        self.wait(self.piece(self.total, 2, 1), 7)
+        for copy in self.started:
+            copy.wait_send()
+
+
+def return_kernel(
+    partial_ref,
+    grad_ref,
+    out_ref,
+    grad_total_ref,
+    partial,
+    far,
+    near,
+    summed,
+    far_two,
+    near_two,
+    grads,
+    grad_far,
+    grad_near,
+    send_sems,
+    recv_sems,
+    ring_send,
+    ring_recv,
+    local_sems,
+):
+    load_grads = pltpu.make_async_copy(grad_ref, grads, local_sems.at[0])
+    load = pltpu.make_async_copy(partial_ref, partial, local_sems.at[1])
+    load_grads.start()
+    load.start()
+    row, column = plane_coords(0)
+    line = lax.axis_index("seq")
+    barrier = pltpu.get_barrier_semaphore()
+    for index in (
+        mod4(row + 1) * 4 + column,
+        mod4(row - 1) * 4 + column,
+        row * 4 + mod4(column + 1),
+        row * 4 + mod4(column - 1),
+    ):
+        pl.semaphore_signal(barrier, inc=1, device_id={"grp": index}, device_id_type=MESH)
+    for step in (1, -1):
+        pl.semaphore_signal(
+            barrier, inc=1, device_id={"seq": mod4(line + step)}, device_id_type=MESH
+        )
+    pl.semaphore_wait(barrier, 6)
     buffers = (far, near, summed, far_two, near_two)
-    run_reduce([PlaneReduce(part, partial, buffers, send_sems, recv_sems, out_ref) for part in (0, 1)])
-
-
-def reduce_plane(partial):
+    reducers = [
+        PlaneReduce(part, partial, buffers, send_sems, recv_sems, out_ref) for part in (0, 1)
+    ]
+    ring = RowRing(grads, grad_total_ref, grad_far, grad_near, ring_send, ring_recv)
+    load_grads.wait()
+    ring.step_far()
+    load.wait()
+    for da in (2, 1, -1, 0):
+        for reducer in reducers:
+            reducer.step_far(da)
+    ring.step_near()
+    for da in (2, 1, -1, 0):
+        for reducer in reducers:
+            reducer.step_near(da)
+    ring.step_sum()
+    for da in (2, 1, -1, 0):
+        for reducer in reducers:
+            reducer.step_sum(da)
+    ring.step_forward()
+    for reducer in reducers:
+        reducer.finish()
+    ring.finish()
+
+
+def return_plane(partial, grads):
+    dma = pltpu.SemaphoreType.DMA
+    rows = grads.shape[0]
+    vmem = pl.BlockSpec(memory_space=pltpu.VMEM)
+    hbm = pl.BlockSpec(memory_space=pl.ANY)
     return pl.pallas_call(
-        reduce_kernel,
-        out_shape=jax.ShapeDtypeStruct((BLOCK, WIDTH), F32),
-        in_specs=[pl.BlockSpec(memory_space=pl.ANY)],
-        out_specs=pl.BlockSpec(memory_space=pltpu.VMEM),
+        return_kernel,
+        out_shape=(
+            jax.ShapeDtypeStruct((BLOCK, WIDTH), F32),
+            jax.ShapeDtypeStruct(grads.shape, BF),
+        ),
+        in_specs=[hbm, hbm],
+        out_specs=(vmem, vmem),
         scratch_shapes=[pltpu.VMEM((PLANE, BLOCK, WIDTH), BF)]
         + reduce_buffers()
         + [
-            pltpu.SemaphoreType.DMA((40,)),
-            pltpu.SemaphoreType.DMA((40,)),
-            pltpu.SemaphoreType.DMA,
+            pltpu.VMEM(grads.shape, BF),
+            pltpu.VMEM((2, rows // 8, WIDTH), BF),
+            pltpu.VMEM((2, rows // 4, WIDTH), BF),
+            dma((40,)),
+            dma((40,)),
+            dma((8,)),
+            dma((8,)),
+            dma((2,)),
         ],
         compiler_params=pltpu.CompilerParams(
             collective_id=1, has_side_effects=True, vmem_limit_bytes=58 << 20
         ),
-    )(partial)
+    )(partial, grads)
+
+
+class CubeSum:
+    def __init__(self, part, matrix, out, far, near, mid, low, send_sems, recv_sems):
+        self.part, self.matrix, self.out = part, matrix, out
+        self.far, self.near, self.mid, self.low = far, near, mid, low
+        self.send_sems, self.recv_sems = send_sems, recv_sems
+        line, plane = lax.axis_index("seq"), lax.axis_index("grp")
+        coords = (line, plane // 4, lax.rem(plane, 4))
+        self.coords = coords
+        self.place = [coords[(part + level) % 3] for level in range(3)]
+        self.started = []
+
+    def device(self, level, step):
+        axis = (self.part + level) % 3
+        there = mod4(self.coords[axis] + step)
+        if axis == 0:
+            return {"seq": there}
+        if axis == 1:
+            return {"grp": there * 4 + self.coords[2]}
+        return {"grp": self.coords[1] * 4 + there}
+
+    def rows(self, level, shift):
+        begin = 0
+        for upper in range(level):
+            begin = begin + self.place[upper] * (256 // 4**upper)
+        return begin + mod4(self.place[level] + shift) * (256 // 4**level)
+
+    def copy(self, source, target, level, step, slot):
+        return pltpu.make_async_remote_copy(
+            src_ref=source,
+            dst_ref=target,
+            send_sem=self.send_sems.at[self.part, slot],
+            recv_sem=self.recv_sems.at[self.part, slot],
+            device_id=self.device(level, step),
+            device_id_type=MESH,
+        )
+
+    def send(self, source, target, level, step, slot):
+        copy = self.copy(source, target, level, step, slot)
+        copy.start()
+        self.started.append(copy)
+
+    def wait(self, target, slot):
+        self.copy(target, target, 0, 0, slot).wait_recv()
+
+    def add(self, target, *sources):
+        value = target[...].astype(F32)
+        for source in sources:
+            value = value + source[...].astype(F32)
+        target[...] = value.astype(BF)
+
+    def step_far(self):
+        begin = self.rows(0, 2)
+        self.send(self.matrix.at[pl.ds(begin, 128)], self.far.at[0], 0, 1, 0)
+        self.send(self.matrix.at[pl.ds(begin + 128, 128)], self.far.at[1], 0, -1, 1)
+
+    def step_near(self):
+        begin = self.rows(0, 1)
+        self.wait(self.far.at[0], 0)
+        self.add(self.matrix.at[pl.ds(begin, 128)], self.far.at[0])
+        self.send(self.matrix.at[pl.ds(begin, 256)], self.near.at[0], 0, 1, 2)
+        begin = self.rows(0, -1)
+        self.wait(self.far.at[1], 1)
+        self.add(self.matrix.at[pl.ds(begin + 128, 128)], self.far.at[1])
+        self.send(self.matrix.at[pl.ds(begin, 256)], self.near.at[1], 0, -1, 3)
+
+    def step_mid(self):
+        self.wait(self.near.at[0], 2)
+        self.wait(self.near.at[1], 3)
+        self.add(self.matrix.at[pl.ds(self.rows(0, 0), 256)], self.near.at[0], self.near.at[1])
+        for step in (1, 2, 3):
+            self.send(
+                self.matrix.at[pl.ds(self.rows(1, step), 64)], self.mid.at[step - 1], 1, step, 3 + step
+            )
+
+    def step_low(self):
+        for step in (1, 2, 3):
+            self.wait(self.mid.at[step - 1], 3 + step)
+        self.add(
+            self.matrix.at[pl.ds(self.rows(1, 0), 64)], self.mid.at[0], self.mid.at[1], self.mid.at[2]
+        )
+        for step in (1, 2, 3):
+            self.send(
+                self.matrix.at[pl.ds(self.rows(2, step), 16)], self.low.at[step - 1], 2, step, 6 + step
+            )
+
+    def step_done(self):
+        for step in (1, 2, 3):
+            self.wait(self.low.at[step - 1], 6 + step)
+        own = self.rows(2, 0)
+        value = self.matrix[pl.ds(own, 16), :].astype(F32)
+        for step in (1, 2, 3):
+            value = value + self.low[step - 1].astype(F32)
+        self.out[pl.ds(own, 16), :] = value.astype(BF)
+        ref = self.out.at[pl.ds(own, 16)]
+        for step in (1, 2, 3):
+            self.send(ref, ref, 2, step, 9 + step)
+
+    def back_mid(self):
+        for step in (1, 2, 3):
+            self.wait(self.out.at[pl.ds(self.rows(2, -step), 16)], 9 + step)
+        ref = self.out.at[pl.ds(self.rows(1, 0), 64)]
+        for step in (1, 2, 3):
+            self.send(ref, ref, 1, step, 12 + step)
+
+    def back_near(self):
+        for step in (1, 2, 3):
+            self.wait(self.out.at[pl.ds(self.rows(1, -step), 64)], 12 + step)
+        ref = self.out.at[pl.ds(self.rows(0, 0), 256)]
+        self.send(ref, ref, 0, 1, 16)
+        self.send(ref, ref, 0, -1, 17)
+        self.share(0, 20)
+
+    def back_far(self):
+        begin = self.rows(0, -1)
+        self.wait(self.out.at[pl.ds(begin, 256)], 16)
+        ref = self.out.at[pl.ds(begin, 128)]
+        self.send(ref, ref, 0, 1, 18)
+        self.share(-1, 21)
+        begin = self.rows(0, 1)
+        self.wait(self.out.at[pl.ds(begin, 256)], 17)
+        ref = self.out.at[pl.ds(begin + 128, 128)]
+        self.send(ref, ref, 0, -1, 19)
+        self.share(1, 22)
+
+    def back_last(self):
+        begin = self.rows(0, 2)
+        self.wait(self.out.at[pl.ds(begin, 128)], 18)
+        self.wait(self.out.at[pl.ds(begin + 128, 128)], 19)
+        self.share(2, 23)
+
+    def share_copy(self, shift, slot):
+        ref = self.out.at[pl.ds(self.rows(0, shift), 256)]
+        return pltpu.make_async_remote_copy(
+            src_ref=ref,
+            dst_ref=ref,
+            send_sem=self.send_sems.at[self.part, slot],
+            recv_sem=self.recv_sems.at[self.part, slot],
+            device_id={"exp": 1 - lax.axis_index("exp")},
+            device_id_type=MESH,
+        )
+
+    def share(self, shift, slot):
+        copy = self.share_copy(shift, slot)
+        copy.start()
+        self.started.append(copy)
+
+    def finish(self, other_out):
+        for shift, slot in ((0, 20), (-1, 21), (1, 22), (2, 23)):
+            ref = other_out.at[pl.ds(self.rows(0, shift), 256)]
+            pltpu.make_async_remote_copy(
+                src_ref=ref,
+                dst_ref=ref,
+                send_sem=self.send_sems.at[self.part, slot],
+                recv_sem=self.recv_sems.at[self.part, slot],
+                device_id={"exp": 1 - lax.axis_index("exp")},
+                device_id_type=MESH,
+            ).wait_recv()
+        for copy in self.started:
+            copy.wait_send()
+
+
+SMALL_ROWS = 40
+
+
+def total_kernel(
+    mats_ref,
+    small_ref,
+    out_ref,
+    small_out_ref,
+    matrix,
+    far,
+    near,
+    mid,
+    low,
+    arrived,
+    small,
+    small_first,
+    send_sems,
+    recv_sems,
+    core_send,
+    core_recv,
+    small_send,
+    small_recv,
+):
+    line, plane, core = lax.axis_index("seq"), lax.axis_index("grp"), lax.axis_index("exp")
+    row, column = plane // 4, lax.rem(plane, 4)
+    other = 1 - core
+    places = (line, row, column)
+
+    def neighbour(axis, step):
+        if axis == 0:
+            return {"seq": mod4(line + step)}
+        if axis == 1:
+            return {"grp": mod4(row + step) * 4 + column}
+        return {"grp": row * 4 + mod4(column + step)}
+
+    barrier = pltpu.get_barrier_semaphore()
+    for axis in range(3):
+        for step in (1, 2, 3):
+            pl.semaphore_signal(
+                barrier, inc=1, device_id=neighbour(axis, step), device_id_type=MESH
+            )
+    pl.semaphore_signal(barrier, inc=1, device_id={"exp": other}, device_id_type=MESH)
+    pl.semaphore_wait(barrier, 10)
+
+    def to_core(source, target, slot):
+        return pltpu.make_async_remote_copy(
+            src_ref=source,
+            dst_ref=target,
+            send_sem=core_send.at[slot],
+            recv_sem=core_recv.at[slot],
+            device_id={"exp": other},
+            device_id_type=MESH,
+        )
+
+    own_small = pl.ds(core * SMALL_ROWS, SMALL_ROWS)
+    core_copies = [to_core(mats_ref.at[other * 3 + part], arrived.at[part], part) for part in range(3)]
+    core_copies.append(
+        to_core(small_ref.at[pl.ds(other * SMALL_ROWS, SMALL_ROWS)], small_first, 3)
+    )
+    for copy in core_copies:
+        copy.start()
+    sums = [
+        CubeSum(
+            part,
+            matrix.at[part],
+            out_ref.at[core * 3 + part],
+            far.at[part],
+            near.at[part],
+            mid.at[part],
+            low.at[part],
+            send_sems,
+            recv_sems,
+        )
+        for part in range(3)
+    ]
+    for part in range(3):
+        core_copies[part].wait()
+        matrix[part] = (
+            mats_ref[core * 3 + part].astype(F32) + arrived[part].astype(F32)
+        ).astype(BF)
+        sums[part].step_far()
+    small_copies = []
+
+    def small_step(axis):
+        for step in (1, 2, 3):
+            copy = pltpu.make_async_remote_copy(
+                src_ref=small.at[axis, places[axis]],
+                dst_ref=small.at[axis, places[axis]],
+                send_sem=small_send.at[axis, step],
+                recv_sem=small_recv.at[axis, step],
+                device_id=neighbour(axis, step),
+                device_id_type=MESH,
+            )
+            copy.start()
+            small_copies.append(copy)
+
+    def small_sum(axis):
+        for step in (1, 2, 3):
+            ref = small.at[axis, mod4(places[axis] - step)]
+            pltpu.make_async_remote_copy(
+                src_ref=ref,
+                dst_ref=ref,
+                send_sem=small_send.at[axis, step],
+                recv_sem=small_recv.at[axis, step],
+                device_id=neighbour(axis, step),
+                device_id_type=MESH,
+            ).wait_recv()
+        return (small[axis, 0] + small[axis, 1]) + (small[axis, 2] + small[axis, 3])
+
+    core_copies[3].wait()
+    small[0, line] = small_ref[own_small, :] + small_first[...]
+    small_step(0)
+    for cube in sums:
+        cube.step_near()
+    small[1, row] = small_sum(0)
+    small_step(1)
+    for cube in sums:
+        cube.step_mid()
+    small[2, column] = small_sum(1)
+    small_step(2)
+    for cube in sums:
+        cube.step_low()
+    small_out_ref[own_small, :] = small_sum(2)
+    small_last = to_core(small_out_ref.at[own_small], small_out_ref.at[own_small], 4)
+    small_last.start()
+    for cube in sums:
+        cube.step_done()
+    for cube in sums:
+        cube.back_mid()
+    for cube in sums:
+        cube.back_near()
+    for cube in sums:
+        cube.back_far()
+    for cube in sums:
+        cube.back_last()
+    for part in range(3):
+        sums[part].finish(out_ref.at[other * 3 + part])
+    small_last.wait_send()
+    theirs = small_out_ref.at[pl.ds(other * SMALL_ROWS, SMALL_ROWS)]
+    to_core(theirs, theirs, 4).wait_recv()
+    for copy in small_copies:
+        copy.wait_send()
+
+
+def total_all(mats, small):
+    dma = pltpu.SemaphoreType.DMA
+    vmem = pl.BlockSpec(memory_space=pltpu.VMEM)
+    return pl.pallas_call(
+        total_kernel,
+        out_shape=(
+            jax.ShapeDtypeStruct((6, 1024, 512), BF),
+            jax.ShapeDtypeStruct((2 * SMALL_ROWS, 512), F32),
+        ),
+        in_specs=[vmem, vmem],
+        out_specs=(vmem, vmem),
+        scratch_shapes=[
+            pltpu.VMEM((3, 1024, 512), BF),
+            pltpu.VMEM((3, 2, 128, 512), BF),
+            pltpu.VMEM((3, 2, 256, 512), BF),
+            pltpu.VMEM((3, 3, 64, 512), BF),
+            pltpu.VMEM((3, 3, 16, 512), BF),
+            pltpu.VMEM((3, 1024, 512), BF),
+            pltpu.VMEM((3, 4, SMALL_ROWS, 512), F32),
+            pltpu.VMEM((SMALL_ROWS, 512), F32),
+            dma((3, 24)),
+            dma((3, 24)),
+            dma((5,)),
+            dma((5,)),
+            dma((3, 4)),
+            dma((3, 4)),
+        ],
+        compiler_params=pltpu.CompilerParams(
+            collective_id=3, has_side_effects=True, vmem_limit_bytes=40 << 20
+        ),
+    )(mats, small)
 
 
 def dot_tn(left, right):
@@ -403,8 +886,7 @@
     row_total_ref,
     score_out_ref,
     moe_ref,
-    d_in_ref,
-    d_out_ref,
+    grad_ref,
     blocks,
     meta_in,
     score_send,
@@ -439,6 +921,9 @@
     local_sems,
     cot_sems,
     moe_sems,
+    pair_send,
+    pair_recv,
+    pair_ready,
 ):
     me = lax.axis_index("grp")
     core = lax.axis_index("exp")
@@ -627,13 +1112,41 @@
         )
         copy.start()
         score_copies.append(copy)
-    store_in = pltpu.make_async_copy(d_in, d_in_ref, local_sems.at[0])
-    store_out = pltpu.make_async_copy(d_out, d_out_ref, local_sems.at[1])
-    store_in.start()
-    store_out.start()
+    other = 1 - core
+    for j in range(4):
+        cots[0, j] = d_in[other, pl.ds(j * BLOCK, BLOCK), :].astype(BF)
+    for j in range(2):
+        cots[1, j] = d_out[other, pl.ds(j * BLOCK, BLOCK), :].astype(BF)
+    pl.semaphore_signal(pair_ready, inc=1, device_id={"exp": other}, device_id_type=MESH)
+    pl.semaphore_wait(pair_ready, 1)
+    pair_copies = []
+    for j in range(6):
+        copy = pltpu.make_async_remote_copy(
+            src_ref=cots.at[j // 4, j % 4],
+            dst_ref=blocks.at[j],
+            send_sem=pair_send.at[j],
+            recv_sem=pair_recv.at[j],
+            device_id={"exp": other},
+            device_id_type=MESH,
+        )
+        copy.start()
+        pair_copies.append(copy)
     for da in (2, 1, -1, 0):
         for reducer in reducers:
             reducer.step_near(da)
+    for j in range(6):
+        pair_copies[j].wait()
+        here = pl.ds((j % 4) * BLOCK, BLOCK)
+        if j < 4:
+            w_in[0, here, :] = (d_in[core, here, :] + blocks[j].astype(F32)).astype(BF)
+        else:
+            w_out[0, here, :] = (d_out[core, here, :] + blocks[j].astype(F32)).astype(BF)
+    store_in = pltpu.make_async_copy(w_in.at[0], grad_ref.at[pl.ds(0, WIDTH)], local_sems.at[0])
+    store_out = pltpu.make_async_copy(
+        w_out.at[0], grad_ref.at[pl.ds(WIDTH, INNER)], local_sems.at[1]
+    )
+    store_in.start()
+    store_out.start()
     for da in (2, 1, -1, 0):
         for reducer in reducers:
             reducer.step_sum(da)
@@ -658,11 +1171,10 @@
             jax.ShapeDtypeStruct((BLOCK, WIDTH), F32),
             jax.ShapeDtypeStruct((PLANE, 8, BLOCK), F32),
             jax.ShapeDtypeStruct((PLANE, BLOCK, WIDTH), BF),
-            jax.ShapeDtypeStruct((2, WIDTH, 2 * INNER), F32),
-            jax.ShapeDtypeStruct((2, INNER, WIDTH), F32),
+            jax.ShapeDtypeStruct((WIDTH + INNER, WIDTH), BF),
         ),
         in_specs=[vmem, vmem, hbm, hbm, hbm],
-        out_specs=(vmem, vmem, hbm, hbm, hbm),
+        out_specs=(vmem, vmem, hbm, hbm),
         scratch_shapes=[
             pltpu.VMEM((PLANE, BLOCK, WIDTH), BF),
             pltpu.VMEM((PLANE, 8, BLOCK), F32),
@@ -685,7 +1197,9 @@
         + [dma((40,))] * 4
         + [dma((PLANE,))] * 4
         + [dma((2,))] * 3
-        + [dma((2, GROUP)), dma((GROUP,))],
+        + [dma((2, GROUP)), dma((GROUP,))]
+        + [dma((6,))] * 2
+        + [pltpu.SemaphoreType.REGULAR],
         compiler_params=pltpu.CompilerParams(
             collective_id=2, has_side_effects=True, vmem_limit_bytes=VMEM_LIMIT
         ),
@@ -817,20 +1331,12 @@
         axis=1,
     )
     cots = gather_plane(cotangent[0])
-    expert_row_sum, scores, moe_partial, d_in, d_out = run_experts(
+    expert_row_sum, scores, moe_partial, expert_grads = run_experts(
         routed_in, meta, cots, expert_in[0], expert_out[0]
     )
-    moe_out = reduce_plane(moe_partial)
+    moe_out, expert_total = return_plane(moe_partial, expert_grads)
     output = (residual + RESIDUAL_MULT * moe_out).astype(jnp.bfloat16)[None]
     upstream = cotangent[0].astype(jnp.float32)
-    core = lax.axis_index("exp")
-
-    def pair_sum(value):
-        other = lax.dynamic_index_in_dim(value, 1 - core, 0, keepdims=True).astype(jnp.bfloat16)
-        own = lax.dynamic_index_in_dim(value, core, 0, keepdims=True)
-        return own + lax.ppermute(other, "exp", [(0, 1), (1, 0)]).astype(jnp.float32)
-
-    up_w_grad, down_w_grad = pair_sum(d_in), pair_sum(d_out)
     gate_grad = scores[:, :2, :].reshape(experts, tok_rows).T
     choice_grad = gates * (gate_grad - jnp.sum(gates * gate_grad, axis=1, keepdims=True))
     logit_grad = choice_grad.astype(jnp.bfloat16)
@@ -845,7 +1351,6 @@
         - residual * scale_two**3 * jnp.mean(weighted_two * residual, axis=-1, keepdims=True)
     )
     branch_grad = (RESIDUAL_MULT * residual_grad).astype(jnp.bfloat16)
-    out_w_grad = inner_rows(heads_out, branch_grad)
     head_gradient = (
         product_back(branch_grad, w_output)
         .astype(jnp.bfloat16)
@@ -901,9 +1406,6 @@
         .reshape(tok_rows, kv_width)
     )
     value_pre_grad = values_grad.astype(jnp.bfloat16)
-    query_w_grad = inner_rows(normed, query_pre_grad)
-    key_w_grad = inner_rows(normed, key_pre_grad)
-    value_w_grad = inner_rows(normed, value_pre_grad)
     normed_grad = (
         product_back(query_pre_grad, w_query)
         + product_back(key_pre_grad, w_key)
@@ -916,24 +1418,36 @@
         + scale_one * weighted_one
         - inputs * scale_one**3 * jnp.mean(weighted_one * inputs, axis=-1, keepdims=True)
     )
-    up_total, down_total = (
-        lax.psum(up_w_grad.astype(jnp.bfloat16), "seq").astype(jnp.float32),
-        lax.psum(down_w_grad.astype(jnp.bfloat16), "seq").astype(jnp.float32),
-    )
-    gain_one_total, query_total, key_total, value_total, out_total, gain_two_total, router_total = (
-        lax.psum(
-            (
-                attn_gain_grad,
-                query_w_grad,
-                key_w_grad,
-                value_w_grad,
-                out_w_grad,
-                ffn_gain_grad,
-                router_w_grad,
-            ),
-            ("seq", "grp", "exp"),
-        )
-    )
+    up_total = expert_total[None, :model_width].astype(jnp.float32)
+    down_total = expert_total[None, model_width:].astype(jnp.float32)
+    half = model_width // 2
+    mats = jnp.stack(
+        [
+            inner_rows(normed, query_pre_grad[:, :half]),
+            inner_rows(normed, query_pre_grad[:, half:]),
+            inner_rows(normed, key_pre_grad),
+            inner_rows(normed, value_pre_grad),
+            inner_rows(heads_out, branch_grad[:, :half]),
+            inner_rows(heads_out, branch_grad[:, half:]),
+        ]
+    ).astype(jnp.bfloat16)
+    small = jnp.concatenate(
+        [
+            router_w_grad.reshape(64, 512),
+            attn_gain_grad.reshape(2, 512),
+            ffn_gain_grad.reshape(2, 512),
+            jnp.zeros((2 * SMALL_ROWS - 68, 512), jnp.float32),
+        ],
+        axis=0,
+    )
+    mats_total, small_total = total_all(mats, small)
+    query_total = jnp.concatenate([mats_total[0], mats_total[1]], axis=1).astype(jnp.float32)
+    key_total = mats_total[2].astype(jnp.float32)
+    value_total = mats_total[3].astype(jnp.float32)
+    out_total = jnp.concatenate([mats_total[4], mats_total[5]], axis=1).astype(jnp.float32)
+    router_total = small_total[:64].reshape(router_w_grad.shape)
+    gain_one_total = small_total[64:66].reshape(model_width)
+    gain_two_total = small_total[66:68].reshape(model_width)
     return (
         output,
         input_grad.astype(jnp.bfloat16)[None],

time: 749 us -> 559 us (0.75)
  waiting for transfers between devices: 177 us -> 24.8 us
  Pallas kernels: 237 us -> 316 us
  blocking collectives: 74.4 us -> 0 us
  local copies, waits for them, and re-layouts: 49.4 us -> 34.1 us
  between operations: 15.5 us -> 2.14 us
    psum x2 -> x0, waiting for transfers between devices: 135 us -> none  [the longest x1 135 us: on_device(): lax.psum((attn_gain_grad, query_w_grad, key_w_grad, value_w_grad, out_w_g...]
    pallas_call x1 -> x2, Pallas kernels: 48.1 us -> 123 us  [the longest x1 67.1 us: total_all(): pl.pallas_call(total_kernel, out_shape=(jax.ShapeDtypeStruct((6, 1024, 51...]
    psum x1 -> x0, blocking collectives: 74.4 us -> none  [on_device(): lax.psum((attn_gain_grad, query_w_grad, key_w_grad, value_w_grad, out_w_g...]
    ppermute x20, waiting for transfers between devices: 41.8 us -> 24.8 us  [from_behind(): lax.ppermute(value, axis, [(source, source + steps) for source in range(i...]
    unnamed x127 -> x106, local copies, waits for them, and re-layouts: 31.8 us -> 20.9 us
  transfers between devices with their start and end apart: 24 -> 20, of which waited for: 8 -> 11; matrix products, arithmetic and copies ran while one was open for 15% -> 4% of each run, Pallas kernels for 7% -> 10%
where the time goes in v2:
time: 559 us; the launch traced here: 551 us
  Pallas kernels  316 us (57%)
  matrix products  80 us (14%)
  starting transfers between devices  52.2 us (9%)
  other arithmetic  42 us (8%)
  local copies, waits for them, and re-layouts  34.1 us (6%)
  waiting for transfers between devices  24.8 us (4%)
    pallas_call x1, Pallas kernels, run_experts(): pl.pallas_call(expert_kernel, out_shape=(jax.ShapeDtypeStruct((BLOCK, WID...  140 us
    pallas_call x1, Pallas kernels, total_all(): pl.pallas_call(total_kernel, out_shape=(jax.ShapeDtypeStruct((6, 1024, 51...  67.1 us
    pallas_call x1, Pallas kernels, return_plane(): pl.pallas_call(return_kernel, out_shape=(jax.ShapeDtypeStruct((BLOCK, WID...  55.5 us
    pallas_call x1, Pallas kernels, gather_plane(): pl.pallas_call(gather_kernel, out_shape=jax.ShapeDtypeStruct((PLANE, BLOC...  53.4 us
    ppermute x20, starting transfers between devices, from_behind(): lax.ppermute(value, axis, [(source, source + steps) for source in range(i...  52.2 us
    ppermute x20, waiting for transfers between devices, from_behind(): lax.ppermute(value, axis, [(source, source + steps) for source in range(i...  24.8 us
    unnamed x106, local copies, waits for them, and re-layouts  20.9 us
    convert_element_type x1, other arithmetic, on_device(): score_gradient = (probs_full * (prob_grad - jnp.sum(probs_full * prob_gra...  14.4 us
  transfers between devices with their start and end apart: 20, of which 11 were waited for; matrix products, arithmetic and copies ran while one was open for 4% of the time, Pallas kernels for 10%

profile of v2, /device:TPU:1, one launch (start us, length us, event | category | flops | bytes accessed | tf_op | source)
XLA Modules:
  0.0 550.9 jit_solution(7105373129816622036)
XLA Ops:
  2.6 2.4 copy.52
  7.8 6.2 %collective-permute-start.8 = (bf16[256,512]{0,1:T(8,128)(2,1)}, bf16[256,512]{0,1:T(8,128)(2,1)}, u32[]{:S(2)}, u32[]{:S(2)}) collective-permute-start(bf16[256,512]{0,1:T(8,128)(2,1)} %bitcast.9), channel_id=1, source_target_pairs={{0,64},{1,65},{32,96},{33,97},{2,66},{3,67},{34,98},{35,99},{4,68}... | collective-permute-start | bytes 786440 | tf_op jit(solution)/shard_map/ppermute | solution.py:27
  16.0 2.9 collective-permute-start.10
  22.3 2.6 copy.53
  24.9 2.5 fusion.66
  29.6 53.4 %shard_map.221.cot_ref = bf16[16,256,1024]{2,1,0:T(8,128)(2,1)} custom-call(bf16[256,1024]{1,0:T(8,128)(2,1)} %bitcast.291), custom_call_target="tpu_custom_call" | custom-call | tf_op jit(solution)/shard_map/pallas_call | solution.py:340
  86.0 5.5 collective-permute-start.6
  92.2 2.6 collective-permute-start.7
  95.6 4.3 collective-permute-start
  101.1 3.4 collective-permute-start.1
  107.9 2.3 collective-permute-start.3
  113.8 2.9 collective-permute-done.2
  117.4 3.1 collective-permute-done.3
  122.8 2.4 copy.51
  125.2 11.5 %exponential_reduce_fusion = (f32[8,2,256]{2,1,0:T(2,128)S(1)}, f32[8,2,256,1280]{2,3,1,0:T(8,128)}) fusion(pred[256,1280]{0,1:T(8,128)(4,1)S(1)} %fusion.41, bf16[1280,8,64]{0,2,1:T(8,128)(2,1)S(1)} %constant_dynamic-update-slice_fusion.6, bf16[256,8,2,32]{0,3,2,1:T(8,128)(2,1)S(1)} %bitcast.304, bf16[256,8,2,32]{0,3,2,1:T(8,128)(2,1)S(1)} %bitcast.300), kind=kOutput, calls=%fused_computation.9 | convolution fusion | flops 693110016 | bytes 23150592 | tf_op jit(solution)/shard_map/sub | solution.py:1305
  136.8 11.3 %fusion.42 = bf16[8,64,2,256]{3,1,2,0:T(8,128)(2,1)S(1)} fusion(bf16[1280,8,64,1]{0,2,3,1:T(8,128)(2,1)} %bitcast.298, f32[8,2,256]{2,1,0:T(2,128)S(1)} %get-tuple-element.99, pred[256,1280]{0,1:T(8,128)(4,1)} %copy-done.29, bf16[1280,8,64]{0,2,1:T(8,128)(2,1)S(1)} %constant_dynamic-update-slice_fusion.6, bf16[256,8,2,32]{0,3,2,1:T(8,128)(2,1)S(1)} %bitcast.305, ...), kind=kOutput, calls=%fused_computation.61 | convolution fusion | flops 1369707776 | bytes 4014080 | tf_op jit(solution)/shard_map/uzjq,quk->juzk/dot_general | solution.py:1307
  148.1 2.6 multiply_reduce_fusion.2
  154.4 139.7 %shard_map.222 = (f32[256,1024]{1,0:T(8,128)}, f32[16,8,256]{2,1,0:T(8,128)}, bf16[16,256,1024]{2,1,0:T(8,128)(2,1)}, bf16[1536,1024]{1,0:T(8,128)(2,1)}) custom-call(bf16[256,1024]{1,0:T(8,128)(2,1)} %copy-done.8, f32[16,8,256]{2,1,0:T(8,128)} %maximum_maximum_fusion.1.meta_ref, bf16[16,256,1024]{2,1,0:T(8,128)(2,1)} %shard_map.221.cot_ref, ...), custom_call_target="tpu_custom_call" | custom-call | tf_op jit(solution)/shard_map/pallas_call | solution.py:1168
  298.5 55.5 %shard_map.223 = (f32[256,1024]{1,0:T(8,128)}, bf16[1536,1024]{1,0:T(8,128)(2,1)}) custom-call(bf16[16,256,1024]{2,1,0:T(8,128)(2,1)} %get-tuple-element.19.partial_ref, bf16[1536,1024]{1,0:T(8,128)(2,1)} %get-tuple-element.20.grad_ref), custom_call_target="tpu_custom_call" | custom-call | tf_op jit(solution)/shard_map/pallas_call | solution.py:504
  354.1 2.9 multiply_convert_fusion
  360.7 13.4 %fusion.112 = (bf16[1280,8,64]{0,2,1:T(8,128)(2,1)}, f32[1280,8,64]{0,2,1:T(8,128)}) fusion(bf16[256,8,2,64]{0,3,2,1:T(8,128)(2,1)S(1)} %bitcast.316, f32[8,2,256]{2,1,0:T(2,128)S(1)} %get-tuple-element.99, pred[256,1280]{0,1:T(8,128)(4,1)} %copy-done.29, bf16[1280,8,64]{0,2,1:T(8,128)(2,1)} %copy-done.14, bf16[256,8,2,32]{0,3,2,1:T(8,128)(2,1)S(1)} %bitcast.306, ...), kind=kOutput, calls=%fused_computation.190 | convolution fusion | flops 1370100992 | bytes 6635520 | tf_op jit(solution)/shard_map/ykze,zykm->eym/dot_general | solution.py:1377
  374.0 13.3 %fusion.2 = (f32[8,2,256]{2,1,0:T(2,128)S(1)}, f32[8,1280,256,2]{2,1,3,0:T(8,128)}) fusion(f32[8,2,256]{2,1,0:T(2,128)S(1)} %get-tuple-element.99, f32[8,2,256,1280]{2,3,1,0:T(8,128)} %get-tuple-element.100, bf16[1280,8,64,1]{0,2,3,1:T(8,128)(2,1)S(1)} %bitcast.299, bf16[256,8,2,64]{0,3,2,1:T(8,128)(2,1)S(1)} %bitcast.317), kind=kOutput, calls=%fused_computation.4 | convolution fusion | flops 686813184 | bytes 43810816 | tf_op jit(solution)/shard_map/dklp,okp->kldo/dot_general | solution.py:1362
  387.3 14.4 %fusion.4 = bf16[8,2,256,1280]{2,3,1,0:T(8,128)(2,1)S(1)} fusion(f32[8,1280,256,2]{2,1,3,0:T(8,128)} %get-tuple-element.107, f32[8,2,256]{2,1,0:T(2,128)S(1)} %get-tuple-element.106, f32[8,2,256]{2,1,0:T(2,128)S(1)} %get-tuple-element.99, f32[8,2,256,1280]{2,3,1,0:T(8,128)} %get-tuple-element.100), kind=kLoop, calls=%fused_computation.6 | loop fusion | flops 20971520 | bytes 52461568 | tf_op jit(solution)/shard_map/convert_element_type | solution.py:1367
  401.8 3.3 fusion.111
  411.1 2.5 bitcast_convert_fusion
  416.2 6.5 %collective-permute-start.16 = (bf16[256,512]{0,1:T(8,128)(2,1)}, bf16[256,512]{0,1:T(8,128)(2,1)}, u32[]{:S(2)}, u32[]{:S(2)}) collective-permute-start(bf16[256,512]{0,1:T(8,128)(2,1)} %bitcast.59), channel_id=1, source_target_pairs={{1,0},{32,1},{33,32},{64,33},{65,64},{96,65},{97,96},{3,2},{34,3},... | collective-permute-start | bytes 786440 | tf_op jit(solution)/shard_map/ppermute | solution.py:27
  435.6 2.5 collective-permute-done.13
  448.7 8.5 %collective-permute-done.19 = bf16[256,512]{0,1:T(8,128)(2,1)S(1)} collective-permute-done((bf16[256,512]{0,1:T(8,128)(2,1)}, bf16[256,512]{0,1:T(8,128)(2,1)S(1)}, u32[]{:S(2)}, u32[]{:S(2)}) %collective-permute-start.19) | collective-permute-done | bytes 262176 | tf_op jit(solution)/shard_map/ppermute | solution.py:27
  466.1 2.8 copy-done.2
  468.9 67.1 %shard_map.224 = (bf16[6,1024,512]{2,1,0:T(8,128)(2,1)S(1)}, f32[80,512]{1,0:T(8,128)S(1)}) custom-call(bf16[6,1024,512]{2,1,0:T(8,128)(2,1)S(1)} %copy-done.2, f32[80,512]{1,0:T(8,128)S(1)} %maximum_maximum_fusion.small_ref), custom_call_target="tpu_custom_call" | custom-call | tf_op jit(solution)/shard_map/pallas_call | solution.py:838
  536.1 3.0 slice_bitcast_fusion.1
  543.1 6.2 %maximum_convert_fusion = (f32[1024,1024]{1,0:T(8,128)}, f32[1024,1024]{1,0:T(8,128)}) fusion(bf16[1024,512]{1,0:T(8,128)(2,1)} %get-tuple-element.72, bf16[1024,512]{1,0:T(8,128)(2,1)} %get-tuple-element.73, bf16[1024,512]{1,0:T(8,128)(2,1)S(1)} %get-tuple-element.69, bf16[1024,512]{1,0:T(8,128)(2,1)S(1)} %get-tuple-element.68), kind=kLoop, calls=%fused_computation.18 | loop fusion | flops 8388608 | bytes 12582912 | tf_op jit(solution)/shard_map/convert_element_type | solution.py:1444
  (212 shorter events, 85.4 us)
Async XLA Ops:
  0.6 152.1 %copy-start = (bf16[1024,32]{0,1:T(8,128)(2,1)S(1)}, bf16[1024,32]{0,1:T(8,128)(2,1)}, u32[]{:S(2)}) copy-start(bf16[1024,32]{0,1:T(8,128)(2,1)} %param.24) | copy-start | bytes 196612
  2.6 25.0 %copy-start.36 = (f32[256]{0:T(256)}, f32[256]{0:T(256)S(1)}, u32[]{:S(2)}) copy-start(f32[256]{0:T(256)S(1)} %get-tuple-element.96) | copy-start | bytes 3076
  2.6 18.4 %copy-start.42 = (s32[1,256]{1,0:T(1,128)S(1)}, s32[1,256]{1,0:T(1,128)}, u32[]{:S(2)}) copy-start(s32[1,256]{1,0:T(1,128)} %param.15) | copy-start | bytes 3076
  2.6 19.7 %copy-start.6 = (bf16[1024,1024]{1,0:T(8,128)(2,1)S(1)}, bf16[1024,1024]{1,0:T(8,128)(2,1)}, u32[]{:S(2)}) copy-start(bf16[1024,1024]{1,0:T(8,128)(2,1)} %param.19) | copy-start | bytes 6291460
  7.8 93.2 %collective-permute-start.8 = (bf16[256,512]{0,1:T(8,128)(2,1)}, bf16[256,512]{0,1:T(8,128)(2,1)}, u32[]{:S(2)}, u32[]{:S(2)}) collective-permute-start(bf16[256,512]{0,1:T(8,128)(2,1)} %bitcast.9), channel_id=1, source_target_pairs={{0,64},{1,65},{32,96},{33,97},{2,66},{3,67},{34,98},{35,99},{4,68}... | collective-permute-start | bytes 786440 | tf_op jit(solution)/shard_map/ppermute | solution.py:27
  14.0 91.5 %collective-permute-start.9 = (bf16[256,512]{0,1:T(8,128)(2,1)}, bf16[256,512]{0,1:T(8,128)(2,1)}, u32[]{:S(2)}, u32[]{:S(2)}) collective-permute-start(bf16[256,512]{0,1:T(8,128)(2,1)} %bitcast.9), channel_id=1, source_target_pairs={{0,33},{1,64},{32,65},{33,96},{64,97},{2,35},{3,66},{34,67},{35,98... | collective-permute-start | bytes 786440 | tf_op jit(solution)/shard_map/ppermute | solution.py:27
  16.0 91.9 %collective-permute-start.10 = (bf16[256,512]{0,1:T(8,128)(2,1)}, bf16[256,512]{0,1:T(8,128)(2,1)}, u32[]{:S(2)}, u32[]{:S(2)}) collective-permute-start(bf16[256,512]{0,1:T(8,128)(2,1)} %bitcast.9), channel_id=1, source_target_pairs={{0,32},{1,33},{32,64},{33,65},{64,96},{65,97},{2,34},{3,35},{34,66... | collective-permute-start | bytes 786440 | tf_op jit(solution)/shard_map/ppermute | solution.py:27
  18.8 92.4 %collective-permute-start.11 = (bf16[256,512]{0,1:T(8,128)(2,1)}, bf16[256,512]{0,1:T(8,128)(2,1)}, u32[]{:S(2)}, u32[]{:S(2)}) collective-permute-start(bf16[256,512]{0,1:T(8,128)(2,1)} %bitcast.9), channel_id=1, source_target_pairs={{0,1},{1,32},{32,33},{33,64},{64,65},{65,96},{96,97},{2,3},{3,34},... | collective-permute-start | bytes 786440 | tf_op jit(solution)/shard_map/ppermute | solution.py:27
  21.0 62.7 %collective-permute-start.4 = (s32[256]{0:T(256)S(1)}, s32[256]{0:T(256)S(1)}, u32[]{:S(2)}, u32[]{:S(2)}) collective-permute-start(s32[256]{0:T(256)S(1)} %bitcast.320), channel_id=1, source_target_pairs={{0,64},{1,65},{32,96},{33,97},{2,66},{3,67},{34,98},{35,99},{4,68}... | collective-permute-start | bytes 3080 | tf_op jit(solution)/shard_map/ppermute | solution.py:27
  27.6 109.2 %copy-start.20 = (bf16[256,16,32]{0,2,1:T(8,128)(2,1)}, bf16[256,16,32]{0,2,1:T(8,128)(2,1)S(1)}, u32[]{:S(2)}) copy-start(bf16[256,16,32]{0,2,1:T(8,128)(2,1)S(1)} %get-tuple-element.85) | copy-start | bytes 786436
  83.7 2.4 collective-permute-start.5
  86.0 6.2 %collective-permute-start.6 = (s32[256]{0:T(256)S(1)}, s32[256]{0:T(256)S(1)}, u32[]{:S(2)}, u32[]{:S(2)}) collective-permute-start(s32[256]{0:T(256)S(1)} %bitcast.322), channel_id=1, source_target_pairs={{0,32},{1,33},{32,64},{33,65},{64,96},{65,97},{2,34},{3,35},{34,66... | collective-permute-start | bytes 3080 | tf_op jit(solution)/shard_map/ppermute | solution.py:27
  92.2 3.3 collective-permute-start.7
  95.6 16.7 %collective-permute-start = (bf16[256,512]{1,0:T(8,128)(2,1)}, bf16[256,512]{1,0:T(8,128)(2,1)S(1)}, u32[]{:S(2)}, u32[]{:S(2)}) collective-permute-start(bf16[256,512]{1,0:T(8,128)(2,1)} %convolution_convert_fusion.7), channel_id=1, source_target_pairs={{0,64},{1,65},{32,96},{33,97},{2,66},{3,67},{34,98},{35,99},{4,68}... | collective-permute-start | bytes 786440 | tf_op jit(solution)/shard_map/ppermute | solution.py:27
  101.0 24.2 %copy-start.29 = (pred[256,1280]{0,1:T(8,128)(4,1)}, pred[256,1280]{0,1:T(8,128)(4,1)S(1)}, u32[]{:S(2)}) copy-start(pred[256,1280]{0,1:T(8,128)(4,1)S(1)} %fusion.41) | copy-start | bytes 983044
  101.1 12.0 %collective-permute-start.1 = (bf16[256,512]{1,0:T(8,128)(2,1)}, bf16[256,512]{1,0:T(8,128)(2,1)S(1)}, u32[]{:S(2)}, u32[]{:S(2)}) collective-permute-start(bf16[256,512]{1,0:T(8,128)(2,1)} %convolution_convert_fusion.7), channel_id=1, source_target_pairs={{0,33},{1,64},{32,65},{33,96},{64,97},{2,35},{3,66},{34,67},{35,98... | collective-permute-start | bytes 786440 | tf_op jit(solution)/shard_map/ppermute | solution.py:27
  105.5 11.1 %collective-permute-start.2 = (bf16[256,512]{1,0:T(8,128)(2,1)}, bf16[256,512]{1,0:T(8,128)(2,1)S(1)}, u32[]{:S(2)}, u32[]{:S(2)}) collective-permute-start(bf16[256,512]{1,0:T(8,128)(2,1)} %convolution_convert_fusion.7), channel_id=1, source_target_pairs={{0,32},{1,33},{32,64},{33,65},{64,96},{65,97},{2,34},{3,35},{34,66... | collective-permute-start | bytes 786440 | tf_op jit(solution)/shard_map/ppermute | solution.py:27
  107.9 12.5 %collective-permute-start.3 = (bf16[256,512]{1,0:T(8,128)(2,1)}, bf16[256,512]{1,0:T(8,128)(2,1)S(1)}, u32[]{:S(2)}, u32[]{:S(2)}) collective-permute-start(bf16[256,512]{1,0:T(8,128)(2,1)} %convolution_convert_fusion.7), channel_id=1, source_target_pairs={{0,1},{1,32},{32,33},{33,64},{64,65},{65,96},{96,97},{2,3},{3,34},... | collective-permute-start | bytes 786440 | tf_op jit(solution)/shard_map/ppermute | solution.py:27
  112.2 24.5 %copy-start.14 = (bf16[1280,8,64]{0,2,1:T(8,128)(2,1)}, bf16[1280,8,64]{0,2,1:T(8,128)(2,1)S(1)}, u32[]{:S(2)}) copy-start(bf16[1280,8,64]{0,2,1:T(8,128)(2,1)S(1)} %constant_dynamic-update-slice_fusion.6) | copy-start | bytes 3932164
  298.5 55.6 %copy-start.4 = (f32[256,1024]{1,0:T(8,128)S(1)}, f32[256,1024]{1,0:T(8,128)}, u32[]{:S(2)}) copy-start(f32[256,1024]{1,0:T(8,128)} %copy-done.3) | copy-start | bytes 3145732
  298.5 55.6 %copy-start.16 = (bf16[1,256,1024]{2,1,0:T(8,128)(2,1)S(1)}, bf16[1,256,1024]{2,1,0:T(8,128)(2,1)}, u32[]{:S(2)}) copy-start(bf16[1,256,1024]{2,1,0:T(8,128)(2,1)} %param.27) | copy-start | bytes 1572868
  298.5 55.6 %copy-start.35 = (f32[256]{0:T(256)S(1)}, f32[256]{0:T(256)}, u32[]{:S(2)}) copy-start(f32[256]{0:T(256)} %copy-done.34) | copy-start | bytes 3076
  298.5 55.6 %copy-start.41 = (f32[256]{0:T(256)S(1)}, f32[256]{0:T(256)}, u32[]{:S(2)}) copy-start(f32[256]{0:T(256)} %get-tuple-element.97) | copy-start | bytes 3076
  416.2 29.1 %collective-permute-start.16 = (bf16[256,512]{0,1:T(8,128)(2,1)}, bf16[256,512]{0,1:T(8,128)(2,1)}, u32[]{:S(2)}, u32[]{:S(2)}) collective-permute-start(bf16[256,512]{0,1:T(8,128)(2,1)} %bitcast.59), channel_id=1, source_target_pairs={{1,0},{32,1},{33,32},{64,33},{65,64},{96,65},{97,96},{3,2},{34,3},... | collective-permute-start | bytes 786440 | tf_op jit(solution)/shard_map/ppermute | solution.py:27
  424.8 9.5 %collective-permute-start.12 = (bf16[256,512]{0,1:T(8,128)(2,1)}, bf16[256,512]{0,1:T(8,128)(2,1)}, u32[]{:S(2)}, u32[]{:S(2)}) collective-permute-start(bf16[256,512]{0,1:T(8,128)(2,1)} %bitcast.48), channel_id=1, source_target_pairs={{1,0},{32,1},{33,32},{64,33},{65,64},{96,65},{97,96},{3,2},{34,3},... | collective-permute-start | bytes 786440 | tf_op jit(solution)/shard_map/ppermute | solution.py:27
  426.7 11.4 %collective-permute-start.13 = (bf16[256,512]{0,1:T(8,128)(2,1)}, bf16[256,512]{0,1:T(8,128)(2,1)}, u32[]{:S(2)}, u32[]{:S(2)}) collective-permute-start(bf16[256,512]{0,1:T(8,128)(2,1)} %bitcast.49), channel_id=1, source_target_pairs={{32,0},{33,1},{64,32},{65,33},{96,64},{97,65},{34,2},{35,3},{66,34... | collective-permute-start | bytes 786440 | tf_op jit(solution)/shard_map/ppermute | solution.py:27
  428.0 12.8 %collective-permute-start.14 = (bf16[256,512]{0,1:T(8,128)(2,1)}, bf16[256,512]{0,1:T(8,128)(2,1)}, u32[]{:S(2)}, u32[]{:S(2)}) collective-permute-start(bf16[256,512]{0,1:T(8,128)(2,1)} %bitcast.50), channel_id=1, source_target_pairs={{33,0},{64,1},{65,32},{96,33},{97,64},{35,2},{66,3},{67,34},{98,35... | collective-permute-start | bytes 786440 | tf_op jit(solution)/shard_map/ppermute | solution.py:27
  429.3 14.1 %collective-permute-start.15 = (bf16[256,512]{0,1:T(8,128)(2,1)S(1)}, bf16[256,512]{0,1:T(8,128)(2,1)}, u32[]{:S(2)}, u32[]{:S(2)}) collective-permute-start(bf16[256,512]{0,1:T(8,128)(2,1)S(1)} %bitcast.318), channel_id=1, source_target_pairs={{64,0},{65,1},{96,32},{97,33},{66,2},{67,3},{98,34},{99,35},{68,4}... | collective-permute-start | bytes 786440 | tf_op jit(solution)/shard_map/ppermute | solution.py:27
  434.3 12.8 %collective-permute-start.17 = (bf16[256,512]{0,1:T(8,128)(2,1)}, bf16[256,512]{0,1:T(8,128)(2,1)S(1)}, u32[]{:S(2)}, u32[]{:S(2)}) collective-permute-start(bf16[256,512]{0,1:T(8,128)(2,1)} %bitcast.60), channel_id=1, source_target_pairs={{32,0},{33,1},{64,32},{65,33},{96,64},{97,65},{34,2},{35,3},{66,34... | collective-permute-start | bytes 786440 | tf_op jit(solution)/shard_map/ppermute | solution.py:27
  438.1 10.7 %collective-permute-start.18 = (bf16[256,512]{0,1:T(8,128)(2,1)}, bf16[256,512]{0,1:T(8,128)(2,1)S(1)}, u32[]{:S(2)}, u32[]{:S(2)}) collective-permute-start(bf16[256,512]{0,1:T(8,128)(2,1)} %bitcast.61), channel_id=1, source_target_pairs={{33,0},{64,1},{65,32},{96,33},{97,64},{35,2},{66,3},{67,34},{98,35... | collective-permute-start | bytes 786440 | tf_op jit(solution)/shard_map/ppermute | solution.py:27
  440.8 16.4 %collective-permute-start.19 = (bf16[256,512]{0,1:T(8,128)(2,1)}, bf16[256,512]{0,1:T(8,128)(2,1)S(1)}, u32[]{:S(2)}, u32[]{:S(2)}) collective-permute-start(bf16[256,512]{0,1:T(8,128)(2,1)} %bitcast.62), channel_id=1, source_target_pairs={{64,0},{65,1},{96,32},{97,33},{66,2},{67,3},{98,34},{99,35},{68,4}... | collective-permute-start | bytes 786440 | tf_op jit(solution)/shard_map/ppermute | solution.py:27
  444.9 13.5 %copy-start.23 = (bf16[1024,512]{1,0:T(8,128)(2,1)S(1)}, bf16[1024,512]{1,0:T(8,128)(2,1)}, u32[]{:S(2)}) copy-start(bf16[1024,512]{1,0:T(8,128)(2,1)} %param.21) | copy-start | bytes 3145732
  (32 other events, 122.5 us)

commit v3 on v2

--- a/solution.py
+++ b/solution.py
@@ -304,54 +304,6 @@
             reducer.step_sum(da)
     for reducer in reducers:
         reducer.finish()
-
-
-def gather_kernel(own_ref, out_ref, blocks, send_sems, recv_sems, local_sem):
-    greet_plane()
-    blocks[lax.axis_index("grp")] = own_ref[...]
-    gathers = [PlaneGather(part, blocks, send_sems, recv_sems) for part in (0, 1)]
-    for gather in gathers:
-        gather.begin()
-    for gather in gathers:
-        gather.spread(0)
-    for gather in gathers:
-        gather.forward_first()
-        gather.spread(-1)
-        gather.spread(1)
-    for gather in gathers:
-        gather.forward_second(0)
-    for gather in gathers:
-        gather.wait_far_first()
-        gather.spread(2)
-    for da in (-1, 1, 2):
-        for gather in gathers:
-            gather.forward_second(da)
-    for da in (0, -1, 1, 2):
-        for gather in gathers:
-            gather.wait_far_second(da)
-    for gather in gathers:
-        gather.finish()
-    copy = pltpu.make_async_copy(blocks, out_ref, local_sem)
-    copy.start()
-    copy.wait()
-
-
-def gather_plane(own):
-    return pl.pallas_call(
-        gather_kernel,
-        out_shape=jax.ShapeDtypeStruct((PLANE, BLOCK, WIDTH), BF),
-        in_specs=[pl.BlockSpec(memory_space=pltpu.VMEM)],
-        out_specs=pl.BlockSpec(memory_space=pl.ANY),
-        scratch_shapes=[
-            pltpu.VMEM((PLANE, BLOCK, WIDTH), BF),
-            pltpu.SemaphoreType.DMA((40,)),
-            pltpu.SemaphoreType.DMA((40,)),
-            pltpu.SemaphoreType.DMA,
-        ],
-        compiler_params=pltpu.CompilerParams(
-            collective_id=0, has_side_effects=True, vmem_limit_bytes=58 << 20
-        ),
-    )(own)
 
 
 class RowRing:
@@ -883,6 +835,8 @@
     cot_ref,
     w_in_ref,
     w_out_ref,
+    sib_in_ref,
+    sib_out_ref,
     row_total_ref,
     score_out_ref,
     moe_ref,
@@ -916,8 +870,6 @@
     meta_recv,
     score_ssem,
     score_rsem,
-    weight_send,
-    weight_recv,
     local_sems,
     cot_sems,
     moe_sems,
@@ -935,10 +887,19 @@
         )
     pl.semaphore_signal(barrier, inc=1, device_id={"exp": 1 - core}, device_id_type=MESH)
 
-    load_in = pltpu.make_async_copy(w_in_ref, w_in.at[core], local_sems.at[0])
-    load_out = pltpu.make_async_copy(w_out_ref, w_out.at[core], local_sems.at[1])
-    load_in.start()
-    load_out.start()
+    loads = [
+        pltpu.make_async_copy(source, target, local_sems.at[slot])
+        for slot, (source, target) in enumerate(
+            (
+                (w_in_ref, w_in.at[core]),
+                (w_out_ref, w_out.at[core]),
+                (sib_in_ref, w_in.at[1 - core]),
+                (sib_out_ref, w_out.at[1 - core]),
+            )
+        )
+    ]
+    for load in loads:
+        load.start()
     blocks[me] = rows_ref[...]
     meta_in[me] = meta_ref[me]
     d_in[...] = jnp.zeros_like(d_in)
@@ -968,22 +929,8 @@
         )
         copy.start()
         meta_copies.append(copy)
-    weight_copies = []
-    for slot, (source, target) in enumerate(((w_in_ref, w_in), (w_out_ref, w_out))):
-        copy = pltpu.make_async_remote_copy(
-            src_ref=source,
-            dst_ref=target.at[core],
-            send_sem=weight_send.at[slot],
-            recv_sem=weight_recv.at[slot],
-            device_id={"exp": 1 - core},
-            device_id_type=MESH,
-        )
-        copy.start()
-        weight_copies.append(copy)
-    load_in.wait()
-    load_out.wait()
-    for copy in weight_copies:
-        copy.wait()
+    for load in loads:
+        load.wait()
     for copy in meta_copies:
         copy.wait()
     for gather in gathers:
@@ -1160,7 +1107,7 @@
     store_out.wait()
 
 
-def run_experts(rows, meta, cots, expert_in, expert_out):
+def run_experts(rows, meta, cots, expert_in, expert_out, sib_in, sib_out):
     vmem = pl.BlockSpec(memory_space=pltpu.VMEM)
     hbm = pl.BlockSpec(memory_space=pl.ANY)
     dma = pltpu.SemaphoreType.DMA
@@ -1173,7 +1120,7 @@
             jax.ShapeDtypeStruct((PLANE, BLOCK, WIDTH), BF),
             jax.ShapeDtypeStruct((WIDTH + INNER, WIDTH), BF),
         ),
-        in_specs=[vmem, vmem, hbm, hbm, hbm],
+        in_specs=[vmem, vmem, hbm, hbm, hbm, hbm, hbm],
         out_specs=(vmem, vmem, hbm, hbm),
         scratch_shapes=[
             pltpu.VMEM((PLANE, BLOCK, WIDTH), BF),
@@ -1196,34 +1143,405 @@
         + reduce_buffers()
         + [dma((40,))] * 4
         + [dma((PLANE,))] * 4
-        + [dma((2,))] * 3
+        + [dma((4,))]
         + [dma((2, GROUP)), dma((GROUP,))]
         + [dma((6,))] * 2
         + [pltpu.SemaphoreType.REGULAR],
         compiler_params=pltpu.CompilerParams(
             collective_id=2, has_side_effects=True, vmem_limit_bytes=VMEM_LIMIT
         ),
-    )(rows, meta, cots, expert_in, expert_out)
+    )(rows, meta, cots, expert_in, expert_out, sib_in, sib_out)
 
 
 VMEM_LIMIT = 63 << 20
 
 
-def place_slots(route_ids, rank_ids, experts):
-    tok_rows, top_count = route_ids.shape
-    hits = route_ids[:, :, None] == jnp.arange(experts, dtype=jnp.int32)
-    rank_of = jnp.sum(jnp.where(hits, rank_ids[:, :, None] + 1, 0), axis=1) - 1
-    chosen = rank_of >= 0
-    ranks = jnp.arange(top_count, dtype=jnp.int32)
-    counts = (rank_of[:, None, :] == ranks[None, :, None]).reshape(tok_rows, top_count * experts)
-    lowered = counts.astype(BF)
-    tok = jnp.arange(tok_rows, dtype=jnp.int32)
-    earlier = (tok[:, None] > tok[None, :]).astype(BF)
-    before = product(earlier, lowered)
-    totals = jnp.sum(counts.astype(F32), axis=0).reshape(top_count, experts)
-    offsets = (jnp.cumsum(totals, axis=0) - totals).reshape(1, top_count * experts)
-    place = jnp.where(counts, before + offsets, 0.0).reshape(tok_rows, top_count, experts)
-    return chosen, jnp.sum(place, axis=1)
+def rope_lanes(values, cosine, sine):
+    lane = lax.broadcasted_iota(jnp.int32, (1, 128), 1)
+    lower = lax.rem(lane, 64) < 32
+    chunks = []
+    for begin in range(0, values.shape[1], 128):
+        chunk = values[:, begin : begin + 128]
+        partner = jnp.where(lower, pltpu.roll(chunk, 96, 1), pltpu.roll(chunk, 32, 1))
+        chunks.append(chunk * cosine + partner * sine)
+    return chunks
+
+
+def norm_scale(values):
+    return lax.rsqrt(jnp.mean(values * values, axis=1, keepdims=True) + EPSILON)
+
+
+def slot_table(routes, ranks):
+    expert = lax.broadcasted_iota(jnp.int32, (BLOCK, 32), 1)
+    rank_of = jnp.zeros((BLOCK, 32), jnp.int32)
+    for k in range(8):
+        rank_of = rank_of + jnp.where(routes[:, k : k + 1] == expert, ranks[:, k : k + 1] + 1, 0)
+    chosen = rank_of > 0
+    row = lax.broadcasted_iota(jnp.int32, (BLOCK, BLOCK), 0)
+    lane = lax.broadcasted_iota(jnp.int32, (BLOCK, BLOCK), 1)
+    source = lax.broadcasted_iota(jnp.int32, (32, BLOCK), 0)
+    target = lax.broadcasted_iota(jnp.int32, (32, BLOCK), 1)
+    repeat = jnp.where(lax.rem(target, 32) == source, 1.0, 0.0).astype(BF)
+    rank_wide = dot_nn(rank_of.astype(F32).astype(BF), repeat)
+    hit = rank_wide == (lane // 32 + 1).astype(F32)
+    counts = jnp.where(hit, 1.0, 0.0)
+    earlier = jnp.where(row > lane, 1.0, 0.0).astype(BF)
+    before = dot_nn(earlier, counts.astype(BF))
+    totals = jnp.sum(counts, axis=0, keepdims=True)
+    lower = (lax.rem(row, 32) == lax.rem(lane, 32)) & (row // 32 < lane // 32)
+    offsets = dot_nn(totals.astype(BF), jnp.where(lower, 1.0, 0.0).astype(BF))
+    place = jnp.where(hit, before + offsets, 0.0)
+    place = place[:, :128] + place[:, 128:]
+    place = place + pltpu.roll(place, 64, 1)
+    place = place + pltpu.roll(place, 32, 1)
+    place = place[:, :32]
+    return chosen, jnp.where(chosen & (place < CAPACITY), place, -1.0)
+
+
+def attend_kernel(
+    tokens_ref,
+    seg_ref,
+    routes_ref,
+    ranks_ref,
+    gain_one_ref,
+    w_query_ref,
+    w_key_ref,
+    w_value_ref,
+    w_output_ref,
+    gain_two_ref,
+    w_router_ref,
+    cosine_ref,
+    sine_ref,
+    cot_ref,
+    w_in_ref,
+    w_out_ref,
+    routed_ref,
+    residual_ref,
+    heads_ref,
+    normed_ref,
+    query_ref,
+    kv_ref,
+    lse_ref,
+    bias_ref,
+    gates_ref,
+    meta_ref,
+    cots_ref,
+    sib_in_ref,
+    sib_out_ref,
+    segs,
+    top,
+    expsum,
+    acc,
+    send_sems,
+    recv_sems,
+    kv_send,
+    kv_recv,
+    seg_send,
+    seg_recv,
+    weight_send,
+    weight_recv,
+    local_sem,
+):
+    line, plane, core = lax.axis_index("seq"), lax.axis_index("grp"), lax.axis_index("exp")
+    block = 2 * line + core
+    row, column = plane // 4, lax.rem(plane, 4)
+    barrier = pltpu.get_barrier_semaphore()
+    for index in (
+        mod4(row + 1) * 4 + column,
+        mod4(row - 1) * 4 + column,
+        row * 4 + mod4(column + 1),
+        row * 4 + mod4(column - 1),
+    ):
+        pl.semaphore_signal(barrier, inc=1, device_id={"grp": index}, device_id_type=MESH)
+    for step in (1, 2, 3):
+        pl.semaphore_signal(
+            barrier, inc=1, device_id={"seq": mod4(line + step)}, device_id_type=MESH
+        )
+    pl.semaphore_signal(barrier, inc=1, device_id={"exp": 1 - core}, device_id_type=MESH)
+    own_cot = pltpu.make_async_copy(cot_ref, cots_ref.at[plane], local_sem)
+    own_cot.start()
+
+    tokens = tokens_ref[...].astype(F32)
+    normed = (tokens * norm_scale(tokens) * gain_one_ref[...]).astype(BF)
+    normed_ref[...] = normed
+    cosine, sine = cosine_ref[...], sine_ref[...]
+    keys = dot_nn(normed, w_key_ref[...])
+    values = dot_nn(normed, w_value_ref[...]).astype(BF)
+    key_chunks = rope_lanes(keys, cosine, sine)
+    for head in range(KV_HEADS):
+        chunk = key_chunks[head // 2].astype(BF)
+        key = chunk[:, (head % 2) * 64 : (head % 2) * 64 + 64]
+        kv_ref[0, head] = jnp.concatenate([key, values[:, head * 64 : head * 64 + 64]], axis=1)
+    segs[0] = seg_ref[...]
+    own_cot.wait()
+    pl.semaphore_wait(barrier, 8)
+
+    def kv_copies(source, target, device, slot):
+        return [
+            pltpu.make_async_remote_copy(
+                src_ref=ref.at[source],
+                dst_ref=ref.at[target],
+                send_sem=sends.at[slot],
+                recv_sem=recvs.at[target],
+                device_id=device,
+                device_id_type=MESH,
+            )
+            for ref, sends, recvs in ((kv_ref, kv_send, kv_recv), (segs, seg_send, seg_recv))
+        ]
+
+    sibling = {"exp": 1 - core}
+    to_near = kv_copies(0, 2, {"seq": mod4(line + 1)}, 1)
+    to_far = kv_copies(0, 4, {"seq": mod4(line + 2)}, 2)
+    to_sibling = kv_copies(0, 1, sibling, 0)
+    forward_near = kv_copies(2, 3 - 2 * core, sibling, 3)
+    forward_far = kv_copies(4, 3, sibling, 4)
+
+    def begin(copies):
+        for copy in copies:
+            copy.start()
+
+    def sent(copies):
+        for copy in copies:
+            copy.wait_send()
+
+    @pl.when(line < 3)
+    def _():
+        begin(to_near)
+
+    @pl.when(core == 0)
+    def _():
+        begin(to_sibling)
+
+    @pl.when(line < 2)
+    def _():
+        begin(to_far)
+
+    gathers = [PlaneGather(part, cots_ref, send_sems, recv_sems) for part in (0, 1)]
+    for gather in gathers:
+        gather.begin()
+    for gather in gathers:
+        gather.spread(0)
+    weight_copies = [
+        pltpu.make_async_remote_copy(
+            src_ref=source,
+            dst_ref=target,
+            send_sem=weight_send.at[slot],
+            recv_sem=weight_recv.at[slot],
+            device_id=sibling,
+            device_id_type=MESH,
+        )
+        for slot, (source, target) in enumerate(((w_in_ref, sib_in_ref), (w_out_ref, sib_out_ref)))
+    ]
+    begin(weight_copies)
+
+    lane = lax.broadcasted_iota(jnp.int32, (1, 128), 1)
+    queries = dot_nn(normed, w_query_ref[...])
+    for head, chunk in enumerate(rope_lanes(queries, cosine, sine)):
+        chunk = (chunk.astype(BF).astype(F32) * ATTENTION_FACTOR)
+        query_ref[head, :BLOCK, :] = jnp.where(lane < 64, chunk, 0.0).astype(BF)
+        query_ref[head, BLOCK:, :] = jnp.where(lane < 64, pltpu.roll(chunk, 64, 1), 0.0).astype(BF)
+    top[...] = jnp.full(top.shape, MASKED, F32)
+    expsum[...] = jnp.zeros(expsum.shape, F32)
+    acc[...] = jnp.zeros(acc.shape, F32)
+    seg_column = seg_ref[...].T[:, :1]
+
+    def attend(slot):
+        i = lax.broadcasted_iota(jnp.int32, (BLOCK, BLOCK), 0)
+        j = lax.broadcasted_iota(jnp.int32, (BLOCK, BLOCK), 1)
+        distance = slot * BLOCK + i - j
+        allowed = (seg_column == segs[slot, 0:1, :]) & (distance >= 0) & (distance < WINDOW)
+        bias = jnp.where(allowed, 0.0, MASKED)
+        bias_ref[slot] = bias
+
+        @pl.loop(0, KV_HEADS)
+        def _(head):
+            pair = kv_ref[slot, head]
+            one = bias_ref[slot]
+            score = dot_nt(query_ref[head], pair)
+            score = score + jnp.concatenate([one, one], axis=0)
+            old = top[head][:, :1]
+            new = jnp.maximum(old, jnp.max(score, axis=1, keepdims=True))
+            weight = jnp.exp(score - new)
+            fade = jnp.exp(old - new)
+            expsum[head] = expsum[head] * fade + jnp.sum(weight, axis=1, keepdims=True)
+            acc[head] = acc[head] * fade + dot_nn(weight.astype(BF), pair)
+            top[head] = jnp.broadcast_to(new, (2 * BLOCK, 128))
+
+    def wait_block(slot):
+        for ref, sends, recvs in ((kv_ref, kv_send, kv_recv), (segs, seg_send, seg_recv)):
+            pltpu.make_async_remote_copy(
+                src_ref=ref.at[slot],
+                dst_ref=ref.at[slot],
+                send_sem=sends.at[0],
+                recv_sem=recvs.at[slot],
+                device_id=sibling,
+                device_id_type=MESH,
+            ).wait_recv()
+
+    attend(0)
+    for gather in gathers:
+        gather.forward_first()
+        gather.spread(-1)
+        gather.spread(1)
+
+    chosen, kept = slot_table(routes_ref[...], ranks_ref[...])
+    kept_rows = jnp.concatenate([kept, jnp.zeros((BLOCK, 96), F32)], axis=1).T
+    for index in range(PLANE):
+        meta_ref[index, 0:2, :] = kept_rows[2 * index : 2 * index + 2]
+        meta_ref[index, 4:8, :] = jnp.zeros((4, BLOCK), F32)
+
+    first = 2 - core
+
+    @pl.when(block >= first)
+    def _():
+        wait_block(first)
+
+        @pl.when(core == 0)
+        def _():
+            begin(forward_near)
+
+        attend(first)
+
+    for gather in gathers:
+        gather.forward_second(0)
+    for gather in gathers:
+        gather.wait_far_first()
+        gather.spread(2)
+    second = 1 + core
+
+    @pl.when(block >= second)
+    def _():
+        wait_block(second)
+
+        @pl.when(core == 1)
+        def _():
+            begin(forward_near)
+
+        attend(second)
+
+    for da in (-1, 1):
+        for gather in gathers:
+            gather.forward_second(da)
+    third = 4 - core
+
+    @pl.when(block >= third)
+    def _():
+        wait_block(third)
+        attend(third)
+
+    for gather in gathers:
+        gather.forward_second(2)
+    fourth = 3 + core
+
+    @pl.when(block >= fourth)
+    def _():
+        wait_block(fourth)
+
+        @pl.when(core == 1)
+        def _():
+            begin(forward_far)
+
+        attend(fourth)
+
+    for head in range(KV_HEADS):
+        inverse = 1.0 / expsum[head][:, :1]
+        pair = acc[head] * inverse
+        heads_ref[:, head * 128 : head * 128 + 128] = jnp.where(
+            lane < 64, pltpu.roll(pair[:BLOCK], 64, 1), pair[BLOCK:]
+        ).astype(BF)
+        lse_ref[head] = top[head] + jnp.log(expsum[head])
+    branch = dot_nn(heads_ref[...], w_output_ref[...])
+    residual = tokens_ref[...].astype(F32) + RESIDUAL_MULT * branch
+    residual_ref[...] = residual
+    routed = (residual * norm_scale(residual) * gain_two_ref[...]).astype(BF)
+    routed_ref[...] = routed
+    logits = dot_nn(routed, w_router_ref[...])
+    logits = jnp.where(chosen, logits, MASKED)
+    powers = jnp.exp(logits - jnp.max(logits, axis=1, keepdims=True))
+    gates = jnp.where(chosen, powers / jnp.sum(powers, axis=1, keepdims=True), 0.0)
+    gates_ref[...] = gates
+    gate_rows = jnp.concatenate([gates, jnp.zeros((BLOCK, 96), F32)], axis=1).T
+    for index in range(PLANE):
+        meta_ref[index, 2:4, :] = gate_rows[2 * index : 2 * index + 2]
+
+    for da in (0, -1, 1, 2):
+        for gather in gathers:
+            gather.wait_far_second(da)
+    for gather in gathers:
+        gather.finish()
+    for copy in weight_copies:
+        copy.wait()
+
+    @pl.when(line < 3)
+    def _():
+        sent(to_near)
+
+    @pl.when(core == 0)
+    def _():
+        sent(to_sibling)
+
+    @pl.when(line < 2)
+    def _():
+        sent(to_far)
+
+    @pl.when(line >= 1)
+    def _():
+        sent(forward_near)
+
+    @pl.when((line >= 2) & (core == 1))
+    def _():
+        sent(forward_far)
+
+
+def run_attention(
+    tokens, seg_tile, routes, ranks, gain_one, w_query, w_key, w_value, w_output, gain_two,
+    w_router, cosine, sine, cot, expert_in, expert_out,
+):
+    vmem = pl.BlockSpec(memory_space=pltpu.VMEM)
+    hbm = pl.BlockSpec(memory_space=pl.ANY)
+    dma = pltpu.SemaphoreType.DMA
+    shape = jax.ShapeDtypeStruct
+    return pl.pallas_call(
+        attend_kernel,
+        out_shape=(
+            shape((BLOCK, WIDTH), BF),
+            shape((BLOCK, WIDTH), F32),
+            shape((BLOCK, WIDTH), BF),
+            shape((BLOCK, WIDTH), BF),
+            shape((KV_HEADS, 2 * BLOCK, 128), BF),
+            shape((5, KV_HEADS, BLOCK, 128), BF),
+            shape((KV_HEADS, 2 * BLOCK, 128), F32),
+            shape((5, BLOCK, BLOCK), F32),
+            shape((BLOCK, 32), F32),
+            shape((PLANE, 8, BLOCK), F32),
+            shape((PLANE, BLOCK, WIDTH), BF),
+            shape((WIDTH, 2 * INNER), BF),
+            shape((INNER, WIDTH), BF),
+        ),
+        in_specs=[vmem] * 13 + [hbm] * 3,
+        out_specs=(vmem,) * 10 + (hbm,) * 3,
+        scratch_shapes=[
+            pltpu.VMEM((5, 8, BLOCK), F32),
+            pltpu.VMEM((KV_HEADS, 2 * BLOCK, 128), F32),
+            pltpu.VMEM((KV_HEADS, 2 * BLOCK, 128), F32),
+            pltpu.VMEM((KV_HEADS, 2 * BLOCK, 128), F32),
+            dma((40,)),
+            dma((40,)),
+            dma((5,)),
+            dma((5,)),
+            dma((5,)),
+            dma((5,)),
+            dma((2,)),
+            dma((2,)),
+            dma,
+        ],
+        compiler_params=pltpu.CompilerParams(
+            collective_id=0, has_side_effects=True, vmem_limit_bytes=58 << 20
+        ),
+    )(
+        tokens, seg_tile, routes, ranks, gain_one, w_query, w_key, w_value, w_output, gain_two,
+        w_router, cosine, sine, cot, expert_in, expert_out,
+    )
 
 
 def on_device(
@@ -1255,84 +1573,23 @@
     hop_count = min(-(-WINDOW // tok_rows), blocks - 1)
     key_span = (hop_count + 1) * tok_rows
     inputs = tokens[0].astype(jnp.float32)
-    seg_ids = segments[0]
-    route_ids = routes[0]
-    rank_ids = rank_order[0]
     positions = block_id * tok_rows + jnp.arange(tok_rows, dtype=jnp.int32)
     cosine, sine_part = rope_tables(positions, head_dim)
+    cosine_lanes = jnp.tile(cosine[:, 0], (1, 4))
+    sine_lanes = jnp.tile(jnp.concatenate([-sine_part[:, 0], sine_part[:, 0]], axis=1), (1, 2))
+    seg_tile = jnp.broadcast_to(segments.astype(jnp.float32), (8, tok_rows))
+    (
+        routed_in, residual, heads_out, normed, query_heads, kv_heads_all, lse, bias, gates, meta,
+        cots, sib_in, sib_out,
+    ) = run_attention(
+        tokens[0], seg_tile, routes[0], rank_order[0], attn_gain[None], w_query, w_key, w_value,
+        w_output, ffn_gain[None], w_router, cosine_lanes, sine_lanes, cotangent[0], expert_in[0],
+        expert_out[0],
+    )
     scale_one = lax.rsqrt(jnp.mean(inputs * inputs, axis=-1, keepdims=True) + EPSILON)
-    normed = (inputs * scale_one * attn_gain).astype(jnp.bfloat16)
-    query_pre = product(normed, w_query).reshape(tok_rows, q_heads, head_dim)
-    key_pre = product(normed, w_key).reshape(tok_rows, kv_heads, head_dim)
-    value_own = product(normed, w_value).astype(jnp.bfloat16)
-    query_rows = (
-        rotate(query_pre, cosine, sine_part)
-        .astype(jnp.bfloat16)
-        .reshape(tok_rows, kv_heads, group_size, head_dim)
-    )
-    key_own = rotate(key_pre, cosine, sine_part).astype(jnp.bfloat16).reshape(tok_rows, kv_width)
-    key_parts = [key_own]
-    value_parts = [value_own]
-    seg_parts = [seg_ids]
-    for hop_index in range(1, hop_count + 1):
-        key_far, value_far, seg_far = from_behind(
-            (key_own, value_own, seg_ids), ("seq", "exp"), hop_index
-        )
-        key_parts.insert(0, key_far)
-        value_parts.insert(0, value_far)
-        seg_parts.insert(0, seg_far)
-    key_gathered = jnp.concatenate(key_parts, axis=0).reshape(key_span, kv_heads, head_dim)
-    value_gathered = jnp.concatenate(value_parts, axis=0).reshape(key_span, kv_heads, head_dim)
-    seg_all = jnp.concatenate(seg_parts, axis=0)
-    key_pos = (block_id - hop_count) * tok_rows + jnp.arange(key_span, dtype=jnp.int32)
-    distance = positions[:, None] - key_pos[None, :]
-    allowed = (
-        (seg_ids[:, None] == seg_all[None, :])
-        & (distance >= 0)
-        & (distance < WINDOW)
-        & (key_pos[None, :] >= 0)
-    )
-
-    def scores_of():
-        raw_scores = ATTENTION_FACTOR * jnp.einsum(
-            "dklp,okp->kldo", query_rows, key_gathered, preferred_element_type=jnp.float32
-        )
-        return jnp.where(allowed[None, None], raw_scores, MASKED)
-
-    score_matrix = scores_of()
-    top_score = jnp.max(score_matrix, axis=-1, keepdims=True)
-    expsum = jnp.sum(jnp.exp(score_matrix - top_score), axis=-1, keepdims=True)
-    probability_lowered = (jnp.exp(score_matrix - top_score) / expsum).astype(jnp.bfloat16)
-    heads_out = (
-        jnp.einsum(
-            "uzjq,quk->juzk",
-            probability_lowered,
-            value_gathered,
-            preferred_element_type=jnp.float32,
-        )
-        .astype(jnp.bfloat16)
-        .reshape(tok_rows, model_width)
-    )
-    branch = product(heads_out, w_output)
-    residual = inputs + RESIDUAL_MULT * branch
     scale_two = lax.rsqrt(jnp.mean(residual * residual, axis=-1, keepdims=True) + EPSILON)
-    routed_in = (residual * scale_two * ffn_gain).astype(jnp.bfloat16)
-    logits = product(routed_in, w_router)
-    chosen, slot_place = place_slots(route_ids, rank_ids, experts)
-    gates = jax.nn.softmax(jnp.where(chosen, logits, MASKED), axis=1)
-    gates = jnp.where(chosen, gates, 0.0)
-    kept_place = jnp.where(chosen & (slot_place < CAPACITY), slot_place, -1.0)
-    meta = jnp.concatenate(
-        [
-            kept_place.T.reshape(PLANE, 2, tok_rows),
-            gates.T.reshape(PLANE, 2, tok_rows),
-            jnp.zeros((PLANE, 4, tok_rows), jnp.float32),
-        ],
-        axis=1,
-    )
-    cots = gather_plane(cotangent[0])
     expert_row_sum, scores, moe_partial, expert_grads = run_experts(
-        routed_in, meta, cots, expert_in[0], expert_out[0]
+        routed_in, meta, cots, expert_in[0], expert_out[0], sib_in, sib_out
     )
     moe_out, expert_total = return_plane(moe_partial, expert_grads)
     output = (residual + RESIDUAL_MULT * moe_out).astype(jnp.bfloat16)[None]
@@ -1356,8 +1613,23 @@
         .astype(jnp.bfloat16)
         .reshape(tok_rows, kv_heads, group_size, head_dim)
     )
-    score_matrix = scores_of()
-    probs_full = jnp.exp(score_matrix - top_score) / expsum
+    kv_cat = jnp.flip(kv_heads_all, 0).transpose(0, 2, 1, 3).reshape(key_span, kv_heads, 128)
+    key_gathered, value_gathered = kv_cat[..., :64], kv_cat[..., 64:]
+    valid = (block_id - jnp.arange(hop_count, -1, -1) >= 0).repeat(tok_rows)
+    key_gathered = jnp.where(valid[:, None, None], key_gathered, 0)
+    value_gathered = jnp.where(valid[:, None, None], value_gathered, 0)
+    query_rows = (
+        (query_heads[..., :64].astype(jnp.float32) * 64).astype(jnp.bfloat16)
+        .reshape(kv_heads, 2, tok_rows, head_dim).transpose(2, 0, 1, 3)
+    )
+    bias_all = jnp.where(
+        valid[None], jnp.flip(bias, 0).transpose(1, 0, 2).reshape(tok_rows, key_span), MASKED
+    )
+    raw_scores = ATTENTION_FACTOR * jnp.einsum(
+        "dklp,okp->kldo", query_rows, key_gathered, preferred_element_type=jnp.float32
+    )
+    lse_rows = lse[:, :, 0].reshape(kv_heads, 2, tok_rows, 1)
+    probs_full = jnp.exp(jnp.where(bias_all == 0, raw_scores, MASKED) - lse_rows)
     probability_lowered = probs_full.astype(jnp.bfloat16)
     prob_grad = jnp.einsum(
         "dklp,okp->kldo", head_gradient, value_gathered, preferred_element_type=jnp.float32

time: 559 us -> 519 us (0.928)
  starting transfers between devices: 52.2 us -> 19 us
  Pallas kernels: 316 us -> 341 us
  matrix products: 80 us -> 59.2 us
  waiting for transfers between devices: 24.8 us -> 11.6 us
    ppermute x20 -> x8, starting transfers between devices: 52.2 us -> 19 us  [from_behind(): lax.ppermute(value, axis, [(source, source + steps) for source in range(i...]
    pallas_call x1, Pallas kernels: 53.4 us -> 72.4 us  [run_attention(): pl.pallas_call(attend_kernel, out_shape=(shape((BLOCK, WIDTH), BF), shape...]
    ppermute x20 -> x8, waiting for transfers between devices: 24.8 us -> 11.6 us  [from_behind(): lax.ppermute(value, axis, [(source, source + steps) for source in range(i...]
    pallas_call x1, Pallas kernels: 55.5 us -> 68.2 us  [return_plane(): pl.pallas_call(return_kernel, out_shape=(jax.ShapeDtypeStruct((BLOCK, WID...]
    unnamed x106 -> x71, local copies, waits for them, and re-layouts: 20.9 us -> 8.2 us
    sub x1 -> x0, matrix products: 11.5 us -> none  [on_device(): score_matrix - top_score]
    pallas_call x1, Pallas kernels: 140 us -> 132 us  [run_experts(): pl.pallas_call(expert_kernel, out_shape=(jax.ShapeDtypeStruct((BLOCK, WID...]
    select_n x2 -> x1, other arithmetic: 0.03 us -> 6.26 us  [on_device(): value_gathered = jnp.where(valid[:, None, None], value_gathered, 0)]
  transfers between devices with their start and end apart: 20 -> 8, of which waited for: 11 -> 3; matrix products, arithmetic and copies ran while one was open for 4% -> 7% of each run, Pallas kernels for 10% -> 0%
where the time goes in v3:
time: 519 us; the launch traced here: 510 us
  Pallas kernels  341 us (66%)
  matrix products  59.2 us (11%)
  other arithmetic  46.4 us (9%)
  local copies, waits for them, and re-layouts  31.3 us (6%)
  starting transfers between devices  19 us (4%)
  waiting for transfers between devices  11.6 us (2%)
    pallas_call x1, Pallas kernels, run_experts(): pl.pallas_call(expert_kernel, out_shape=(jax.ShapeDtypeStruct((BLOCK, WID...  132 us
    pallas_call x1, Pallas kernels, run_attention(): pl.pallas_call(attend_kernel, out_shape=(shape((BLOCK, WIDTH), BF), shape...  72.4 us
    pallas_call x1, Pallas kernels, return_plane(): pl.pallas_call(return_kernel, out_shape=(jax.ShapeDtypeStruct((BLOCK, WID...  68.2 us
    pallas_call x1, Pallas kernels, total_all(): pl.pallas_call(total_kernel, out_shape=(jax.ShapeDtypeStruct((6, 1024, 51...  67.8 us
    ppermute x8, starting transfers between devices, from_behind(): lax.ppermute(value, axis, [(source, source + steps) for source in range(i...  19 us
    dot_general x1, matrix products, on_device(): jnp.einsum('dklp,okp->kldo', query_rows, key_gathered, preferred_element_...  15.2 us
    convert_element_type x1, other arithmetic, on_device(): score_gradient = (probs_full * (prob_grad - jnp.sum(probs_full * prob_gra...  14 us
    dot_general x1, matrix products, on_device(): jnp.einsum('ykze,zykm->eym', probability_lowered, head_gradient, preferre...  11.7 us
  transfers between devices with their start and end apart: 8, of which 3 were waited for; matrix products, arithmetic and copies ran while one was open for 7% of the time, Pallas kernels for 0%

profile of v3, /device:TPU:1, one launch (start us, length us, event | category | flops | bytes accessed | tf_op | source)
XLA Modules:
  0.0 509.8 jit_solution(14357853017048692739)
XLA Ops:
  3.1 1.7 copy.43.w_router_ref
  9.0 72.4 %shard_map.221 = (bf16[256,1024]{1,0:T(8,128)(2,1)}, f32[256,1024]{1,0:T(8,128)}, bf16[256,1024]{1,0:T(8,128)(2,1)}, bf16[256,1024]{1,0:T(8,128)(2,1)}, bf16[8,5...) custom-call(bf16[256,1024]{1,0:T(8,128)(2,1)} %bitcast.193, ...), custom_call_target="tpu_custom_call" | custom-call | tf_op jit(solution)/shard_map/pallas_call | solution.py:1504
  81.5 132.1 %shard_map.222 = (f32[256,1024]{1,0:T(8,128)}, f32[16,8,256]{2,1,0:T(8,128)}, bf16[16,256,1024]{2,1,0:T(8,128)(2,1)}, bf16[1536,1024]{1,0:T(8,128)(2,1)}) custom-call(bf16[256,1024]{1,0:T(8,128)(2,1)} %get-tuple-element.33.rows_ref, f32[16,8,256]{2,1,0:T(8,128)} %get-tuple-element.34.meta_ref, bf16[16,256,1024]{2,1,0:T(8,128)(2,1)} %get-tuple-element.35.cot_ref, ...), custom_call_target="tpu_custom_call" | custom-call | tf_op jit(solution)/shard_map/pallas_call | solution.py:1115
  216.4 1.7 multiply_reduce_fusion
  218.1 68.2 %shard_map.223 = (f32[256,1024]{1,0:T(8,128)}, bf16[1536,1024]{1,0:T(8,128)(2,1)}) custom-call(bf16[16,256,1024]{2,1,0:T(8,128)(2,1)} %get-tuple-element.38.partial_ref, bf16[1536,1024]{1,0:T(8,128)(2,1)} %get-tuple-element.39.grad_ref), custom_call_target="tpu_custom_call" | custom-call | tf_op jit(solution)/shard_map/pallas_call | solution.py:456
  286.4 3.0 multiply_convert_fusion.1
  290.1 1.5 convolution_convert_fusion.6
  293.1 1.7 copy.47
  294.9 6.3 %fusion.12 = (bf16[1280,8,64,1]{2,1,0,3:T(8,128)(2,1)}, bf16[1280,8,64,1]{2,1,0,3:T(8,128)(2,1)}) fusion(bf16[1280,8,128]{2,1,0:T(8,128)(2,1)S(1)} %bitcast.192, pred[1280]{0:T(1024)(128)(4,1)S(1)} %broadcast_in_dim.83), kind=kLoop, calls=%fused_computation.15 | loop fusion | flops 1310720 | bytes 5244160 | tf_op jit(solution)/shard_map/jit(_where)/select_n | solution.py:1620
  301.2 3.9 copy.61
  306.3 1.7 copy.48
  308.3 2.4 multiply_convert_fusion
  310.7 1.5 copy.49
  312.3 2.2 slice_reduce_fusion
  314.5 10.4 %fusion.14 = f32[8,1280,256,2]{2,1,3,0:T(8,128)} fusion(bf16[256,8,2,64]{0,3,2,1:T(8,128)(2,1)S(1)} %bitcast.196, bf16[1280,8,64,1]{2,1,0,3:T(8,128)(2,1)} %get-tuple-element.87), kind=kOutput, calls=%fused_computation.18 | convolution fusion | flops 671088640 | bytes 22806528 | tf_op jit(solution)/shard_map/dklp,okp->kldo/dot_general | solution.py:1634
  324.9 15.2 %fusion = (f32[8,2,256]{2,1,0:T(2,128)S(1)}, f32[8,2,256,1280]{2,3,1,0:T(8,128)}) fusion(f32[8,1280,256,2]{2,1,3,0:T(8,128)} %fusion.14, f32[8,2,256]{2,1,0:T(2,128)S(1)} %sub.49, bf16[1280,8,64,1]{0,2,3,1:T(8,128)(2,1)S(1)} %copy.61, bf16[8,2,256,64]{2,3,1,0:T(8,128)(2,1)S(1)} %copy.49, pred[256,1280]{0,1:T(8,128)(4,1)S(1)} %fusion.28), kind=kOutput, calls=%fused_computation.2 | convolution fusion | flops 697298944 | bytes 44138496 | tf_op jit(solution)/shard_map/dklp,okp->kldo/dot_general | solution.py:1628
  340.1 11.7 %fusion.58 = (bf16[1280,8,64]{0,2,1:T(8,128)(2,1)S(1)}, f32[1280,8,64]{0,2,1:T(8,128)}) fusion(bf16[256,8,2,64]{0,3,2,1:T(8,128)(2,1)S(1)} %bitcast.197, f32[8,2,256,1280]{2,3,1,0:T(8,128)} %get-tuple-element.113), kind=kOutput, calls=%fused_computation.123 | convolution fusion | flops 676986880 | bytes 25427968 | tf_op jit(solution)/shard_map/ykze,zykm->eym/dot_general | solution.py:1649
  352.8 9.0 %collective-permute-start.4 = (bf16[256,512]{0,1:T(8,128)(2,1)}, bf16[256,512]{0,1:T(8,128)(2,1)}, u32[]{:S(2)}, u32[]{:S(2)}) collective-permute-start(bf16[256,512]{0,1:T(8,128)(2,1)} %bitcast.44), channel_id=1, source_target_pairs={{1,0},{32,1},{33,32},{64,33},{65,64},{96,65},{97,96},{3,2},{34,3},... | collective-permute-start | bytes 786440 | tf_op jit(solution)/shard_map/ppermute | solution.py:27
  361.8 14.0 %fusion.2 = bf16[8,2,256,1280]{2,3,1,0:T(8,128)(2,1)S(1)} fusion(f32[8,2,256,1280]{2,3,1,0:T(8,128)} %get-tuple-element.113, f32[8,1280,256,2]{2,1,3,0:T(8,128)} %fusion.14, f32[8,2,256]{2,1,0:T(2,128)S(1)} %get-tuple-element.112), kind=kLoop, calls=%fused_computation.4 | loop fusion | flops 15728640 | bytes 52445184 | tf_op jit(solution)/shard_map/convert_element_type | solution.py:1639
  375.8 3.3 fusion.57
  380.1 1.9 collective-permute-start
  384.7 1.7 collective-permute-start.3
  386.4 1.9 convolution_multiply_fusion
  389.6 2.5 bitcast_convert_fusion
  392.1 1.6 bitcast_convert_fusion.1
  408.1 5.4 %collective-permute-done.5 = bf16[256,512]{0,1:T(8,128)(2,1)S(1)} collective-permute-done((bf16[256,512]{0,1:T(8,128)(2,1)S(1)}, bf16[256,512]{0,1:T(8,128)(2,1)S(1)}, u32[]{:S(2)}, u32[]{:S(2)}) %collective-permute-start.5) | collective-permute-done | bytes 262176 | tf_op jit(solution)/shard_map/ppermute | solution.py:27
  413.5 4.3 collective-permute-done.6
  417.8 1.8 collective-permute-done.7
  420.8 2.1 fusion.35
  429.0 67.8 %shard_map.224 = (bf16[6,1024,512]{2,1,0:T(8,128)(2,1)S(1)}, f32[80,512]{1,0:T(8,128)S(1)}) custom-call(bf16[6,1024,512]{2,1,0:T(8,128)(2,1)} %fusion.27.mats_ref, f32[80,512]{1,0:T(8,128)S(1)} %maximum_maximum_fusion.small_ref), custom_call_target="tpu_custom_call" | custom-call | tf_op jit(solution)/shard_map/pallas_call | solution.py:790
  496.8 3.0 slice_bitcast_fusion.1
  502.0 6.2 %maximum_convert_fusion = (f32[1024,1024]{1,0:T(8,128)}, f32[1024,1024]{1,0:T(8,128)}) fusion(bf16[1024,512]{1,0:T(8,128)(2,1)} %get-tuple-element.85, bf16[1024,512]{1,0:T(8,128)(2,1)} %get-tuple-element.86, bf16[1024,512]{1,0:T(8,128)(2,1)S(1)} %get-tuple-element.82, bf16[1024,512]{1,0:T(8,128)(2,1)S(1)} %get-tuple-element.81), kind=kLoop, calls=%fused_computation.21 | loop fusion | flops 8388608 | bytes 12582912 | tf_op jit(solution)/shard_map/convert_element_type | solution.py:1716
  (137 shorter events, 43.8 us)
Async XLA Ops:
  0.9 80.5 %copy-start.18 = (f32[256,32]{0,1:T(8,128)}, f32[256,32]{0,1:T(8,128)S(1)}, u32[]{:S(2)}) copy-start(f32[256,32]{0,1:T(8,128)S(1)} %get-tuple-element.106) | copy-start | bytes 98308
  81.4 133.3 %copy-start.17 = (f32[256,32]{1,0:T(8,128)S(1)}, f32[256,32]{1,0:T(8,128)}, u32[]{:S(2)}) copy-start(f32[256,32]{1,0:T(8,128)} %get-tuple-element.41) | copy-start | bytes 98308
  81.5 134.9 %copy-start.22 = (bf16[1024,32]{0,1:T(8,128)(2,1)S(1)}, bf16[1024,32]{0,1:T(8,128)(2,1)}, u32[]{:S(2)}) copy-start(bf16[1024,32]{0,1:T(8,128)(2,1)} %param.24) | copy-start | bytes 196612
  81.5 134.9 %copy-start.26 = (f32[1024]{0:T(1024)S(1)}, f32[1024]{0:T(1024)}, u32[]{:S(2)}) copy-start(f32[1024]{0:T(1024)} %param.23) | copy-start | bytes 12292
  218.1 68.2 %copy-start.9 = (bf16[1,256,1024]{2,1,0:T(8,128)(2,1)S(1)}, bf16[1,256,1024]{2,1,0:T(8,128)(2,1)}, u32[]{:S(2)}) copy-start(bf16[1,256,1024]{2,1,0:T(8,128)(2,1)} %param.27) | copy-start | bytes 1572868
  286.4 3.8 copy-start.12
  289.3 3.6 copy-start.8
  301.2 4.0 copy-start.14
  352.8 55.2 %collective-permute-start.4 = (bf16[256,512]{0,1:T(8,128)(2,1)}, bf16[256,512]{0,1:T(8,128)(2,1)}, u32[]{:S(2)}, u32[]{:S(2)}) collective-permute-start(bf16[256,512]{0,1:T(8,128)(2,1)} %bitcast.44), channel_id=1, source_target_pairs={{1,0},{32,1},{33,32},{64,33},{65,64},{96,65},{97,96},{3,2},{34,3},... | collective-permute-start | bytes 786440 | tf_op jit(solution)/shard_map/ppermute | solution.py:27
  380.1 22.0 %collective-permute-start = (bf16[256,512]{0,1:T(8,128)(2,1)}, bf16[256,512]{0,1:T(8,128)(2,1)}, u32[]{:S(2)}, u32[]{:S(2)}) collective-permute-start(bf16[256,512]{0,1:T(8,128)(2,1)} %bitcast.33), channel_id=1, source_target_pairs={{1,0},{32,1},{33,32},{64,33},{65,64},{96,65},{97,96},{3,2},{34,3},... | collective-permute-start | bytes 786440 | tf_op jit(solution)/shard_map/ppermute | solution.py:27
  382.0 21.4 %collective-permute-start.1 = (bf16[256,512]{0,1:T(8,128)(2,1)}, bf16[256,512]{0,1:T(8,128)(2,1)}, u32[]{:S(2)}, u32[]{:S(2)}) collective-permute-start(bf16[256,512]{0,1:T(8,128)(2,1)} %bitcast.34), channel_id=1, source_target_pairs={{32,0},{33,1},{64,32},{65,33},{96,64},{97,65},{34,2},{35,3},{66,34... | collective-permute-start | bytes 786440 | tf_op jit(solution)/shard_map/ppermute | solution.py:27
  383.3 21.4 %collective-permute-start.2 = (bf16[256,512]{0,1:T(8,128)(2,1)}, bf16[256,512]{0,1:T(8,128)(2,1)}, u32[]{:S(2)}, u32[]{:S(2)}) collective-permute-start(bf16[256,512]{0,1:T(8,128)(2,1)} %bitcast.35), channel_id=1, source_target_pairs={{33,0},{64,1},{65,32},{96,33},{97,64},{35,2},{66,3},{67,34},{98,35... | collective-permute-start | bytes 786440 | tf_op jit(solution)/shard_map/ppermute | solution.py:27
  384.6 3.6 copy-start.1
  384.7 3.8 copy-start.13
  384.7 21.4 %collective-permute-start.3 = (bf16[256,512]{0,1:T(8,128)(2,1)}, bf16[256,512]{0,1:T(8,128)(2,1)}, u32[]{:S(2)}, u32[]{:S(2)}) collective-permute-start(bf16[256,512]{0,1:T(8,128)(2,1)} %bitcast.36), channel_id=1, source_target_pairs={{64,0},{65,1},{96,32},{97,33},{66,2},{67,3},{98,34},{99,35},{68,4}... | collective-permute-start | bytes 786440 | tf_op jit(solution)/shard_map/ppermute | solution.py:27
  392.1 3.7 copy-start.19
  392.1 3.7 copy-start.21
  398.5 3.6 copy-start.25
  398.6 4.9 copy-start.24
  398.6 6.2 %copy-start.23 = (bf16[256,8,64]{0,2,1:T(8,128)(2,1)S(1)}, bf16[256,8,64]{0,2,1:T(8,128)(2,1)}, u32[]{:S(2)}) copy-start(bf16[256,8,64]{0,2,1:T(8,128)(2,1)} %get-tuple-element.90) | copy-start | bytes 786436
  398.6 7.5 %copy-start.11 = (f32[256,8,64]{0,2,1:T(8,128)S(1)}, f32[256,8,64]{0,2,1:T(8,128)}, u32[]{:S(2)}) copy-start(f32[256,8,64]{0,2,1:T(8,128)} %slice.164) | copy-start | bytes 1572868
  400.7 6.9 %copy-start.6 = (bf16[1024,512]{1,0:T(8,128)(2,1)S(1)}, bf16[1024,512]{1,0:T(8,128)(2,1)}, u32[]{:S(2)}) copy-start(bf16[1024,512]{1,0:T(8,128)(2,1)} %w_key_ref.1) | copy-start | bytes 3145732
  402.1 11.4 %collective-permute-start.5 = (bf16[256,512]{0,1:T(8,128)(2,1)S(1)}, bf16[256,512]{0,1:T(8,128)(2,1)S(1)}, u32[]{:S(2)}, u32[]{:S(2)}) collective-permute-start(bf16[256,512]{0,1:T(8,128)(2,1)S(1)} %bitcast.215), channel_id=1, source_target_pairs={{32,0},{33,1},{64,32},{65,33},{96,64},{97,65},{34,2},{35,3},{66,34... | collective-permute-start | bytes 786440 | tf_op jit(solution)/shard_map/ppermute | solution.py:27
  403.4 14.4 %collective-permute-start.6 = (bf16[256,512]{0,1:T(8,128)(2,1)S(1)}, bf16[256,512]{0,1:T(8,128)(2,1)S(1)}, u32[]{:S(2)}, u32[]{:S(2)}) collective-permute-start(bf16[256,512]{0,1:T(8,128)(2,1)S(1)} %bitcast.214), channel_id=1, source_target_pairs={{33,0},{64,1},{65,32},{96,33},{97,64},{35,2},{66,3},{67,34},{98,35... | collective-permute-start | bytes 786440 | tf_op jit(solution)/shard_map/ppermute | solution.py:27
  404.8 14.9 %collective-permute-start.7 = (bf16[256,512]{0,1:T(8,128)(2,1)S(1)}, bf16[256,512]{0,1:T(8,128)(2,1)S(1)}, u32[]{:S(2)}, u32[]{:S(2)}) collective-permute-start(bf16[256,512]{0,1:T(8,128)(2,1)S(1)} %bitcast.213), channel_id=1, source_target_pairs={{64,0},{65,1},{96,32},{97,33},{66,2},{67,3},{98,34},{99,35},{68,4}... | collective-permute-start | bytes 786440 | tf_op jit(solution)/shard_map/ppermute | solution.py:27
  407.5 13.2 %copy-start.5 = (bf16[1024,512]{1,0:T(8,128)(2,1)S(1)}, bf16[1024,512]{1,0:T(8,128)(2,1)}, u32[]{:S(2)}) copy-start(bf16[1024,512]{1,0:T(8,128)(2,1)} %w_value_ref.1) | copy-start | bytes 3145732
  407.6 13.2 %copy-start.27 = (f32[1024]{0:T(1024)S(1)}, f32[1024]{0:T(1024)}, u32[]{:S(2)}) copy-start(f32[1024]{0:T(1024)} %param.18) | copy-start | bytes 12292
  424.4 4.5 copy-start.30
  496.8 5.2 %copy-start.29 = (f32[256]{0:T(256)S(1)}, f32[256]{0:T(256)}, u32[]{:S(2)}) copy-start(f32[256]{0:T(256)} %get-tuple-element.78) | copy-start | bytes 3076
  502.0 6.2 %copy-start.3 = (f32[256,1024]{1,0:T(8,128)S(1)}, f32[256,1024]{1,0:T(8,128)}, u32[]{:S(2)}) copy-start(f32[256,1024]{1,0:T(8,128)} %get-tuple-element.80) | copy-start | bytes 3145732
  502.0 6.2 %copy-start.4 = (f32[256,1024]{1,0:T(8,128)S(1)}, f32[256,1024]{1,0:T(8,128)}, u32[]{:S(2)}) copy-start(f32[256,1024]{1,0:T(8,128)} %get-tuple-element.118) | copy-start | bytes 3145732
  502.0 6.2 %copy-start.28 = (f32[256]{0:T(256)S(1)}, f32[256]{0:T(256)}, u32[]{:S(2)}) copy-start(f32[256]{0:T(256)} %get-tuple-element.107) | copy-start | bytes 3076
  (8 other events, 18.4 us)
